TPU v7x, 128 devices: a whole 4x4x4 slice. The times are simulated.
128 devices in a mesh: prow: 8 (over y, core), pcol: 16 (over z, x).
Axes of the slice: x: 4, y: 4, z: 4, core: 2. Of those that a mesh axis runs over, the one named last changes fastest.
Arguments:
- spectra: bfloat16 [80, 128, 16, 2, 128], P('pcol', 'prow'), may hold values from -6 to 6
- tile_list: int32 [8, 16, 10, 2], P('prow', 'pcol'), may hold values from 0 to 79, as said below
- tile_count: int32 [8, 16], P('prow', 'pcol'), may hold values from 0 to 10, as said below
- observed: bfloat16 [8, 16, 10, 16, 2, 128, 128], P('prow', 'pcol'), may hold values from -0.59765625 to 0.59765625
Outputs:
- gradient: float32 [80, 128, 16, 2, 128], P('pcol', 'prow')
Inputs may be any that keep to these rules, and one draw needn't show every extreme that they name: Entries are channel block numbers; the row block of every entry of tile_list[r, q] lies among the 5 blocks of pcol index q; every pair (a, b) with a <= b <= a + 8 and b < 80 appears exactly once among the live entries of the 8 lists of that pcol index; entries past tile_count are (q * 5, q * 5). `tile_count`: loads differ strongly between the devices of one block column; in every draw some device has a full list of 10 live tiles.
All inputs are finite; a program needn't handle non-finite values.
Results may differ from a plain program's by a relative error of at most 0.0075.
Values may be sent and summed in bfloat16 or wider, within the bound.
No kernel may reach another device: no remote copies, remote signals or barrier semaphores. Data moves between devices by JAX's collectives and lax.ppermute only.
A program may use at most 192 MiB of HBM per device.

v0:
```python
import jax
import jax.numpy as jnp
from jax import lax
from jax.sharding import PartitionSpec as P

BAND = 8


eps_power = 1e-06
misfit_scale = 0.1


def shifted(block, axis, distance):
    devices = range(lax.axis_size(axis))
    route = [(i - distance, i) for i in devices if i - distance in devices]
    return lax.ppermute(block, axis, route)


def whiten(spectra):
    values = spectra.astype(jnp.float32)
    power = jnp.sum(values * values, axis=(3, 4), keepdims=True) / values.shape[4]
    factor = lax.rsqrt(power + eps_power)
    return (values, factor)


def tile_terms(row_block, col_block, observed_tile, tile_mask):
    windows = row_block.shape[3]
    col_turn = jnp.stack([col_block[:, :, 1], -col_block[:, :, 0]], axis=2)
    row_turn = jnp.stack([-row_block[:, :, 1], row_block[:, :, 0]], axis=2)
    real_part = (
        jnp.einsum("ifkw,jfkw->fij", row_block, col_block, preferred_element_type=jnp.float32)
        / windows
    )
    imag_part = (
        jnp.einsum("ifkw,jfkw->fij", row_block, col_turn, preferred_element_type=jnp.float32)
        / windows
    )
    resid = jnp.stack([real_part, imag_part], axis=1) - observed_tile.astype(jnp.float32)
    scaled = resid / misfit_scale
    slope = (resid / jnp.sqrt(1.0 + scaled * scaled) * tile_mask).astype(jnp.bfloat16)
    slope_real = slope[:, 0]
    slope_imag = slope[:, 1]
    row_grad = jnp.einsum(
        "fij,jfkw->ifkw", slope_real, col_block, preferred_element_type=jnp.float32
    ) + jnp.einsum("fij,jfkw->ifkw", slope_imag, col_turn, preferred_element_type=jnp.float32)
    col_grad = jnp.einsum(
        "fij,ifkw->jfkw", slope_real, row_block, preferred_element_type=jnp.float32
    ) + jnp.einsum("fij,ifkw->jfkw", slope_imag, row_turn, preferred_element_type=jnp.float32)
    return (row_grad, col_grad)


def tile_adder(extended, block_base):
    width = extended.shape[1]
    upper_mask = (
        lax.broadcasted_iota(jnp.int32, (width, width), 1)
        > lax.broadcasted_iota(jnp.int32, (width, width), 0)
    ).astype(jnp.float32)

    def add_tile(grad_buffer, tile_pair, observed_tile):
        first_id = tile_pair[0]
        second_id = tile_pair[1]
        row_place = first_id - block_base
        col_place = second_id - block_base
        row_block = lax.dynamic_index_in_dim(extended, row_place, 0, keepdims=False)
        col_block = lax.dynamic_index_in_dim(extended, col_place, 0, keepdims=False)
        tile_mask = jnp.where(first_id == second_id, upper_mask, 1.0)
        row_grad, col_grad = tile_terms(row_block, col_block, observed_tile, tile_mask)
        grad_buffer = grad_buffer.at[row_place].add(row_grad)
        return grad_buffer.at[col_place].add(col_grad)

    return add_tile


def local(spectra, tile_list, tile_count, observed):
    local_blocks = spectra.shape[0]
    shift_count = -(-BAND // local_blocks)
    block_base = lax.axis_index("pcol") * local_blocks
    values, factor = whiten(spectra)
    whitened = (values * factor).astype(jnp.bfloat16)
    complete = lax.all_gather(whitened, "prow", axis=1, tiled=True)
    gathered = [complete]
    for hop_count in range(1, shift_count + 1):
        send_size = min(local_blocks, BAND - (hop_count - 1) * local_blocks)
        gathered.append(shifted(complete[:send_size], "pcol", -hop_count))
    extended = jnp.concatenate(gathered, axis=0)
    own_list = tile_list[0, 0]
    own_count = tile_count[0, 0]
    own_obs = observed[0, 0]
    add_tile = tile_adder(extended, block_base)
    grad_buffer = jnp.zeros((local_blocks + BAND,) + extended.shape[1:], jnp.float32)
    grad_buffer = lax.fori_loop(
        0,
        own_count,
        lambda slot_id, buffer_now: add_tile(buffer_now, own_list[slot_id], own_obs[slot_id]),
        grad_buffer,
    )
    own_terms = grad_buffer[:local_blocks]
    for hop_count in range(1, shift_count + 1):
        send_size = min(local_blocks, BAND - (hop_count - 1) * local_blocks)
        begin_at = local_blocks + (hop_count - 1) * local_blocks
        arrived = shifted(
            grad_buffer[begin_at : begin_at + send_size].astype(jnp.bfloat16), "pcol", hop_count
        ).astype(jnp.float32)
        own_terms = own_terms.at[:send_size].add(arrived)
    summed = lax.psum_scatter(own_terms, "prow", scatter_dimension=1, tiled=True)
    inner = jnp.sum(summed * values, axis=(3, 4), keepdims=True) / spectra.shape[4]
    return factor * summed - values * (factor * factor * factor) * inner


def solution(mesh):
    placed = (
        P("pcol", "prow", None, None, None),
        P("prow", "pcol", None, None),
        P("prow", "pcol"),
        P("prow", "pcol", None, None, None, None, None),
    )
    return jax.shard_map(
        local,
        mesh=mesh,
        in_specs=placed,
        out_specs=P("pcol", "prow", None, None, None),
        check_vma=False,
    )
```

profile of v0, /device:TPU:32, one launch (start us, length us, event | category | flops | bytes accessed | tf_op | source)
XLA Modules:
  0.0 831.1 jit_solution(17685589029834975499)
XLA Ops:
  10.1 38.6 %all-gather.2.cloned.1.call-done = bf16[5,128,16,2,128]{4,2,3,0,1:T(8,128)(2,1)} async-done(((bf16[5,16,16,2,128]{4,2,3,0,1:T(8,128)(2,1)}), bf16[5,128,16,2,128]{4,2,3,0,1:T(8,128)(2,1)}) %all-gather.2.cloned.1.call-update) | async-done | bytes 5242896 | tf_op jit(solution)/shard_map/all_gather | solution.py:80
  48.8 4.5 collective-permute-start
  55.8 2.8 collective-permute-start.1
  58.5 12.7 %copy.46 = bf16[1,1,10,16,2,128,128]{6,5,3,4,2,1,0:T(8,128)(2,1)} copy(bf16[1,1,10,16,2,128,128]{6,5,4,3,2,1,0:T(8,128)(2,1)} %param.19) | data formatting | bytes 20971520 | tf_op args[3]
  71.2 58.0 %collective-permute-done.1 = bf16[3,128,16,2,128]{4,2,3,0,1:T(8,128)(2,1)} collective-permute-done((bf16[3,128,16,2,128]{4,2,3,0,1:T(8,128)(2,1)S(1)}, bf16[3,128,16,2,128]{4,2,3,0,1:T(8,128)(2,1)}, u32[]{:S(2)}, u32[]{:S(2)}) %collective-permute-start.1) | collective-permute-done | bytes 3145760 | tf_op jit(solution)/shard_map/ppermute | solution.py:16
  129.2 104.5 %collective-permute-done = bf16[5,128,16,2,128]{4,2,3,0,1:T(8,128)(2,1)} collective-permute-done((bf16[5,128,16,2,128]{4,2,3,0,1:T(8,128)(2,1)}, bf16[5,128,16,2,128]{4,2,3,0,1:T(8,128)(2,1)}, u32[]{:S(2)}, u32[]{:S(2)}) %collective-permute-start) | collective-permute-done | bytes 5242912 | tf_op jit(solution)/shard_map/ppermute | solution.py:16
  233.8 7.9 pad_maximum_fusion.3
  241.7 6.2 copy.29
  247.9 12.5 %broadcast_in_dim.6 = f32[13,128,16,2,128]{1,4,3,2,0:T(8,128)} broadcast(f32[]{:T(128)} %constant.139.clone.1), dimensions={} | broadcast | bytes 27262980 | tf_op jit(solution)/shard_map/broadcast_in_dim | solution.py:90
  260.4 153.6 %while.16 = (s32[]{:T(128)}, f32[13,128,16,2,128]{1,4,3,2,0:T(8,128)}, s32[]{:T(128)}, s32[10,2]{0,1:T(2,128)S(1)}, s32[]{:T(128)}, /*index=5*/bf16[13,128,16,2,...) while((s32[]{:T(128)}, ...), condition=%wide.region_4.5_spmd.clone, body=%wide.region_1.4_spmd.clone.sunk | while | flops 815841280 | bytes 50465328 | solution.py:91
  270.1 2.5 multiply_convert_fusion.2
  275.3 5.1 fusion.52
  281.6 4.3 fusion.54
  295.6 2.5 multiply_convert_fusion.2
  300.8 5.1 fusion.52
  307.1 4.2 fusion.54
  326.2 5.1 fusion.52
  332.6 4.3 fusion.54
  351.7 5.0 fusion.52
  358.0 4.3 fusion.54
  377.2 5.1 fusion.52
  383.5 4.2 fusion.54
  402.6 5.1 fusion.52
  408.9 4.2 fusion.54
  414.0 28.6 %copy.30 = f32[13,128,16,2,128]{4,2,3,0,1:T(8,128)} copy(f32[13,128,16,2,128]{1,4,3,2,0:T(8,128)} %get-tuple-element.104) | data formatting | bytes 54525952 | tf_op jit(solution)/shard_map/while | solution.py:91
  442.6 10.9 %convert.5 = bf16[13,128,16,2,128]{4,2,3,0,1:T(8,128)(2,1)S(1)} convert(f32[13,128,16,2,128]{4,2,3,0,1:T(8,128)} %copy.30) | non-fusion elementwise | flops 6815744 | bytes 40894464 | tf_op jit(solution)/shard_map/convert.2
  454.4 80.5 %collective-permute-start.2 = (bf16[5,128,16,2,128]{4,2,3,0,1:T(8,128)(2,1)S(1)}, bf16[5,128,16,2,128]{4,2,3,0,1:T(8,128)(2,1)}, u32[]{:S(2)}, u32[]{:S(2)}) collective-permute-start(bf16[5,128,16,2,128]{4,2,3,0,1:T(8,128)(2,1)S(1)} %slice.182), channel_id=1, source_target_pairs={{0,1},{1,2},{2,3},{3,4},{4,5},{5,6},{6,7},{7,8},{8,9},{9,10},{10,1... | collective-permute-start | bytes 15728648 | tf_op jit(solution)/shard_map/ppermute | solution.py:16
  537.4 88.9 %collective-permute-done.2 = bf16[5,128,16,2,128]{4,2,3,0,1:T(8,128)(2,1)} collective-permute-done((bf16[5,128,16,2,128]{4,2,3,0,1:T(8,128)(2,1)S(1)}, bf16[5,128,16,2,128]{4,2,3,0,1:T(8,128)(2,1)}, u32[]{:S(2)}, u32[]{:S(2)}) %collective-permute-start.2) | collective-permute-done | bytes 5242912 | tf_op jit(solution)/shard_map/ppermute | solution.py:16
  626.3 11.2 %slice_add_fusion = f32[5,128,16,2,128]{4,2,3,0,1:T(8,128)} fusion(f32[13,128,16,2,128]{4,2,3,0,1:T(8,128)} %copy.30, bf16[5,128,16,2,128]{4,2,3,0,1:T(8,128)(2,1)} %collective-permute-done.2), kind=kLoop, calls=%fused_computation.34 | loop fusion | flops 5242880 | bytes 26214400 | tf_op jit(solution)/shard_map/add | solution.py:104
  637.5 56.3 %collective-permute-done.3 = bf16[3,128,16,2,128]{4,2,3,0,1:T(8,128)(2,1)} collective-permute-done((bf16[3,128,16,2,128]{4,2,3,0,1:T(8,128)(2,1)S(1)}, bf16[3,128,16,2,128]{4,2,3,0,1:T(8,128)(2,1)}, u32[]{:S(2)}, u32[]{:S(2)}) %collective-permute-start.3) | collective-permute-done | bytes 3145760 | tf_op jit(solution)/shard_map/ppermute | solution.py:16
  693.7 7.4 fusion.16
  701.2 119.0 %reduce-scatter.2.cloned.1.call-done = f32[5,16,16,2,128]{4,2,3,0,1:T(8,128)} async-done(((f32[5,128,16,2,128]{4,2,3,0,1:T(8,128)}), f32[5,16,16,2,128]{4,2,3,0,1:T(8,128)}) %reduce-scatter.2.cloned.1.call-update) | async-done | bytes 1310736 | tf_op jit(solution)/shard_map/reduce_scatter | solution.py:105
  (147 shorter events, 85.2 us)
Async XLA Ops:
  6.5 42.3 %all-gather.2.cloned.1.call-start = ((), (), s32[]{:S(2)}) async-start(), calls=%async_computation.1 | async-start | bytes 5898240 | tf_op jit(solution)/shard_map/all_gather | solution.py:80
  10.1 810.1 %reduce-scatter.2.cloned.1.call-start = ((), (), s32[]{:S(2)}) async-start(), calls=%async_computation.2 | async-start | bytes 11796480 | tf_op jit(solution)/shard_map/reduce_scatter | solution.py:105
  48.8 185.0 %collective-permute-start = (bf16[5,128,16,2,128]{4,2,3,0,1:T(8,128)(2,1)}, bf16[5,128,16,2,128]{4,2,3,0,1:T(8,128)(2,1)}, u32[]{:S(2)}, u32[]{:S(2)}) collective-permute-start(bf16[5,128,16,2,128]{4,2,3,0,1:T(8,128)(2,1)} %all-gather.2.cloned.1.call-done), channel_id=1, source_target_pairs={{1,0},{2,1},{3,2},{4,3},{5,4},{6,5},{7,6},{8,7},{9,8},{10,9},{11,1... | collective-permute-start | bytes 15728648 | tf_op jit(solution)/shard_map/ppermute | solution.py:16
  55.8 73.5 %collective-permute-start.1 = (bf16[3,128,16,2,128]{4,2,3,0,1:T(8,128)(2,1)S(1)}, bf16[3,128,16,2,128]{4,2,3,0,1:T(8,128)(2,1)}, u32[]{:S(2)}, u32[]{:S(2)}) collective-permute-start(bf16[3,128,16,2,128]{4,2,3,0,1:T(8,128)(2,1)S(1)} %slice.180), channel_id=1, source_target_pairs={{2,0},{3,1},{4,2},{5,3},{6,4},{7,5},{8,6},{9,7},{10,8},{11,9},{12,... | collective-permute-start | bytes 9437192 | tf_op jit(solution)/shard_map/ppermute | solution.py:16
  247.9 12.5 %copy-start.6 = (s32[1,1,10,2]{2,3,1,0:T(2,128)S(1)}, s32[1,1,10,2]{2,3,1,0:T(2,128)}, u32[]{:S(2)}) copy-start(s32[1,1,10,2]{2,3,1,0:T(2,128)} %param.17) | copy-start | bytes 244
  247.9 12.5 %copy-start.7 = (s32[5]{0:T(128)S(1)}, s32[5]{0:T(128)}, u32[]{:S(2)}) copy-start(s32[5]{0:T(128)} %constant.134.clone.2) | copy-start | bytes 64
  267.3 2.8 copy-start.2
  267.3 2.8 copy-start.3
  280.4 1.0 copy-start
  280.4 1.2 copy-start.1
  292.8 2.8 copy-start.2
  292.8 2.8 copy-start.3
  305.9 1.0 copy-start
  305.9 1.2 copy-start.1
  318.3 2.8 copy-start.2
  318.3 2.8 copy-start.3
  331.4 1.0 copy-start
  331.4 1.2 copy-start.1
  343.8 2.8 copy-start.2
  343.8 2.8 copy-start.3
  356.8 1.0 copy-start
  356.8 1.2 copy-start.1
  369.2 2.8 copy-start.2
  369.2 2.8 copy-start.3
  382.3 1.2 copy-start.1
  394.6 2.8 copy-start.2
  394.6 2.8 copy-start.3
  407.7 1.2 copy-start.1
  454.4 171.9 %collective-permute-start.2 = (bf16[5,128,16,2,128]{4,2,3,0,1:T(8,128)(2,1)S(1)}, bf16[5,128,16,2,128]{4,2,3,0,1:T(8,128)(2,1)}, u32[]{:S(2)}, u32[]{:S(2)}) collective-permute-start(bf16[5,128,16,2,128]{4,2,3,0,1:T(8,128)(2,1)S(1)} %slice.182), channel_id=1, source_target_pairs={{0,1},{1,2},{2,3},{3,4},{4,5},{5,6},{6,7},{7,8},{8,9},{9,10},{10,1... | collective-permute-start | bytes 15728648 | tf_op jit(solution)/shard_map/ppermute | solution.py:16
  535.5 158.3 %collective-permute-start.3 = (bf16[3,128,16,2,128]{4,2,3,0,1:T(8,128)(2,1)S(1)}, bf16[3,128,16,2,128]{4,2,3,0,1:T(8,128)(2,1)}, u32[]{:S(2)}, u32[]{:S(2)}) collective-permute-start(bf16[3,128,16,2,128]{4,2,3,0,1:T(8,128)(2,1)S(1)} %slice.184), channel_id=1, source_target_pairs={{0,2},{1,3},{2,4},{3,5},{4,6},{5,7},{6,8},{7,9},{8,10},{9,11},{10,... | collective-permute-start | bytes 9437192 | tf_op jit(solution)/shard_map/ppermute | solution.py:16
  701.1 119.0 %copy-start.4 = (bf16[5,16,16,2,128]{4,3,2,1,0:T(2,128)(2,1)S(1)}, bf16[5,16,16,2,128]{4,3,2,1,0:T(2,128)(2,1)}, u32[]{:S(2)}) copy-start(bf16[5,16,16,2,128]{4,3,2,1,0:T(2,128)(2,1)} %param.16) | copy-start | bytes 1966084
  820.2 1.7 copy-start.5
  (2 other events, 2.1 us)
Sparse Core Ops, SparseCore 0:
  10.2 38.5 all-gather.1
  701.3 118.8 reduce-scatter.1
where the time goes:
time: 834 us; the launch traced here: 831 us
  waiting for transfers between devices  465 us (56%)
  starting transfers between devices  89.7 us (11%)
  matrix products  87.4 us (10%)
  local copies, waits for them, and re-layouts  85.1 us (10%)
  other arithmetic  69.1 us (8%)
  loops' own time  20.9 us (3%)
  between operations  13.5 us (2%)
    ppermute x4, waiting for transfers between devices, shifted(): return lax.ppermute(block, axis, route)  308 us
    reduce_scatter x1, waiting for transfers between devices, local(): lax.psum_scatter(own_terms, 'prow', scatter_dimension=1, tiled=True)  119 us
    ppermute x4, starting transfers between devices, shifted(): return lax.ppermute(block, axis, route)  89.7 us
    all_gather x1, waiting for transfers between devices, local(): complete = lax.all_gather(whitened, 'prow', axis=1, tiled=True)  38.6 us
    dot_general x6, matrix products, tile_terms(): jnp.einsum('fij,jfkw->ifkw', slope_imag, col_turn, preferred_element_type...  30.6 us
    while x1, local copies, waits for them, and re-layouts, local(): lax.fori_loop(0, own_count, lambda slot_id, buffer_now: add_tile(buffer_n...  28.6 us
    dot_general x6, matrix products, tile_terms(): jnp.einsum('fij,ifkw->jfkw', slope_imag, row_turn, preferred_element_type...  25.4 us
    another operation x1, loops' own time, local(): lax.fori_loop(0, own_count, lambda slot_id, buffer_now: add_tile(buffer_n...  20.9 us
  transfers between devices with their start and end apart: 6, of which 6 were waited for; matrix products, arithmetic and copies ran while one was open for 3% of the time, Pallas kernels for 0%

commit v1 on v0

v1 whole, which is shorter than its diff:
```python
import functools

import jax
import jax.numpy as jnp
from jax import lax
from jax.experimental import pallas as pl
from jax.experimental.pallas import tpu as pltpu
from jax.sharding import PartitionSpec as P

BAND = 8
EPS = 1e-06
CURVE = 100.0


def turn(block):
    half = block.shape[-1] // 2
    return jnp.concatenate([block[:, half:], -block[:, :half]], axis=1)


def tile_kernel(slots, meta, obs_own, *rest):
    others = rest[:7]
    own, near, far, grad_own, grad_near, grad_far = rest[7:13]
    order, held, stack, back, grad, first, second, sems = rest[13:]
    blocks = own.shape[0]
    reach = far.shape[0]
    width = own.shape[1]
    total = 2 * blocks + reach
    copies = []
    for k, piece in enumerate((obs_own,) + others):
        copies.append(pltpu.make_async_copy(piece, held.at[pl.ds(k * slots, slots)], sems.at[k]))
        copies[-1].start()

    live = 0
    for k in range(8):

        def put(s, at, k=k):
            order[0, at] = meta[k, 1 + 2 * s]
            order[1, at] = meta[k, 2 + 2 * s]
            order[2, at] = k * slots + s
            return at + 1

        live = lax.fori_loop(0, meta[k, 0], put, live)
    for extra in range(3):
        for row in range(3):
            order[row, live + extra] = 0

    for n in range(total):
        if n < blocks:
            block = own[n]
        elif n < 2 * blocks:
            block = near[n - blocks]
        else:
            block = far[n - 2 * blocks]
        turned = turn(block)
        stack[n, :width] = block
        stack[n, width:] = turned
        if n < blocks:
            back[n, :width] = block
            back[n, width:] = -turned
    grad[...] = jnp.zeros_like(grad)
    for copy in copies:
        copy.wait()

    gap = lax.broadcasted_iota(jnp.int32, (width, width), 1) - lax.broadcasted_iota(
        jnp.int32, (width, width), 0
    )

    def slope_of(t, into):
        a = order[0, t]
        b = order[1, t]
        spot = order[2, t]
        least = jnp.where(t < live, jnp.where(a == b, 0, -width), width)
        sums = lax.dot_general(
            stack[a, :width], stack[b], (((1,), (1,)), ((), ())), preferred_element_type=jnp.float32
        )
        keep = gap > least
        for part in range(2):
            seen = held[spot, part].astype(jnp.float32) * width
            diff = sums[:, part * width : (part + 1) * width] - seen
            slope = diff * lax.rsqrt(diff * diff * CURVE + float(width * width))
            into[part * width : (part + 1) * width] = jnp.where(keep, slope, 0.0).astype(jnp.bfloat16)

    def grads_of(t, slope):
        a = order[0, t]
        b = order[1, t]
        both = slope[...]
        wide = jnp.concatenate([both[:width], both[width:]], axis=1)
        row = jnp.dot(wide, stack[b], preferred_element_type=jnp.float32)
        col = lax.dot_general(
            both, back[a], (((0,), (0,)), ((), ())), preferred_element_type=jnp.float32
        )
        grad[a] += row
        grad[b] += col

    slope_of(0, first)

    def pair(m, carry):
        t = 2 * m
        slope_of(t + 1, second)
        grads_of(t, first)
        slope_of(t + 2, first)
        grads_of(t + 1, second)
        return carry

    lax.fori_loop(0, (live + 1) // 2, pair, 0)
    grad_own[...] = grad[:blocks]
    grad_near[...] = grad[blocks : 2 * blocks].astype(jnp.bfloat16)
    grad_far[...] = grad[2 * blocks :].astype(jnp.bfloat16)


def tile_call(meta, pieces, own, near, far):
    slots = pieces[0].shape[0]
    blocks, width, depth = own.shape
    reach = far.shape[0]
    total = 2 * blocks + reach
    vmem = pl.BlockSpec(memory_space=pltpu.VMEM)
    return pl.pallas_call(
        functools.partial(tile_kernel, slots),
        out_shape=(
            jax.ShapeDtypeStruct((blocks, width, depth), jnp.float32),
            jax.ShapeDtypeStruct((blocks, width, depth), jnp.bfloat16),
            jax.ShapeDtypeStruct((reach, width, depth), jnp.bfloat16),
        ),
        in_specs=[pl.BlockSpec(memory_space=pltpu.SMEM)]
        + [pl.BlockSpec(memory_space=pl.ANY)] * 8
        + [vmem] * 3,
        out_specs=(vmem, vmem, vmem),
        scratch_shapes=[
            pltpu.SMEM((3, 8 * slots + 8), jnp.int32),
            pltpu.VMEM((8 * slots, 2, width, width), jnp.bfloat16),
            pltpu.VMEM((total, 2 * width, depth), jnp.bfloat16),
            pltpu.VMEM((blocks, 2 * width, depth), jnp.bfloat16),
            pltpu.VMEM((total, width, depth), jnp.float32),
            pltpu.VMEM((2 * width, width), jnp.bfloat16),
            pltpu.VMEM((2 * width, width), jnp.bfloat16),
            pltpu.SemaphoreType.DMA((8,)),
        ],
        compiler_params=pltpu.CompilerParams(vmem_limit_bytes=40 * 1024 * 1024),
        cost_estimate=pl.CostEstimate(
            flops=45 * 6 * width * depth * depth, bytes_accessed=8 * 1024 * 1024, transcendentals=0
        ),
    )(meta, *pieces, own, near, far)


def final_kernel(spectra, own, near, far, out):
    blocks = own.shape[0]
    reach = far.shape[0]
    scale = 2.0 / spectra.shape[-1]
    for n in range(blocks):
        values = spectra[n].astype(jnp.float32)
        power = jnp.sum(values * values, axis=1, keepdims=True) * scale
        factor = lax.rsqrt(power + EPS)
        total = own[n] + near[n].astype(jnp.float32)
        if n < reach:
            total = total + far[n].astype(jnp.float32)
        inner = jnp.sum(total * values, axis=1, keepdims=True) * scale
        grad = factor * total - values * (factor * factor * factor * inner)
        out[n] = grad.astype(jnp.bfloat16)


def final_call(spectra, own, near, far):
    vmem = pl.BlockSpec(memory_space=pltpu.VMEM)
    return pl.pallas_call(
        final_kernel,
        out_shape=jax.ShapeDtypeStruct(spectra.shape, jnp.bfloat16),
        in_specs=[vmem] * 4,
        out_specs=vmem,
        compiler_params=pltpu.CompilerParams(vmem_limit_bytes=40 * 1024 * 1024),
    )(spectra, own, near, far)


HOPS = ((1, 0), (3, 0), (1, 1), (3, 1), (2, 0), (2, 1), (0, 1))


def across(values, step, flip):
    chips = lax.axis_size("prow") // 2
    route = [
        (2 * y + c, 2 * ((y + step) % chips) + (c ^ flip)) for y in range(chips) for c in range(2)
    ]
    return lax.ppermute(values, "prow", route)


def along(values, distance):
    devices = range(lax.axis_size("pcol"))
    route = [(i - distance, i) for i in devices if i - distance in devices]
    return lax.ppermute(values, "pcol", route)


def local(spectra, tile_list, tile_count, observed):
    blocks, share, bins, parts, windows = spectra.shape
    slots = tile_list.shape[2]
    width = 8 * share
    me = lax.axis_index("prow")
    chip = me // 2
    core = me % 2
    base = lax.axis_index("pcol") * blocks
    obs = observed[0, 0]

    targets = [(chip + step) % 4 * 2 + (core ^ flip) for step, flip in HOPS]
    sources = [(chip - step) % 4 * 2 + (core ^ flip) for step, flip in HOPS]

    pieces = []
    for j in range(2):
        got = [lax.dynamic_index_in_dim(obs, 8 * j + me, 1, keepdims=False)]
        for (step, flip), target in zip(HOPS, targets):
            part = lax.dynamic_index_in_dim(obs, 8 * j + target, 1, keepdims=False)
            got.append(across(part, step, flip))
        pieces.append(got)

    meta = jnp.concatenate([tile_count.reshape(1), (tile_list - base).reshape(-1)])
    meta = lax.all_gather(meta, "prow", axis=0)
    meta = meta[jnp.stack([me] + sources)]

    split = spectra.reshape(blocks, share, 2, 8, parts * windows)
    mine = lax.all_to_all(split, "prow", split_axis=3, concat_axis=0, tiled=False)
    mine = mine.transpose(3, 1, 0, 2, 4).reshape(2, blocks, width, parts * windows)
    values = mine.astype(jnp.float32)
    power = jnp.sum(values * values, axis=-1, keepdims=True) / windows
    white = (values * lax.rsqrt(power + EPS)).astype(jnp.bfloat16)

    outs = []
    reach = BAND - blocks
    near = along(white, -1)
    far = along(white[:, :reach], -2)
    for j in range(2):
        own_sum, near_sum, far_sum = tile_call(meta, pieces[j], white[j], near[j], far[j])
        near_got = along(near_sum, 1)
        far_got = along(far_sum, 2)
        grad = final_call(mine[j], own_sum, near_got, far_got)
        grad = grad.reshape(blocks, 8, share, parts * windows)
        outs.append(lax.all_to_all(grad, "prow", split_axis=1, concat_axis=0, tiled=False))
    whole = jnp.stack(outs).reshape(bins, blocks, share, parts, windows)
    return whole.transpose(1, 2, 0, 3, 4).astype(jnp.float32)


def solution(mesh):
    placed = (
        P("pcol", "prow", None, None, None),
        P("prow", "pcol", None, None),
        P("prow", "pcol"),
        P("prow", "pcol", None, None, None, None, None),
    )
    return jax.shard_map(
        local,
        mesh=mesh,
        in_specs=placed,
        out_specs=P("pcol", "prow", None, None, None),
        check_vma=False,
    )
```

time: 834 us -> 208 us (0.25)
  waiting for transfers between devices: 465 us -> 61.7 us
  matrix products: 87.4 us -> 0 us
  other arithmetic: 69.1 us -> 3.98 us
  local copies, waits for them, and re-layouts: 85.1 us -> 24.7 us
  starting transfers between devices: 89.7 us -> 61.5 us
  Pallas kernels: 0 us -> 28.2 us
  blocking collectives: 0 us -> 25.2 us
  loops' own time: 20.9 us -> 0 us
  between operations: 13.5 us -> 1.65 us
    ppermute x4 -> x20, waiting for transfers between devices: 308 us -> 61.7 us  [the longest x14 55.5 us: across(): return lax.ppermute(values, 'prow', route)]
    reduce_scatter x1 -> x0, waiting for transfers between devices: 119 us -> none  [local(): lax.psum_scatter(own_terms, 'prow', scatter_dimension=1, tiled=True)]
    dot_general x36 -> x0, matrix products: 87.4 us -> none  [the longest x6 30.6 us: tile_terms(): jnp.einsum('fij,jfkw->ifkw', slope_imag, col_turn, preferred_element_type...]
    all_gather x1 -> x0, waiting for transfers between devices: 38.6 us -> none  [local(): complete = lax.all_gather(whitened, 'prow', axis=1, tiled=True)]
    ppermute x4 -> x20, starting transfers between devices: 89.7 us -> 53.6 us  [the longest x14 28.6 us: across(): return lax.ppermute(values, 'prow', route)]
    while x49 -> x0, local copies, waits for them, and re-layouts: 32.9 us -> none  [the longest x1 28.6 us: local(): lax.fori_loop(0, own_count, lambda slot_id, buffer_now: add_tile(buffer_n...]
    pallas_call x0 -> x4, Pallas kernels: none -> 28.2 us  [the longest x2 27.6 us: tile_call(): pl.pallas_call(functools.partial(tile_kernel, slots), out_shape=(jax.Shap...]
    another operation x1 -> x0, loops' own time: 20.9 us -> none  [local(): lax.fori_loop(0, own_count, lambda slot_id, buffer_now: add_tile(buffer_n...]
  transfers between devices with their start and end apart: 6 -> 22, of which waited for: 6 -> 5; matrix products, arithmetic and copies ran while one was open for 3% -> 11% of each run, Pallas kernels for 0% -> 14%
where the time goes in v1:
time: 208 us; the launch traced here: 207 us
  waiting for transfers between devices  61.7 us (30%)
  starting transfers between devices  61.5 us (30%)
  Pallas kernels  28.2 us (14%)
  blocking collectives  25.2 us (12%)
  local copies, waits for them, and re-layouts  24.7 us (12%)
  other arithmetic  3.98 us (2%)
    ppermute x14, waiting for transfers between devices, across(): return lax.ppermute(values, 'prow', route)  55.5 us
    ppermute x14, starting transfers between devices, across(): return lax.ppermute(values, 'prow', route)  28.6 us
    pallas_call x2, Pallas kernels, tile_call(): pl.pallas_call(functools.partial(tile_kernel, slots), out_shape=(jax.Shap...  27.6 us
    ppermute x6, starting transfers between devices, along(): return lax.ppermute(values, 'pcol', route)  25 us
    unnamed x1, blocking collectives  13 us
    all_to_all x1, blocking collectives, local(): lax.all_to_all(grad, 'prow', split_axis=1, concat_axis=0, tiled=False)  12.2 us
    squeeze x1, local copies, waits for them, and re-layouts, local(): part = lax.dynamic_index_in_dim(obs, 8 * j + target, 1, keepdims=False)  9.28 us
    ppermute x6, waiting for transfers between devices, along(): return lax.ppermute(values, 'pcol', route)  6.2 us
  transfers between devices with their start and end apart: 22, of which 5 were waited for; matrix products, arithmetic and copies ran while one was open for 11% of the time, Pallas kernels for 14%

profile of v1, /device:TPU:32, one launch (start us, length us, event | category | flops | bytes accessed | tf_op | source)
XLA Modules:
  0.0 207.0 jit_solution(12119741432604433937)
XLA Ops:
  0.0 2.2 %broadcast_in_dim_reshape.9 = bf16[1,5,16,2,8,256]{5,4,3,2,1,0:T(8,128)(2,1)S(1)} reshape(bf16[5,16,16,2,128]{4,3,2,1,0:T(2,128)(2,1)} %param.4) | data formatting | bytes 1310720 | tf_op jit(solution)/shard_map/broadcast_in_dim;reshape | solution.py:215
  3.3 4.5 %all-to-all-start = ((bf16[1,5,16,2,8,256]{5,2,1,3,0,4:T(8,128)(2,1)}), bf16[1,5,16,2,8,256]{5,2,1,3,0,4:T(8,128)(2,1)}, u32[]{:S(2)}, u32[]{:S(2)}) async-start(bf16[1,5,16,2,8,256]{5,2,1,3,0,4:T(8,128)(2,1)} %copy.22), calls=%async_computation | async-start | bytes 1310720 | tf_op jit(solution)/shard_map/all_to_all | solution.py:215
  7.8 9.3 %dynamic-slice_bitcast_fusion.8 = (bf16[10,2,128,128]{3,2,1,0:T(8,128)(2,1)}, bf16[10,2,128,128]{3,2,1,0:T(8,128)(2,1)}, bf16[10,2,128,128]{3,2,1,0:T(8,128)(2,1...) fusion(bf16[1,1,10,16,2,128,128]{6,5,4,3,2,1,0:T(8,128)(2,1)} %, ...), kind=kLoop, calls=%fused_computation.14 | loop fusion | bytes 20971584 | tf_op jit(solution)/shard_map/jit(dynamic_index_in_dim)/squeeze | solution.py:206
  17.6 3.2 %collective-permute-start.15 = (bf16[10,2,128,128]{3,2,1,0:T(8,128)(2,1)}, bf16[10,2,128,128]{3,2,1,0:T(8,128)(2,1)S(1)}, u32[]{:S(2)}, u32[]{:S(2)}) collective-permute-start(bf16[10,2,128,128]{3,2,1,0:T(8,128)(2,1)} %get-tuple-element.18), channel_id=1, source_target_pairs={{0,64},{16,80},{32,96},{48,112},{64,0},{80,16},{96,32},{112,48},{1... | collective-permute-start | bytes 1966088 | tf_op jit(solution)/shard_map/ppermute | solution.py:180
  21.6 1.5 collective-permute-start.5
  23.1 2.1 collective-permute-start.4
  27.4 1.3 multiply_reduce_fusion
  28.9 1.3 bitcast_convert_fusion
  31.4 5.4 %collective-permute-done.15.rest_4_ = bf16[10,2,128,128]{3,2,1,0:T(8,128)(2,1)S(1)} collective-permute-done((bf16[10,2,128,128]{3,2,1,0:T(8,128)(2,1)}, bf16[10,2,128,128]{3,2,1,0:T(8,128)(2,1)S(1)}, u32[]{:S(2)}, u32[]{:S(2)}) %collective-permute-start.15) | collective-permute-done | bytes 655392 | tf_op jit(solution)/shard_map/ppermute | solution.py:180
  37.1 12.9 %collective-permute-done.14.rest_3_ = bf16[10,2,128,128]{3,2,1,0:T(8,128)(2,1)S(1)} collective-permute-done((bf16[10,2,128,128]{3,2,1,0:T(8,128)(2,1)}, bf16[10,2,128,128]{3,2,1,0:T(8,128)(2,1)S(1)}, u32[]{:S(2)}, u32[]{:S(2)}) %collective-permute-start.14) | collective-permute-done | bytes 655392 | tf_op jit(solution)/shard_map/ppermute | solution.py:180
  50.0 3.7 %collective-permute-start.1 = (bf16[10,2,128,128]{3,2,1,0:T(8,128)(2,1)}, bf16[10,2,128,128]{3,2,1,0:T(8,128)(2,1)}, u32[]{:S(2)}, u32[]{:S(2)}) collective-permute-start(bf16[10,2,128,128]{3,2,1,0:T(8,128)(2,1)} %get-tuple-element.28), channel_id=1, source_target_pairs={{0,96},{16,112},{32,0},{48,16},{64,32},{80,48},{96,64},{112,80},{1... | collective-permute-start | bytes 1966088 | tf_op jit(solution)/shard_map/ppermute | solution.py:180
  53.7 12.0 %collective-permute-start = (bf16[10,2,128,128]{3,2,1,0:T(8,128)(2,1)}, bf16[10,2,128,128]{3,2,1,0:T(8,128)(2,1)}, u32[]{:S(2)}, u32[]{:S(2)}) collective-permute-start(bf16[10,2,128,128]{3,2,1,0:T(8,128)(2,1)} %get-tuple-element.29), channel_id=1, source_target_pairs={{0,32},{16,48},{32,64},{48,80},{64,96},{80,112},{96,0},{112,16},{1... | collective-permute-start | bytes 1966088 | tf_op jit(solution)/shard_map/ppermute | solution.py:180
  65.7 4.2 %collective-permute-start.7 = (bf16[2,5,128,256]{3,2,1,0:T(8,128)(2,1)}, bf16[2,5,128,256]{3,2,1,0:T(8,128)(2,1)}, u32[]{:S(2)}, u32[]{:S(2)}) collective-permute-start(bf16[2,5,128,256]{3,2,1,0:T(8,128)(2,1)} %fusion), channel_id=1, source_target_pairs={{1,0},{2,1},{3,2},{4,3},{5,4},{6,5},{7,6},{8,7},{9,8},{10,9},{11,1... | collective-permute-start | bytes 1966088 | tf_op jit(solution)/shard_map/ppermute | solution.py:186
  69.9 1.8 slice.43
  71.7 20.4 %collective-permute-done.3.rest_3_ = bf16[10,2,128,128]{3,2,1,0:T(8,128)(2,1)S(1)} collective-permute-done((bf16[10,2,128,128]{3,2,1,0:T(8,128)(2,1)}, bf16[10,2,128,128]{3,2,1,0:T(8,128)(2,1)S(1)}, u32[]{:S(2)}, u32[]{:S(2)}) %collective-permute-start.3) | collective-permute-done | bytes 655392 | tf_op jit(solution)/shard_map/ppermute | solution.py:180
  93.0 4.5 %collective-permute-start.8 = (bf16[2,3,128,256]{3,2,1,0:T(8,128)(2,1)}, bf16[2,3,128,256]{3,2,1,0:T(8,128)(2,1)}, u32[]{:S(2)}, u32[]{:S(2)}) collective-permute-start(bf16[2,3,128,256]{3,2,1,0:T(8,128)(2,1)} %slice.43), channel_id=1, source_target_pairs={{2,0},{3,1},{4,2},{5,3},{6,4},{7,5},{8,6},{9,7},{10,8},{11,9},{12,... | collective-permute-start | bytes 1179656 | tf_op jit(solution)/shard_map/ppermute | solution.py:186
  97.7 13.0 %all-reduce = s32[168]{0:T(256)S(1)} all-reduce(s32[168]{0:T(256)S(1)} %add_dynamic-update-slice_fusion), channel_id=2, replica_groups=mesh['prow'=8,'pcol'=16] {'prow'}, use_global_device_ids=true, to_apply=%add | all-reduce | flops 168 | bytes 1344
  111.3 1.2 slice_bitcast_fusion.3
  112.6 1.5 collective-permute-start.12
  115.8 1.1 collective-permute-start.16
  119.1 13.5 %shard_map.46 = (f32[5,128,256]{2,1,0:T(8,128)S(1)}, bf16[5,128,256]{2,1,0:T(8,128)(2,1)S(1)}, bf16[3,128,256]{2,1,0:T(8,128)(2,1)S(1)}) custom-call(s32[8,21]{1,0:T(8,128)S(1)} %gather_fusion, bf16[10,2,128,128]{3,2,1,0:T(8,128)(2,1)S(1)} %get-tuple-element.30.obs_own, bf16[10,2,128,128]{3,2,1,0:T(8,128)(2,1)} %collective-permute-done.rest_0_, ...), custom_call_target="tpu_custom_call" | custom-call | flops 2264924160 | bytes 8388608 | tf_op jit(solution)/shard_map/pallas_call | solution.py:117
  132.7 4.9 %collective-permute-start.10 = (bf16[3,128,256]{2,1,0:T(8,128)(2,1)S(1)}, bf16[3,128,256]{2,1,0:T(8,128)(2,1)S(1)}, u32[]{:S(2)}, u32[]{:S(2)}) collective-permute-start(bf16[3,128,256]{2,1,0:T(8,128)(2,1)S(1)} %get-tuple-element.13), channel_id=1, source_target_pairs={{0,2},{1,3},{2,4},{3,5},{4,6},{5,7},{6,8},{7,9},{8,10},{9,11},{10,... | collective-permute-start | bytes 589832 | tf_op jit(solution)/shard_map/ppermute | solution.py:186
  137.6 2.5 %collective-permute-start.9 = (bf16[5,128,256]{2,1,0:T(8,128)(2,1)S(1)}, bf16[5,128,256]{2,1,0:T(8,128)(2,1)S(1)}, u32[]{:S(2)}, u32[]{:S(2)}) collective-permute-start(bf16[5,128,256]{2,1,0:T(8,128)(2,1)S(1)} %get-tuple-element.12), channel_id=1, source_target_pairs={{0,1},{1,2},{2,3},{3,4},{4,5},{5,6},{6,7},{7,8},{8,9},{9,10},{10,1... | collective-permute-start | bytes 983048 | tf_op jit(solution)/shard_map/ppermute | solution.py:186
  140.1 16.7 %collective-permute-done.11.rest_0_ = bf16[10,2,128,128]{3,2,1,0:T(8,128)(2,1)S(1)} collective-permute-done((bf16[10,2,128,128]{3,2,1,0:T(8,128)(2,1)}, bf16[10,2,128,128]{3,2,1,0:T(8,128)(2,1)S(1)}, u32[]{:S(2)}, u32[]{:S(2)}) %collective-permute-start.11) | collective-permute-done | bytes 655392 | tf_op jit(solution)/shard_map/ppermute | solution.py:180
  156.9 14.0 %shard_map.48 = (f32[5,128,256]{2,1,0:T(8,128)S(1)}, bf16[5,128,256]{2,1,0:T(8,128)(2,1)S(1)}, bf16[3,128,256]{2,1,0:T(8,128)(2,1)S(1)}) custom-call(s32[8,21]{1,0:T(8,128)S(1)} %gather_fusion, bf16[10,2,128,128]{3,2,1,0:T(8,128)(2,1)S(1)} %get-tuple-element.23.obs_own, bf16[10,2,128,128]{3,2,1,0:T(8,128)(2,1)S(1)} %collective-permute-done.11.rest_0_, ...), custom_call_target="tpu_custom_call" | custom-call | flops 2264924160 | bytes 8388608 | tf_op jit(solution)/shard_map/pallas_call | solution.py:117
  170.9 3.4 %collective-permute-start.18 = (bf16[5,128,256]{2,1,0:T(8,128)(2,1)S(1)}, bf16[5,128,256]{2,1,0:T(8,128)(2,1)S(1)}, u32[]{:S(2)}, u32[]{:S(2)}) collective-permute-start(bf16[5,128,256]{2,1,0:T(8,128)(2,1)S(1)} %get-tuple-element.15), channel_id=1, source_target_pairs={{0,1},{1,2},{2,3},{3,4},{4,5},{5,6},{6,7},{7,8},{8,9},{9,10},{10,1... | collective-permute-start | bytes 983048 | tf_op jit(solution)/shard_map/ppermute | solution.py:186
  174.3 1.1 fusion.4
  176.6 3.4 %all-to-all-start.1 = ((bf16[1,5,8,16,256]{4,3,1,0,2:T(8,128)(2,1)}), bf16[1,5,8,16,256]{4,3,1,0,2:T(8,128)(2,1)S(1)}, u32[]{:S(2)}, u32[]{:S(2)}) async-start(bf16[1,5,8,16,256]{4,3,1,0,2:T(8,128)(2,1)} %copy.29), calls=%async_computation.1 | async-start | bytes 655360 | tf_op jit(solution)/shard_map/all_to_all | solution.py:231
  180.0 5.5 %collective-permute-start.19 = (bf16[3,128,256]{2,1,0:T(8,128)(2,1)S(1)}, bf16[3,128,256]{2,1,0:T(8,128)(2,1)S(1)}, u32[]{:S(2)}, u32[]{:S(2)}) collective-permute-start(bf16[3,128,256]{2,1,0:T(8,128)(2,1)S(1)} %get-tuple-element.16), channel_id=1, source_target_pairs={{0,2},{1,3},{2,4},{3,5},{4,6},{5,7},{6,8},{7,9},{8,10},{9,11},{10,... | collective-permute-start | bytes 589832 | tf_op jit(solution)/shard_map/ppermute | solution.py:186
  185.6 6.2 %collective-permute-done.19.far = bf16[3,128,256]{2,1,0:T(8,128)(2,1)S(1)} collective-permute-done((bf16[3,128,256]{2,1,0:T(8,128)(2,1)S(1)}, bf16[3,128,256]{2,1,0:T(8,128)(2,1)S(1)}, u32[]{:S(2)}, u32[]{:S(2)}) %collective-permute-start.19) | collective-permute-done | bytes 196640 | tf_op jit(solution)/shard_map/ppermute | solution.py:186
  192.1 12.2 %all_to_all.45 = bf16[1,5,8,16,256]{4,3,1,0,2:T(8,128)(2,1)S(1)} all-to-all(bf16[1,5,8,16,256]{4,3,1,0,2:T(8,128)(2,1)S(1)} %copy.31), channel_id=1, replica_groups=mesh['prow'=8,'pcol'=16] {'prow'}, dimensions={2} | all-to-all | bytes 655360 | tf_op jit(solution)/shard_map/all_to_all | solution.py:231
  205.2 1.8 copy.41
  (62 shorter events, 12.8 us)
Async XLA Ops:
  3.3 24.1 %all-to-all-start = ((bf16[1,5,16,2,8,256]{5,2,1,3,0,4:T(8,128)(2,1)}), bf16[1,5,16,2,8,256]{5,2,1,3,0,4:T(8,128)(2,1)}, u32[]{:S(2)}, u32[]{:S(2)}) async-start(bf16[1,5,16,2,8,256]{5,2,1,3,0,4:T(8,128)(2,1)} %copy.22), calls=%async_computation | async-start | bytes 1310720 | tf_op jit(solution)/shard_map/all_to_all | solution.py:215
  7.7 18.1 %copy-start.4 = (s32[1,1,10,2]{2,3,1,0:T(2,128)S(1)}, s32[1,1,10,2]{2,3,1,0:T(2,128)}, u32[]{:S(2)}) copy-start(s32[1,1,10,2]{2,3,1,0:T(2,128)} %param.5) | copy-start | bytes 244
  7.7 18.3 %copy-start.5 = (u32[128]{0:T(128)S(1)}, u32[128]{0:T(128)}, u32[]{:S(2)}) copy-start(u32[128]{0:T(128)} %constant.167) | copy-start | bytes 1540
  17.0 11.8 %collective-permute-start.6 = (bf16[10,2,128,128]{3,2,1,0:T(8,128)(2,1)}, bf16[10,2,128,128]{3,2,1,0:T(8,128)(2,1)S(1)}, u32[]{:S(2)}, u32[]{:S(2)}) collective-permute-start(bf16[10,2,128,128]{3,2,1,0:T(8,128)(2,1)} %get-tuple-element.17), channel_id=1, source_target_pairs={{0,16},{16,0},{32,48},{48,32},{64,80},{80,64},{96,112},{112,96},{1... | collective-permute-start | bytes 1966088 | tf_op jit(solution)/shard_map/ppermute | solution.py:180
  17.6 19.3 %collective-permute-start.15 = (bf16[10,2,128,128]{3,2,1,0:T(8,128)(2,1)}, bf16[10,2,128,128]{3,2,1,0:T(8,128)(2,1)S(1)}, u32[]{:S(2)}, u32[]{:S(2)}) collective-permute-start(bf16[10,2,128,128]{3,2,1,0:T(8,128)(2,1)} %get-tuple-element.18), channel_id=1, source_target_pairs={{0,64},{16,80},{32,96},{48,112},{64,0},{80,16},{96,32},{112,48},{1... | collective-permute-start | bytes 1966088 | tf_op jit(solution)/shard_map/ppermute | solution.py:180
  20.7 29.2 %collective-permute-start.14 = (bf16[10,2,128,128]{3,2,1,0:T(8,128)(2,1)}, bf16[10,2,128,128]{3,2,1,0:T(8,128)(2,1)S(1)}, u32[]{:S(2)}, u32[]{:S(2)}) collective-permute-start(bf16[10,2,128,128]{3,2,1,0:T(8,128)(2,1)} %get-tuple-element.19), channel_id=1, source_target_pairs={{0,112},{16,96},{32,16},{48,0},{64,48},{80,32},{96,80},{112,64},{1... | collective-permute-start | bytes 1966088 | tf_op jit(solution)/shard_map/ppermute | solution.py:180
  21.6 32.1 %collective-permute-start.5 = (bf16[10,2,128,128]{3,2,1,0:T(8,128)(2,1)}, bf16[10,2,128,128]{3,2,1,0:T(8,128)(2,1)}, u32[]{:S(2)}, u32[]{:S(2)}) collective-permute-start(bf16[10,2,128,128]{3,2,1,0:T(8,128)(2,1)} %get-tuple-element.24), channel_id=1, source_target_pairs={{0,80},{16,64},{32,112},{48,96},{64,16},{80,0},{96,48},{112,32},{1... | collective-permute-start | bytes 1966088 | tf_op jit(solution)/shard_map/ppermute | solution.py:180
  23.1 42.6 %collective-permute-start.4 = (bf16[10,2,128,128]{3,2,1,0:T(8,128)(2,1)}, bf16[10,2,128,128]{3,2,1,0:T(8,128)(2,1)}, u32[]{:S(2)}, u32[]{:S(2)}) collective-permute-start(bf16[10,2,128,128]{3,2,1,0:T(8,128)(2,1)} %get-tuple-element.25), channel_id=1, source_target_pairs={{0,64},{16,80},{32,96},{48,112},{64,0},{80,16},{96,32},{112,48},{1... | collective-permute-start | bytes 1966088 | tf_op jit(solution)/shard_map/ppermute | solution.py:180
  28.8 63.3 %collective-permute-start.3 = (bf16[10,2,128,128]{3,2,1,0:T(8,128)(2,1)}, bf16[10,2,128,128]{3,2,1,0:T(8,128)(2,1)S(1)}, u32[]{:S(2)}, u32[]{:S(2)}) collective-permute-start(bf16[10,2,128,128]{3,2,1,0:T(8,128)(2,1)} %get-tuple-element.26), channel_id=1, source_target_pairs={{0,112},{16,96},{32,16},{48,0},{64,48},{80,32},{96,80},{112,64},{1... | collective-permute-start | bytes 1966088 | tf_op jit(solution)/shard_map/ppermute | solution.py:180
  36.8 75.7 %collective-permute-start.2 = (bf16[10,2,128,128]{3,2,1,0:T(8,128)(2,1)}, bf16[10,2,128,128]{3,2,1,0:T(8,128)(2,1)}, u32[]{:S(2)}, u32[]{:S(2)}) collective-permute-start(bf16[10,2,128,128]{3,2,1,0:T(8,128)(2,1)} %get-tuple-element.27), channel_id=1, source_target_pairs={{0,48},{16,32},{32,80},{48,64},{64,112},{80,96},{96,16},{112,0},{1... | collective-permute-start | bytes 1966088 | tf_op jit(solution)/shard_map/ppermute | solution.py:180
  50.0 62.6 %collective-permute-start.1 = (bf16[10,2,128,128]{3,2,1,0:T(8,128)(2,1)}, bf16[10,2,128,128]{3,2,1,0:T(8,128)(2,1)}, u32[]{:S(2)}, u32[]{:S(2)}) collective-permute-start(bf16[10,2,128,128]{3,2,1,0:T(8,128)(2,1)} %get-tuple-element.28), channel_id=1, source_target_pairs={{0,96},{16,112},{32,0},{48,16},{64,32},{80,48},{96,64},{112,80},{1... | collective-permute-start | bytes 1966088 | tf_op jit(solution)/shard_map/ppermute | solution.py:180
  53.7 60.5 %collective-permute-start = (bf16[10,2,128,128]{3,2,1,0:T(8,128)(2,1)}, bf16[10,2,128,128]{3,2,1,0:T(8,128)(2,1)}, u32[]{:S(2)}, u32[]{:S(2)}) collective-permute-start(bf16[10,2,128,128]{3,2,1,0:T(8,128)(2,1)} %get-tuple-element.29), channel_id=1, source_target_pairs={{0,32},{16,48},{32,64},{48,80},{64,96},{80,112},{96,0},{112,16},{1... | collective-permute-start | bytes 1966088 | tf_op jit(solution)/shard_map/ppermute | solution.py:180
  65.7 50.1 %collective-permute-start.7 = (bf16[2,5,128,256]{3,2,1,0:T(8,128)(2,1)}, bf16[2,5,128,256]{3,2,1,0:T(8,128)(2,1)}, u32[]{:S(2)}, u32[]{:S(2)}) collective-permute-start(bf16[2,5,128,256]{3,2,1,0:T(8,128)(2,1)} %fusion), channel_id=1, source_target_pairs={{1,0},{2,1},{3,2},{4,3},{5,4},{6,5},{7,6},{8,7},{9,8},{10,9},{11,1... | collective-permute-start | bytes 1966088 | tf_op jit(solution)/shard_map/ppermute | solution.py:186
  92.2 0.8 copy-start
  93.0 21.7 %collective-permute-start.8 = (bf16[2,3,128,256]{3,2,1,0:T(8,128)(2,1)}, bf16[2,3,128,256]{3,2,1,0:T(8,128)(2,1)}, u32[]{:S(2)}, u32[]{:S(2)}) collective-permute-start(bf16[2,3,128,256]{3,2,1,0:T(8,128)(2,1)} %slice.43), channel_id=1, source_target_pairs={{2,0},{3,1},{4,2},{5,3},{6,4},{7,5},{8,6},{9,7},{10,8},{11,9},{12,... | collective-permute-start | bytes 1179656 | tf_op jit(solution)/shard_map/ppermute | solution.py:186
  111.3 3.5 %copy-start.3 = (bf16[10,2,128,128]{3,2,1,0:T(8,128)(2,1)S(1)}, bf16[10,2,128,128]{3,2,1,0:T(8,128)(2,1)}, u32[]{:S(2)}) copy-start(bf16[10,2,128,128]{3,2,1,0:T(8,128)(2,1)} %get-tuple-element.31) | copy-start | bytes 1966084
  111.3 4.5 %copy-start.2 = (bf16[10,2,128,128]{3,2,1,0:T(8,128)(2,1)S(1)}, bf16[10,2,128,128]{3,2,1,0:T(8,128)(2,1)}, u32[]{:S(2)}) copy-start(bf16[10,2,128,128]{3,2,1,0:T(8,128)(2,1)} %get-tuple-element.32) | copy-start | bytes 1966084
  112.5 6.6 %copy-start.1 = (bf16[10,2,128,128]{3,2,1,0:T(8,128)(2,1)S(1)}, bf16[10,2,128,128]{3,2,1,0:T(8,128)(2,1)}, u32[]{:S(2)}) copy-start(bf16[10,2,128,128]{3,2,1,0:T(8,128)(2,1)} %copy-done) | copy-start | bytes 1966084
  112.6 20.1 %collective-permute-start.13 = (bf16[10,2,128,128]{3,2,1,0:T(8,128)(2,1)}, bf16[10,2,128,128]{3,2,1,0:T(8,128)(2,1)S(1)}, u32[]{:S(2)}, u32[]{:S(2)}) collective-permute-start(bf16[10,2,128,128]{3,2,1,0:T(8,128)(2,1)} %get-tuple-element.20), channel_id=1, source_target_pairs={{0,48},{16,32},{32,80},{48,64},{64,112},{80,96},{96,16},{112,0},{1... | collective-permute-start | bytes 1966088 | tf_op jit(solution)/shard_map/ppermute | solution.py:180
  112.6 25.0 %collective-permute-start.12 = (bf16[10,2,128,128]{3,2,1,0:T(8,128)(2,1)}, bf16[10,2,128,128]{3,2,1,0:T(8,128)(2,1)S(1)}, u32[]{:S(2)}, u32[]{:S(2)}) collective-permute-start(bf16[10,2,128,128]{3,2,1,0:T(8,128)(2,1)} %get-tuple-element.21), channel_id=1, source_target_pairs={{0,96},{16,112},{32,0},{48,16},{64,32},{80,48},{96,64},{112,80},{1... | collective-permute-start | bytes 1966088 | tf_op jit(solution)/shard_map/ppermute | solution.py:180
  114.2 42.7 %collective-permute-start.11 = (bf16[10,2,128,128]{3,2,1,0:T(8,128)(2,1)}, bf16[10,2,128,128]{3,2,1,0:T(8,128)(2,1)S(1)}, u32[]{:S(2)}, u32[]{:S(2)}) collective-permute-start(bf16[10,2,128,128]{3,2,1,0:T(8,128)(2,1)} %get-tuple-element.22), channel_id=1, source_target_pairs={{0,32},{16,48},{32,64},{48,80},{64,96},{80,112},{96,0},{112,16},{1... | collective-permute-start | bytes 1966088 | tf_op jit(solution)/shard_map/ppermute | solution.py:180
  114.7 42.1 %collective-permute-start.17 = (bf16[10,2,128,128]{3,2,1,0:T(8,128)(2,1)S(1)}, bf16[10,2,128,128]{3,2,1,0:T(8,128)(2,1)S(1)}, u32[]{:S(2)}, u32[]{:S(2)}) collective-permute-start(bf16[10,2,128,128]{3,2,1,0:T(8,128)(2,1)S(1)} %copy-done.3), channel_id=1, source_target_pairs={{0,16},{16,0},{32,48},{48,32},{64,80},{80,64},{96,112},{112,96},{1... | collective-permute-start | bytes 1966088 | tf_op jit(solution)/shard_map/ppermute | solution.py:180
  115.8 41.1 %collective-permute-start.16 = (bf16[10,2,128,128]{3,2,1,0:T(8,128)(2,1)S(1)}, bf16[10,2,128,128]{3,2,1,0:T(8,128)(2,1)S(1)}, u32[]{:S(2)}, u32[]{:S(2)}) collective-permute-start(bf16[10,2,128,128]{3,2,1,0:T(8,128)(2,1)S(1)} %copy-done.2), channel_id=1, source_target_pairs={{0,80},{16,64},{32,112},{48,96},{64,16},{80,0},{96,48},{112,32},{1... | collective-permute-start | bytes 1966088 | tf_op jit(solution)/shard_map/ppermute | solution.py:180
  132.7 42.8 %collective-permute-start.10 = (bf16[3,128,256]{2,1,0:T(8,128)(2,1)S(1)}, bf16[3,128,256]{2,1,0:T(8,128)(2,1)S(1)}, u32[]{:S(2)}, u32[]{:S(2)}) collective-permute-start(bf16[3,128,256]{2,1,0:T(8,128)(2,1)S(1)} %get-tuple-element.13), channel_id=1, source_target_pairs={{0,2},{1,3},{2,4},{3,5},{4,6},{5,7},{6,8},{7,9},{8,10},{9,11},{10,... | collective-permute-start | bytes 589832 | tf_op jit(solution)/shard_map/ppermute | solution.py:186
  137.6 37.9 %collective-permute-start.9 = (bf16[5,128,256]{2,1,0:T(8,128)(2,1)S(1)}, bf16[5,128,256]{2,1,0:T(8,128)(2,1)S(1)}, u32[]{:S(2)}, u32[]{:S(2)}) collective-permute-start(bf16[5,128,256]{2,1,0:T(8,128)(2,1)S(1)} %get-tuple-element.12), channel_id=1, source_target_pairs={{0,1},{1,2},{2,3},{3,4},{4,5},{5,6},{6,7},{7,8},{8,9},{9,10},{10,1... | collective-permute-start | bytes 983048 | tf_op jit(solution)/shard_map/ppermute | solution.py:186
  170.9 20.9 %collective-permute-start.18 = (bf16[5,128,256]{2,1,0:T(8,128)(2,1)S(1)}, bf16[5,128,256]{2,1,0:T(8,128)(2,1)S(1)}, u32[]{:S(2)}, u32[]{:S(2)}) collective-permute-start(bf16[5,128,256]{2,1,0:T(8,128)(2,1)S(1)} %get-tuple-element.15), channel_id=1, source_target_pairs={{0,1},{1,2},{2,3},{3,4},{4,5},{5,6},{6,7},{7,8},{8,9},{9,10},{10,1... | collective-permute-start | bytes 983048 | tf_op jit(solution)/shard_map/ppermute | solution.py:186
  176.6 15.6 %all-to-all-start.1 = ((bf16[1,5,8,16,256]{4,3,1,0,2:T(8,128)(2,1)}), bf16[1,5,8,16,256]{4,3,1,0,2:T(8,128)(2,1)S(1)}, u32[]{:S(2)}, u32[]{:S(2)}) async-start(bf16[1,5,8,16,256]{4,3,1,0,2:T(8,128)(2,1)} %copy.29), calls=%async_computation.1 | async-start | bytes 655360 | tf_op jit(solution)/shard_map/all_to_all | solution.py:231
  180.0 11.8 %collective-permute-start.19 = (bf16[3,128,256]{2,1,0:T(8,128)(2,1)S(1)}, bf16[3,128,256]{2,1,0:T(8,128)(2,1)S(1)}, u32[]{:S(2)}, u32[]{:S(2)}) collective-permute-start(bf16[3,128,256]{2,1,0:T(8,128)(2,1)S(1)} %get-tuple-element.16), channel_id=1, source_target_pairs={{0,2},{1,3},{2,4},{3,5},{4,6},{5,7},{6,8},{7,9},{8,10},{9,11},{10,... | collective-permute-start | bytes 589832 | tf_op jit(solution)/shard_map/ppermute | solution.py:186

commit v2 on v0

v2 whole, which is shorter than its diff:
```python
import functools

import jax
import jax.numpy as jnp
from jax import lax
from jax.experimental import pallas as pl
from jax.experimental.pallas import tpu as pltpu
from jax.sharding import PartitionSpec as P

BAND = 8
EPS = 1e-06
CURVE = 100.0
HOPS = ((1, 0), (3, 0), (1, 1), (3, 1), (0, 1), (2, 0), (2, 1))
STEPS = (1, 3, 2)
PLACES = (0, 2, 4, 3, 5, 1, 6, 7)
VMEM = pl.BlockSpec(memory_space=pltpu.VMEM)
SMEM = pl.BlockSpec(memory_space=pltpu.SMEM)
ANY = pl.BlockSpec(memory_space=pl.ANY)
HBM = pl.BlockSpec(memory_space=pltpu.HBM)
COPY_PARAMS = pltpu.CompilerParams(vmem_limit_bytes=55 * 1024 * 1024)
PARAMS = pltpu.CompilerParams(vmem_limit_bytes=40 * 1024 * 1024)


def setup_kernel(slots, meta, own, near, far, table0, table1, stack0, stack1, back0, back1):
    blocks, width, depth = own.shape[1:]
    reach = far.shape[1]
    span = blocks + reach + 1
    half = depth // 2
    for i in range(blocks * span):
        table0[i] = -1
        table1[i] = -1
    for k in range(8):

        def put(s, carry, k=k):
            a = meta[k, 1 + 2 * s]
            spot = a * span + meta[k, 2 + 2 * s] - a
            table0[spot] = k * slots + s
            table1[spot] = PLACES[k] * slots + s
            return carry

        lax.fori_loop(0, meta[k, 0], put, 0)
    for j, (stack, back) in enumerate(((stack0, back0), (stack1, back1))):
        for n in range(2 * blocks + reach):
            if n < blocks:
                block = own[j, n]
            elif n < 2 * blocks:
                block = near[j, n - blocks]
            else:
                block = far[j, n - 2 * blocks]
            turned = jnp.concatenate([block[:, half:], -block[:, :half]], axis=1)
            stack[n, :width] = block
            stack[n, width:] = turned
            if n < blocks:
                back[n, :width] = block
                back[n, width:] = -turned


def setup_call(slots, meta, own, near, far):
    blocks, width, depth = own.shape[1:]
    reach = far.shape[1]
    total = 2 * blocks + reach
    stack = jax.ShapeDtypeStruct((total, 2 * width, depth), own.dtype)
    back = jax.ShapeDtypeStruct((blocks, 2 * width, depth), own.dtype)
    return pl.pallas_call(
        functools.partial(setup_kernel, slots),
        out_shape=(
            jax.ShapeDtypeStruct((blocks * (blocks + reach + 1),), jnp.int32),
            jax.ShapeDtypeStruct((blocks * (blocks + reach + 1),), jnp.int32),
            stack,
            stack,
            back,
            back,
        ),
        in_specs=[SMEM, VMEM, VMEM, VMEM],
        out_specs=(SMEM, SMEM, VMEM, VMEM, VMEM, VMEM),
        compiler_params=PARAMS,
        name="setup",
    )(meta, own, near, far)


def slopes_of(table, held, upper, span, sums, b, low, high):
    width = upper.shape[0]
    pairs = []
    for a in range(low, high):
        spot = table[a * span + b - a]
        keep = spot >= 0
        spot = jnp.maximum(spot, 0)
        if a == high - 1:
            keep = jnp.logical_and(keep, jnp.logical_or(upper, a != b))
        halves = []
        for part in range(2):
            seen = held[spot, part].astype(jnp.float32) * width
            place = (a - low) * width
            diff = sums[place : place + width, part * width : (part + 1) * width] - seen
            slope = diff * lax.rsqrt(diff * diff * CURVE + float(width * width))
            halves.append(jnp.where(keep, slope, 0.0).astype(jnp.bfloat16))
        pairs.append(halves)
    return pairs


def products(back, block, low, high):
    width = back.shape[1] // 2
    rows = jnp.concatenate([back[a, :width] for a in range(low, high)], axis=0)
    return lax.dot_general(
        rows, block, (((1,), (1,)), ((), ())), preferred_element_type=jnp.float32
    )


def turned_product(slopes, back, a, first, last):
    left = jnp.concatenate([slopes[a, d] for d in range(first, last)], axis=1)
    return lax.dot_general(
        left, back[a], (((0,), (0,)), ((), ())), preferred_element_type=jnp.float32
    )


def upper_of(width):
    return lax.broadcasted_iota(jnp.int32, (width, width), 1) > lax.broadcasted_iota(
        jnp.int32, (width, width), 0
    )


def row_range(b, blocks, span):
    return max(0, b - span + 1), min(blocks, b + 1)


def side_kernel(start, table, held, stack, back, slopes, out, grad):
    blocks, double, depth = back.shape
    width = double // 2
    reach = stack.shape[0] - 2 * blocks
    span = blocks + reach + 1
    count = out.shape[0]
    upper = upper_of(width)
    grad[...] = jnp.zeros_like(grad)

    def column(b, low, high):
        sums = products(back, stack[b], low, high)
        pairs = slopes_of(table, held, upper, span, sums, b, low, high)
        for a in range(low, high):
            for part in range(2):
                slopes[a, b - start, part * width : (part + 1) * width] = pairs[a - low][part]

    def full(b, carry):
        column(b, 0, blocks)
        return carry

    stop = start + count
    lax.fori_loop(start, max(start, min(stop, span)), full, 0)
    for b in range(max(start, span), stop):
        column(b, *row_range(b, blocks, span))
    for a in range(blocks):
        last = min(stop, a + span)
        if last <= start:
            continue
        add = turned_product(slopes, back, a, 0, last - start)
        for b in range(start, last):
            grad[b - start] += add[(b - start) * width : (b - start + 1) * width]
    out[...] = grad[...].astype(jnp.bfloat16)


def nearby_kernel(table, held, stack, back, close, distant, grad, fresh):
    blocks, double, depth = back.shape
    width = double // 2
    total = stack.shape[0]
    reach = total - 2 * blocks
    span = blocks + reach + 1
    upper = upper_of(width)
    grad[...] = jnp.zeros_like(grad)

    def rows(b, low, high, wide):
        add = jnp.dot(jnp.concatenate(wide, axis=0), stack[b], preferred_element_type=jnp.float32)
        for a in range(low, high):
            grad[a] += add[(a - low) * width : (a - low + 1) * width]

    for b in range(blocks):
        sums = products(back, stack[b], 0, b + 1)
        pairs = slopes_of(table, held, upper, span, sums, b, 0, b + 1)
        for a in range(b + 1):
            for part in range(2):
                fresh[a, b - a, part * width : (part + 1) * width] = pairs[a][part]
        rows(b, 0, b + 1, [jnp.concatenate(pair, axis=1) for pair in pairs])

    def kept(slopes, a, n):
        return jnp.concatenate([slopes[a, n, :width], slopes[a, n, width:]], axis=1)

    def full(b, carry):
        rows(b, 0, blocks, [kept(close, a, b - blocks) for a in range(blocks)])
        return carry

    lax.fori_loop(blocks, span, full, 0)
    for b in range(span, total):
        low, high = row_range(b, blocks, span)
        slopes, first = (close, blocks) if b < 2 * blocks else (distant, 2 * blocks)
        rows(b, low, high, [kept(slopes, a, b - first) for a in range(low, high)])
    for a in range(blocks):
        add = turned_product(fresh, back, a, 0, blocks - a)
        for d in range(blocks - a):
            grad[a + d] += add[d * width : (d + 1) * width]


def cost(tiles, width, depth):
    return pl.CostEstimate(
        flops=tiles * 6 * width * depth * depth,
        bytes_accessed=tiles * 512 * 1024,
        transcendentals=0,
    )


def side_call(start, count, table, held, stack, back):
    blocks, double, depth = back.shape
    width = double // 2
    return pl.pallas_call(
        functools.partial(side_kernel, start),
        out_shape=(
            jax.ShapeDtypeStruct((blocks, count, double, width), jnp.bfloat16),
            jax.ShapeDtypeStruct((count, width, depth), jnp.bfloat16),
        ),
        in_specs=[SMEM] + [VMEM] * 3,
        out_specs=(VMEM, VMEM),
        scratch_shapes=[pltpu.VMEM((count, width, depth), jnp.float32)],
        compiler_params=PARAMS,
        cost_estimate=cost(4 * count, width, depth),
        name="side",
    )(table, held, stack, back)


def nearby_call(table, held, stack, back, close, distant):
    blocks, double, depth = back.shape
    width = double // 2
    return pl.pallas_call(
        nearby_kernel,
        out_shape=jax.ShapeDtypeStruct((blocks, width, depth), jnp.float32),
        in_specs=[SMEM] + [VMEM] * 5,
        out_specs=VMEM,
        scratch_shapes=[pltpu.VMEM((blocks, blocks, double, width), jnp.bfloat16)],
        compiler_params=PARAMS,
        cost_estimate=cost(20, width, depth),
        name="nearby",
    )(table, held, stack, back, close, distant)


def gather(pieces, held, sems):
    slots = pieces[0].shape[0]
    copies = [
        pltpu.make_async_copy(piece, held.at[pl.ds(k * slots, slots)], sems.at[k])
        for k, piece in enumerate(pieces)
    ]
    for copy in copies:
        copy.start()
    return copies


def collect_kernel(j, place, obs, pair, first, second, third, held, sems):
    slots = pair.shape[0]
    parts = [obs.at[:, j, place[0], place[1]], pair.at[:, place[0]], first, second, third]
    starts = [0, 1, 2, 4, 6]
    copies = [
        pltpu.make_async_copy(
            part, held.at[pl.ds(start * slots, part.shape[0])], sems.at[k]
        )
        for k, (part, start) in enumerate(zip(parts, starts))
    ]
    for copy in copies:
        copy.start()
    for copy in copies:
        copy.wait()


def collect_call(j, place, obs, pair, arrived):
    slots = pair.shape[0]
    return pl.pallas_call(
        functools.partial(collect_kernel, j),
        out_shape=jax.ShapeDtypeStruct((8 * slots,) + pair.shape[2:], pair.dtype),
        in_specs=[SMEM, HBM] + [ANY] * 4,
        out_specs=VMEM,
        scratch_shapes=[pltpu.SemaphoreType.DMA((5,))],
        compiler_params=PARAMS,
        name="collect",
    )(place, obs, pair, *arrived)


def swap_kernel(j, place, obs, out, sem):
    copy = pltpu.make_async_copy(obs.at[:, j, :, 1 - place[1]], out, sem)
    copy.start()
    copy.wait()


def swap_call(j, place, obs):
    slots, _, chips = obs.shape[:3]
    return pl.pallas_call(
        functools.partial(swap_kernel, j),
        out_shape=jax.ShapeDtypeStruct((slots, chips) + obs.shape[4:], obs.dtype),
        in_specs=[SMEM, HBM],
        out_specs=VMEM,
        scratch_shapes=[pltpu.SemaphoreType.DMA(())],
        compiler_params=COPY_PARAMS,
        name="swap",
    )(place, obs)


def pack_kernel(j, place, obs, pair, first, second, third, sems):
    chips = pair.shape[1]
    copies = []
    for k, (step, out) in enumerate(zip(STEPS, (first, second, third))):
        chip = lax.rem(place[0] + step, chips)
        copies.append((obs.at[:, j, chip, place[1]], out.at[pl.ds(0, out.shape[0] // 2)], 2 * k))
        copies.append((pair.at[:, chip], out.at[pl.ds(out.shape[0] // 2, out.shape[0] // 2)], 2 * k + 1))
    copies = [pltpu.make_async_copy(src, dst, sems.at[k]) for src, dst, k in copies]
    for copy in copies:
        copy.start()
    for copy in copies:
        copy.wait()


def pack_call(j, place, obs, pair):
    slots = pair.shape[0]
    out = jax.ShapeDtypeStruct((2 * slots,) + pair.shape[2:], pair.dtype)
    return pl.pallas_call(
        functools.partial(pack_kernel, j),
        out_shape=(out, out, out),
        in_specs=[SMEM, HBM, ANY],
        out_specs=(VMEM, VMEM, VMEM),
        scratch_shapes=[pltpu.SemaphoreType.DMA((6,))],
        compiler_params=COPY_PARAMS,
        name="pack",
    )(place, obs, pair)


def tile_kernel(table, *refs):
    stack, back, grad_own, grad_near, grad_far, held, slopes, grad, sems = refs[8:]
    blocks, double, _ = back.shape
    width = double // 2
    total = stack.shape[0]
    reach = total - 2 * blocks
    span = blocks + reach + 1
    copies = gather(refs[:8], held, sems)
    grad[...] = jnp.zeros_like(grad)
    upper = upper_of(width)
    for copy in copies:
        copy.wait()

    def column(b, low, high):
        pairs = slopes_of(
            table, held, upper, span, products(back, stack[b], low, high), b, low, high
        )
        wide = []
        for a in range(low, high):
            for part in range(2):
                slopes[a, b - a, part * width : (part + 1) * width] = pairs[a - low][part]
            wide.append(jnp.concatenate(pairs[a - low], axis=1))
        add = jnp.dot(jnp.concatenate(wide, axis=0), stack[b], preferred_element_type=jnp.float32)
        for a in range(low, high):
            grad[a] += add[(a - low) * width : (a - low + 1) * width]

    for b in range(blocks - 1):
        column(b, 0, b + 1)

    def full(b, carry):
        column(b, 0, blocks)
        return carry

    lax.fori_loop(blocks - 1, span, full, 0)
    for b in range(span, total):
        column(b, *row_range(b, blocks, span))

    def mirror(a, carry):
        add = turned_product(slopes, back, a, 0, span)
        for d in range(span):
            grad[a + d] += add[d * width : (d + 1) * width]
        return carry

    lax.fori_loop(0, blocks, mirror, 0)
    grad_own[...] = grad[:blocks]
    grad_near[...] = grad[blocks : 2 * blocks].astype(jnp.bfloat16)
    grad_far[...] = grad[2 * blocks :].astype(jnp.bfloat16)


def tile_call(table, pieces, stack, back):
    slots = pieces[0].shape[0]
    blocks, double, depth = back.shape
    width = double // 2
    total = stack.shape[0]
    reach = total - 2 * blocks
    span = blocks + reach + 1
    return pl.pallas_call(
        tile_kernel,
        out_shape=(
            jax.ShapeDtypeStruct((blocks, width, depth), jnp.float32),
            jax.ShapeDtypeStruct((blocks, width, depth), jnp.bfloat16),
            jax.ShapeDtypeStruct((reach, width, depth), jnp.bfloat16),
        ),
        in_specs=[SMEM] + [ANY] * 8 + [VMEM] * 2,
        out_specs=(VMEM, VMEM, VMEM),
        scratch_shapes=[
            pltpu.VMEM((8 * slots, 2, width, width), jnp.bfloat16),
            pltpu.VMEM((blocks, span, double, width), jnp.bfloat16),
            pltpu.VMEM((total, width, depth), jnp.float32),
            pltpu.SemaphoreType.DMA((8,)),
        ],
        compiler_params=PARAMS,
        cost_estimate=cost(0, width, depth),
        name="tiles",
    )(table, *pieces, stack, back)


def final_kernel(spectra, own0, near0, far0, own1, near1, far1, out):
    for j, (own, near, far) in enumerate(((own0, near0, far0), (own1, near1, far1))):
        blocks = own.shape[0]
        reach = far.shape[0]
        scale = 2.0 / spectra.shape[-1]
        for n in range(blocks):
            values = spectra[j, n].astype(jnp.float32)
            power = jnp.sum(values * values, axis=1, keepdims=True) * scale
            factor = lax.rsqrt(power + EPS)
            total = own[n] + near[n].astype(jnp.float32)
            if n < reach:
                total = total + far[n].astype(jnp.float32)
            inner = jnp.sum(total * values, axis=1, keepdims=True) * scale
            grad = factor * total - values * (factor * factor * factor * inner)
            share = grad.shape[0] // 8
            for r in range(8):
                out[r, j, n] = grad[r * share : (r + 1) * share].astype(jnp.bfloat16)


def final_call(spectra, sums0, sums1):
    _, blocks, width, depth = spectra.shape
    return pl.pallas_call(
        final_kernel,
        out_shape=jax.ShapeDtypeStruct((8, 2, blocks, width // 8, depth), jnp.bfloat16),
        in_specs=[VMEM] * 7,
        out_specs=VMEM,
        compiler_params=PARAMS,
        name="final",
    )(spectra, *sums0, *sums1)


def route_across(step, flip):
    chips = lax.axis_size("prow") // 2
    return "prow", [
        (2 * y + c, 2 * ((y + step) % chips) + (c ^ flip)) for y in range(chips) for c in range(2)
    ]


def route_along(distance):
    devices = range(lax.axis_size("pcol"))
    return "pcol", [(i - distance, i) for i in devices if i - distance in devices]


def send(values, route, after=None):
    if after is not None:
        values, _ = lax.optimization_barrier((values, after))
    return lax.ppermute(values, *route)


def local(spectra, tile_list, tile_count, observed):
    blocks, share, bins, parts, windows = spectra.shape
    slots = tile_list.shape[2]
    width = 8 * share
    depth = parts * windows
    reach = BAND - blocks
    me = lax.axis_index("prow")
    chip = me // 2
    core = me % 2
    base = lax.axis_index("pcol") * blocks
    targets = [(chip + step) % 4 * 2 + (core ^ flip) for step, flip in HOPS]
    lists = [me] + [(chip - step) % 4 * 2 + (core ^ flip) for step, flip in HOPS]
    routes = [route_across(*hop) for hop in HOPS]
    obs = observed[0, 0]

    meta = jnp.concatenate([tile_count.reshape(1), (tile_list - base).reshape(-1)])
    count = meta.shape[0]
    meta = jnp.pad(meta.astype(jnp.bfloat16).reshape(1, count), ((0, share - 1), (0, depth - count)))
    load = spectra.reshape(blocks, share, 2, 8, depth).transpose(3, 2, 0, 1, 4)
    load = load.reshape(8, 2 * blocks, share, depth)
    load = jnp.concatenate([load, jnp.broadcast_to(meta, (8, 1) + meta.shape)], axis=1)

    def cut(data, j, k):
        return lax.dynamic_index_in_dim(data, 8 * j + targets[k], 1, keepdims=False)

    early = [cut(obs, 0, k) for k in range(2)]
    early, load, obs = lax.optimization_barrier((early, load, obs))
    load = lax.all_to_all(load, "prow", split_axis=0, concat_axis=0, tiled=True)
    parts0 = early + [cut(obs, 0, k) for k in range(2, 4)]
    _, obs = lax.optimization_barrier((parts0[2:], obs))
    parts0 += [cut(obs, 0, k) for k in range(4, 7)]
    load, _ = lax.optimization_barrier((load, parts0))
    sent0 = [send(parts0[k], routes[k]) for k in range(4)]
    sent0.append(send(parts0[4], routes[4], sent0[0]))
    sent0.append(send(parts0[5], routes[5], sent0[0]))
    sent0.append(send(parts0[6], routes[6], sent0[1]))
    whole_obs = observed.reshape((slots, 2, 4, 2) + observed.shape[4:])
    place = jnp.stack([chip, core])
    place, _ = lax.optimization_barrier((place, parts0[2:4]))
    swapped = swap_call(1, place, whole_obs)
    load, swapped = lax.optimization_barrier((load, swapped))
    pair = send(swapped, route_across(0, 1), sent0[:4])
    meta = load[:, -1, 0, :count].astype(jnp.int32)[jnp.stack(lists)]
    mine = load[:, :-1].reshape(8, 2, blocks, share, depth)
    mine = mine.transpose(1, 2, 0, 3, 4).reshape(2, blocks, width, depth)
    values = mine.astype(jnp.float32)
    power = jnp.sum(values * values, axis=-1, keepdims=True) / windows
    white = (values * lax.rsqrt(power + EPS)).astype(jnp.bfloat16)
    near = send(white, route_along(-1))
    far = send(white[:, :reach], route_along(-2))
    packed = pack_call(1, place, whole_obs, pair)
    sent1 = [
        send(part, route_across(step, 0), after)
        for part, step, after in zip(packed, STEPS, ((near, sent0[5]), (far, sent0[6]), sent0[4]))
    ]
    table0, table1, stack0, stack1, back0, back1 = setup_call(slots, meta, white, near, far)

    own = lax.dynamic_index_in_dim(obs, me, 1, keepdims=False)
    own_sum, near_sum, far_sum = tile_call(table0, [own] + sent0, stack0, back0)
    sums0 = own_sum, send(near_sum, route_along(1)), send(far_sum, route_along(2))
    sent1, sums0 = lax.optimization_barrier((sent1, sums0))
    held = collect_call(1, place, whole_obs, pair, sent1)
    distant, far_sum = side_call(2 * blocks, reach, table1, held, stack1, back1)
    far_sum, held = lax.optimization_barrier((far_sum, held))
    far_sum = send(far_sum, route_along(2))
    close, near_sum = side_call(blocks, blocks, table1, held, stack1, back1)
    near_sum = send(near_sum, route_along(1))
    own_sum = nearby_call(table1, held, stack1, back1, close, distant)
    grad = final_call(mine, sums0, (own_sum, near_sum, far_sum))
    grad = lax.all_to_all(grad, "prow", split_axis=0, concat_axis=0, tiled=True)
    whole = grad.transpose(2, 3, 1, 0, 4).reshape(blocks, share, bins, parts, windows)
    return whole.astype(jnp.float32)


def solution(mesh):
    placed = (
        P("pcol", "prow", None, None, None),
        P("prow", "pcol", None, None),
        P("prow", "pcol"),
        P("prow", "pcol", None, None, None, None, None),
    )
    return jax.shard_map(
        local,
        mesh=mesh,
        in_specs=placed,
        out_specs=P("pcol", "prow", None, None, None),
        check_vma=False,
    )
```

time: 834 us -> 186 us (0.22)
  waiting for transfers between devices: 465 us -> 63.4 us
  matrix products: 87.4 us -> 0 us
  other arithmetic: 69.1 us -> 2.98 us
  local copies, waits for them, and re-layouts: 85.1 us -> 31.9 us
  starting transfers between devices: 89.7 us -> 41.3 us
  Pallas kernels: 0 us -> 30.2 us
  loops' own time: 20.9 us -> 0 us
  blocking collectives: 0 us -> 14.7 us
  between operations: 13.5 us -> 1.12 us
    ppermute x4 -> x17, waiting for transfers between devices: 308 us -> 42.6 us  [send(): return lax.ppermute(values, *route)]
    reduce_scatter x1 -> x0, waiting for transfers between devices: 119 us -> none  [local(): lax.psum_scatter(own_terms, 'prow', scatter_dimension=1, tiled=True)]
    dot_general x36 -> x0, matrix products: 87.4 us -> none  [the longest x6 30.6 us: tile_terms(): jnp.einsum('fij,jfkw->ifkw', slope_imag, col_turn, preferred_element_type...]
    ppermute x4 -> x17, starting transfers between devices: 89.7 us -> 37.7 us  [send(): return lax.ppermute(values, *route)]
    all_gather x1 -> x0, waiting for transfers between devices: 38.6 us -> none  [local(): complete = lax.all_gather(whitened, 'prow', axis=1, tiled=True)]
    while x49 -> x0, local copies, waits for them, and re-layouts: 32.9 us -> none  [the longest x1 28.6 us: local(): lax.fori_loop(0, own_count, lambda slot_id, buffer_now: add_tile(buffer_n...]
    pallas_call x0 -> x9, Pallas kernels: none -> 30.2 us  [the longest x1 8.88 us: tile_call(): pl.pallas_call(tile_kernel, out_shape=(jax.ShapeDtypeStruct((blocks, widt...]
    another operation x1 -> x0, loops' own time: 20.9 us -> none  [local(): lax.fori_loop(0, own_count, lambda slot_id, buffer_now: add_tile(buffer_n...]
  transfers between devices with their start and end apart: 6 -> 18, of which waited for: 6 -> 9; matrix products, arithmetic and copies ran while one was open for 3% -> 6% of each run, Pallas kernels for 0% -> 12%
where the time goes in v2:
time: 186 us
  waiting for transfers between devices  63.4 us (34%)
  starting transfers between devices  41.3 us (22%)
  local copies, waits for them, and re-layouts  31.9 us (17%)
  Pallas kernels  30.2 us (16%)
  blocking collectives  14.7 us (8%)
  other arithmetic  2.98 us (2%)
    ppermute x17, waiting for transfers between devices, send(): return lax.ppermute(values, *route)  42.6 us
    ppermute x17, starting transfers between devices, send(): return lax.ppermute(values, *route)  37.7 us
    all_to_all x1, waiting for transfers between devices, local(): load = lax.all_to_all(load, 'prow', split_axis=0, concat_axis=0, tiled=True)  20.7 us
    unnamed x52, local copies, waits for them, and re-layouts  15.1 us
    all_to_all x1, blocking collectives, local(): grad = lax.all_to_all(grad, 'prow', split_axis=0, concat_axis=0, tiled=True)  14.7 us
    pallas_call x1, Pallas kernels, tile_call(): pl.pallas_call(tile_kernel, out_shape=(jax.ShapeDtypeStruct((blocks, widt...  8.88 us
    squeeze x2, local copies, waits for them, and re-layouts, cut(): return lax.dynamic_index_in_dim(data, 8 * j + targets[k], 1, keepdims=False)  5.01 us
    pallas_call x1, Pallas kernels, pack_call(): pl.pallas_call(functools.partial(pack_kernel, j), out_shape=(out, out, ou...  4.77 us
  transfers between devices with their start and end apart: 18, of which 9 were waited for; matrix products, arithmetic and copies ran while one was open for 6% of the time, Pallas kernels for 12%

profile of v2, /device:TPU:32, one launch (start us, length us, event | category | flops | bytes accessed | tf_op | source)
XLA Modules:
  0.0 185.6 jit_solution(5719139005866448639)
XLA Ops:
  1.5 2.2 %reshape.386 = bf16[5,16,2,8,256]{4,3,2,1,0:T(8,128)(2,1)S(1)} reshape(bf16[5,16,16,2,128]{4,3,2,1,0:T(2,128)(2,1)} %param.4) | data formatting | bytes 1310720 | tf_op jit(solution)/shard_map/reshape | solution.py:472
  5.0 2.5 %dynamic-slice_bitcast_fusion.6 = (bf16[10,2,128,128]{3,2,1,0:T(8,128)(2,1)}, bf16[10,2,128,128]{3,2,1,0:T(8,128)(2,1)}) fusion(bf16[1,1,10,16,2,128,128]{6,5,4,3,2,1,0:T(8,128)(2,1)} %param.7, s32[]{:T(128)S(6)} %select_n.93, s32[]{:T(128)S(6)} %select_n.91), kind=kLoop, calls=%fused_computation.11 | loop fusion | bytes 2621448 | tf_op jit(solution)/shard_map/jit(dynamic_index_in_dim)/squeeze | solution.py:477
  7.5 1.6 collective-permute-start
  9.1 1.7 collective-permute-start.1
  10.7 2.5 %dynamic-slice_bitcast_fusion.4 = (bf16[10,2,128,128]{3,2,1,0:T(8,128)(2,1)}, bf16[10,2,128,128]{3,2,1,0:T(8,128)(2,1)}) fusion(bf16[10,16,2,128,128]{4,3,2,1,0:T(8,128)(2,1)} %bitcast.51, s32[]{:T(128)S(6)} %select_n.95, s32[]{:T(128)S(6)} %select_n.94), kind=kLoop, calls=%fused_computation.9 | loop fusion | bytes 2621448 | tf_op jit(solution)/shard_map/jit(dynamic_index_in_dim)/squeeze | solution.py:477
  13.3 3.0 %collective-permute-start.3 = (bf16[10,2,128,128]{3,2,1,0:T(8,128)(2,1)}, bf16[10,2,128,128]{3,2,1,0:T(8,128)(2,1)S(1)}, u32[]{:S(2)}, u32[]{:S(2)}) collective-permute-start(bf16[10,2,128,128]{3,2,1,0:T(8,128)(2,1)} %get-tuple-element.89), channel_id=1, source_target_pairs={{0,112},{16,96},{32,16},{48,0},{64,48},{80,32},{96,80},{112,64},{1... | collective-permute-start | bytes 1966088 | tf_op jit(solution)/shard_map/ppermute | solution.py:451
  16.2 3.5 %all-to-all-start = ((bf16[8,11,16,256]{3,2,1,0:T(8,128)(2,1)}), bf16[8,11,16,256]{3,2,1,0:T(8,128)(2,1)S(1)}, u32[]{:S(2)}, u32[]{:S(2)}) async-start(bf16[8,11,16,256]{3,2,1,0:T(8,128)(2,1)} %pad_maximum_fusion), calls=%async_computation | async-start | bytes 1441792 | tf_op jit(solution)/shard_map/all_to_all | solution.py:481
  20.4 3.9 %swap.1 = bf16[10,4,2,128,128]{4,3,2,1,0:T(8,128)(2,1)} custom-call(s32[2]{0:T(128)} %pad_add_fusion.place, bf16[10,2,4,2,2,128,128]{6,5,4,3,2,1,0:T(8,128)(2,1)} %bitcast.52), custom_call_target="tpu_custom_call" | custom-call | tf_op jit(solution)/shard_map/swap/pallas_call | solution.py:289
  24.3 3.3 %dynamic-slice_bitcast_fusion = (bf16[10,2,128,128]{3,2,1,0:T(8,128)(2,1)}, bf16[10,2,128,128]{3,2,1,0:T(8,128)(2,1)}, bf16[10,2,128,128]{3,2,1,0:T(8,128)(2,1)}, bf16[10,2,128,128]{3,2,1,0:T(8,128)(2,1)}) fusion(bf16[10,16,2,128,128]{4,3,2,1,0:T(8,128)(2,1)} %bitcast.53, s32[]{:T(128)S(6)} %select_n.105, s32[]{:T(128)S(6)} %select_n.100, s32[]{:T(128)S(6)} %select_n.99, ...), kind=kLoop, calls=%fused_computation.5 | loop fusion | bytes 5242896 | tf_op jit(solution)/shard_map/jit(dynamic_index_in_dim)/squeeze | solution.py:511
  27.7 20.7 %all-to-all-done = bf16[8,11,16,256]{3,2,1,0:T(8,128)(2,1)S(1)} async-done(((bf16[8,11,16,256]{3,2,1,0:T(8,128)(2,1)}), bf16[8,11,16,256]{3,2,1,0:T(8,128)(2,1)S(1)}, u32[]{:S(2)}, u32[]{:S(2)}) %all-to-all-start) | async-done | bytes 720928 | tf_op jit(solution)/shard_map/all_to_all | solution.py:481
  54.7 4.2 %collective-permute-start.5 = (bf16[2,5,128,256]{3,2,1,0:T(8,128)(2,1)S(1)}, bf16[2,5,128,256]{3,2,1,0:T(8,128)(2,1)S(1)}, u32[]{:S(2)}, u32[]{:S(2)}) collective-permute-start(bf16[2,5,128,256]{3,2,1,0:T(8,128)(2,1)S(1)} %multiply_convert_fusion.own), channel_id=1, source_target_pairs={{1,0},{2,1},{3,2},{4,3},{5,4},{6,5},{7,6},{8,7},{9,8},{10,9},{11,1... | collective-permute-start | bytes 1966088 | tf_op jit(solution)/shard_map/ppermute | solution.py:451
  58.9 2.9 %collective-permute-start.6 = (bf16[10,2,128,128]{3,2,1,0:T(8,128)(2,1)S(1)}, bf16[10,2,128,128]{3,2,1,0:T(8,128)(2,1)S(1)}, u32[]{:S(2)}, u32[]{:S(2)}) collective-permute-start(bf16[10,2,128,128]{3,2,1,0:T(8,128)(2,1)S(1)} %copy-done.25), channel_id=1, source_target_pairs={{0,64},{16,80},{32,96},{48,112},{64,0},{80,16},{96,32},{112,48},{1... | collective-permute-start | bytes 1966088 | tf_op jit(solution)/shard_map/ppermute | solution.py:451
  61.8 2.7 %collective-permute-start.8 = (bf16[2,3,128,256]{3,2,1,0:T(8,128)(2,1)S(1)}, bf16[2,3,128,256]{3,2,1,0:T(8,128)(2,1)S(1)}, u32[]{:S(2)}, u32[]{:S(2)}) collective-permute-start(bf16[2,3,128,256]{3,2,1,0:T(8,128)(2,1)S(1)} %slice.14), channel_id=1, source_target_pairs={{2,0},{3,1},{4,2},{5,3},{6,4},{7,5},{8,6},{9,7},{10,8},{11,9},{12,... | collective-permute-start | bytes 1179656 | tf_op jit(solution)/shard_map/ppermute | solution.py:451
  64.6 4.8 %pack.1 = (bf16[20,2,128,128]{3,2,1,0:T(8,128)(2,1)}, bf16[20,2,128,128]{3,2,1,0:T(8,128)(2,1)}, bf16[20,2,128,128]{3,2,1,0:T(8,128)(2,1)}) custom-call(s32[2]{0:T(128)} %pad_add_fusion.place, bf16[10,2,4,2,2,128,128]{6,5,4,3,2,1,0:T(8,128)(2,1)} %bitcast.54, bf16[10,4,2,128,128]{4,3,2,1,0:T(8,128)(2,1)} %copy-done), custom_call_target="tpu_custom_call" | custom-call | tf_op jit(solution)/shard_map/pack/pallas_call | solution.py:317
  71.0 5.2 %collective-permute-done.8.far = bf16[2,3,128,256]{3,2,1,0:T(8,128)(2,1)S(1)} collective-permute-done((bf16[2,3,128,256]{3,2,1,0:T(8,128)(2,1)S(1)}, bf16[2,3,128,256]{3,2,1,0:T(8,128)(2,1)S(1)}, u32[]{:S(2)}, u32[]{:S(2)}) %collective-permute-start.8) | collective-permute-done | bytes 393248 | tf_op jit(solution)/shard_map/ppermute | solution.py:451
  77.7 1.8 collective-permute-start.10
  79.5 2.4 %collective-permute-done.5.near = bf16[2,5,128,256]{3,2,1,0:T(8,128)(2,1)S(1)} collective-permute-done((bf16[2,5,128,256]{3,2,1,0:T(8,128)(2,1)S(1)}, bf16[2,5,128,256]{3,2,1,0:T(8,128)(2,1)S(1)}, u32[]{:S(2)}, u32[]{:S(2)}) %collective-permute-start.5) | collective-permute-done | bytes 655392 | tf_op jit(solution)/shard_map/ppermute | solution.py:451
  82.8 4.3 %collective-permute-done.6.refs_6_ = bf16[10,2,128,128]{3,2,1,0:T(8,128)(2,1)S(1)} collective-permute-done((bf16[10,2,128,128]{3,2,1,0:T(8,128)(2,1)S(1)}, bf16[10,2,128,128]{3,2,1,0:T(8,128)(2,1)S(1)}, u32[]{:S(2)}, u32[]{:S(2)}) %collective-permute-start.6) | collective-permute-done | bytes 655392 | tf_op jit(solution)/shard_map/ppermute | solution.py:451
  93.4 2.0 %setup.1 = (s32[45]{0:T(128)S(1)}, s32[45]{0:T(128)S(1)}, bf16[13,256,256]{2,1,0:T(8,128)(2,1)S(1)}, bf16[13,256,256]{2,1,0:T(8,128)(2,1)S(1)}, bf16[5,256,256]{...) custom-call(s32[8,21]{1,0:T(8,128)S(1)} %gather_fusion, bf16[2,5,128,256]{3,2,1,0:T(8,128)(2,1)S(1)} %copy-done.3, ...), custom_call_target="tpu_custom_call" | custom-call | tf_op jit(solution)/shard_map/setup/pallas_call | solution.py:64
  100.9 8.9 %tiles.1 = (f32[5,128,256]{2,1,0:T(8,128)S(1)}, bf16[5,128,256]{2,1,0:T(8,128)(2,1)S(1)}, bf16[3,128,256]{2,1,0:T(8,128)(2,1)S(1)}) custom-call(s32[45]{0:T(128)S(1)} %get-tuple-element.64.table, bf16[10,2,128,128]{3,2,1,0:T(8,128)(2,1)S(1)} %copy-done.4, bf16[10,2,128,128]{3,2,1,0:T(8,128)(2,1)S(1)} %copy-done.8, bf16[10,2,128,128]{3,2,1,0:T(8,128)(2,1)S(1)} %copy-done.10, ...), custom_call_target="tpu_custom_call" | custom-call | tf_op jit(solution)/shard_map/tiles/pallas_call | solution.py:384
  109.8 3.7 %collective-permute-start.13 = (bf16[5,128,256]{2,1,0:T(8,128)(2,1)S(1)}, bf16[5,128,256]{2,1,0:T(8,128)(2,1)S(1)}, u32[]{:S(2)}, u32[]{:S(2)}) collective-permute-start(bf16[5,128,256]{2,1,0:T(8,128)(2,1)S(1)} %get-tuple-element.68), channel_id=1, source_target_pairs={{0,1},{1,2},{2,3},{3,4},{4,5},{5,6},{6,7},{7,8},{8,9},{9,10},{10,1... | collective-permute-start | bytes 983048 | tf_op jit(solution)/shard_map/ppermute | solution.py:451
  113.4 5.2 %collective-permute-start.14 = (bf16[3,128,256]{2,1,0:T(8,128)(2,1)S(1)}, bf16[3,128,256]{2,1,0:T(8,128)(2,1)S(1)}, u32[]{:S(2)}, u32[]{:S(2)}) collective-permute-start(bf16[3,128,256]{2,1,0:T(8,128)(2,1)S(1)} %get-tuple-element.69), channel_id=1, source_target_pairs={{0,2},{1,3},{2,4},{3,5},{4,6},{5,7},{6,8},{7,9},{8,10},{9,11},{10,... | collective-permute-start | bytes 589832 | tf_op jit(solution)/shard_map/ppermute | solution.py:451
  118.7 8.5 %collective-permute-done.14.far0 = bf16[3,128,256]{2,1,0:T(8,128)(2,1)S(1)} collective-permute-done((bf16[3,128,256]{2,1,0:T(8,128)(2,1)S(1)}, bf16[3,128,256]{2,1,0:T(8,128)(2,1)S(1)}, u32[]{:S(2)}, u32[]{:S(2)}) %collective-permute-start.14) | collective-permute-done | bytes 196640 | tf_op jit(solution)/shard_map/ppermute | solution.py:451
  127.3 15.0 %collective-permute-done.10.second = bf16[20,2,128,128]{3,2,1,0:T(8,128)(2,1)} collective-permute-done((bf16[20,2,128,128]{3,2,1,0:T(8,128)(2,1)}, bf16[20,2,128,128]{3,2,1,0:T(8,128)(2,1)}, u32[]{:S(2)}, u32[]{:S(2)}) %collective-permute-start.10) | collective-permute-done | bytes 1310752 | tf_op jit(solution)/shard_map/ppermute | solution.py:451
  143.1 2.5 %collect.1.held = bf16[80,2,128,128]{3,2,1,0:T(8,128)(2,1)S(1)} custom-call(s32[2]{0:T(128)S(1)} %copy-done.23, bf16[10,2,4,2,2,128,128]{6,5,4,3,2,1,0:T(8,128)(2,1)} %bitcast.55, bf16[10,4,2,128,128]{4,3,2,1,0:T(8,128)(2,1)S(1)} %copy-done.1, bf16[20,2,128,128]{3,2,1,0:T(8,128)(2,1)} %collective-permute-done.7.first, ...), custom_call_target="tpu_custom_call" | custom-call | tf_op jit(solution)/shard_map/collect/pallas_call | solution.py:270
  146.8 2.9 %side.3 = (bf16[5,5,256,128]{3,2,1,0:T(8,128)(2,1)S(1)}, bf16[5,128,256]{2,1,0:T(8,128)(2,1)S(1)}) custom-call(s32[45]{0:T(128)S(1)} %get-tuple-element.73.table, bf16[80,2,128,128]{3,2,1,0:T(8,128)(2,1)S(1)} %collect.1.held, bf16[13,256,256]{2,1,0:T(8,128)(2,1)S(1)} %get-tuple-element.77.stack, bf16[5,256,256]{2,1,0:T(8,128)(2,1)S(1)} %get-tuple-element.78.back), custom_call_target="tpu_custom_call" | custom-call | flops 1006632960 | bytes 10485760 | tf_op jit(solution)/shard_map/side/pallas_call | solution.py:211
  149.7 3.4 %collective-permute-start.15 = (bf16[5,128,256]{2,1,0:T(8,128)(2,1)S(1)}, bf16[5,128,256]{2,1,0:T(8,128)(2,1)S(1)}, u32[]{:S(2)}, u32[]{:S(2)}) collective-permute-start(bf16[5,128,256]{2,1,0:T(8,128)(2,1)S(1)} %get-tuple-element.83), channel_id=1, source_target_pairs={{0,1},{1,2},{2,3},{3,4},{4,5},{5,6},{6,7},{7,8},{8,9},{9,10},{10,1... | collective-permute-start | bytes 983048 | tf_op jit(solution)/shard_map/ppermute | solution.py:451
  153.2 4.6 %collective-permute-start.16 = (bf16[3,128,256]{2,1,0:T(8,128)(2,1)S(1)}, bf16[3,128,256]{2,1,0:T(8,128)(2,1)S(1)}, u32[]{:S(2)}, u32[]{:S(2)}) collective-permute-start(bf16[3,128,256]{2,1,0:T(8,128)(2,1)S(1)} %get-tuple-element.84), channel_id=1, source_target_pairs={{0,2},{1,3},{2,4},{3,5},{4,6},{5,7},{6,8},{7,9},{8,10},{9,11},{10,... | collective-permute-start | bytes 589832 | tf_op jit(solution)/shard_map/ppermute | solution.py:451
  157.8 3.4 %nearby.1.own1 = f32[5,128,256]{2,1,0:T(8,128)S(1)} custom-call(s32[45]{0:T(128)S(1)} %get-tuple-element.73.table, bf16[80,2,128,128]{3,2,1,0:T(8,128)(2,1)S(1)} %collect.1.held, bf16[13,256,256]{2,1,0:T(8,128)(2,1)S(1)} %get-tuple-element.77.stack, bf16[5,256,256]{2,1,0:T(8,128)(2,1)S(1)} %get-tuple-element.78.back, ...), custom_call_target="tpu_custom_call" | custom-call | flops 1006632960 | bytes 10485760 | tf_op jit(solution)/shard_map/nearby/pallas_call | solution.py:229
  161.2 6.1 %collective-permute-done.16.far1 = bf16[3,128,256]{2,1,0:T(8,128)(2,1)S(1)} collective-permute-done((bf16[3,128,256]{2,1,0:T(8,128)(2,1)S(1)}, bf16[3,128,256]{2,1,0:T(8,128)(2,1)S(1)}, u32[]{:S(2)}, u32[]{:S(2)}) %collective-permute-start.16) | collective-permute-done | bytes 196640 | tf_op jit(solution)/shard_map/ppermute | solution.py:451
  168.2 14.7 %all_to_all.10 = bf16[8,2,5,16,256]{4,3,2,1,0:T(8,128)(2,1)S(1)} all-to-all(bf16[8,2,5,16,256]{4,3,2,1,0:T(8,128)(2,1)S(1)} %final.1), channel_id=1, replica_groups=mesh['prow'=8,'pcol'=16] {'prow'}, dimensions={0} | all-to-all | bytes 1310720 | tf_op jit(solution)/shard_map/all_to_all | solution.py:523
  183.9 1.7 reshape.392
  (94 shorter events, 28.7 us)
Async XLA Ops:
  7.5 40.9 %collective-permute-start = (bf16[10,2,128,128]{3,2,1,0:T(8,128)(2,1)}, bf16[10,2,128,128]{3,2,1,0:T(8,128)(2,1)S(1)}, u32[]{:S(2)}, u32[]{:S(2)}) collective-permute-start(bf16[10,2,128,128]{3,2,1,0:T(8,128)(2,1)} %get-tuple-element.46), channel_id=1, source_target_pairs={{0,32},{16,48},{32,64},{48,80},{64,96},{80,112},{96,0},{112,16},{1... | collective-permute-start | bytes 1966088 | tf_op jit(solution)/shard_map/ppermute | solution.py:451
  9.1 40.2 %collective-permute-start.1 = (bf16[10,2,128,128]{3,2,1,0:T(8,128)(2,1)}, bf16[10,2,128,128]{3,2,1,0:T(8,128)(2,1)S(1)}, u32[]{:S(2)}, u32[]{:S(2)}) collective-permute-start(bf16[10,2,128,128]{3,2,1,0:T(8,128)(2,1)} %get-tuple-element.47), channel_id=1, source_target_pairs={{0,96},{16,112},{32,0},{48,16},{64,32},{80,48},{96,64},{112,80},{1... | collective-permute-start | bytes 1966088 | tf_op jit(solution)/shard_map/ppermute | solution.py:451
  13.3 36.9 %collective-permute-start.2 = (bf16[10,2,128,128]{3,2,1,0:T(8,128)(2,1)}, bf16[10,2,128,128]{3,2,1,0:T(8,128)(2,1)S(1)}, u32[]{:S(2)}, u32[]{:S(2)}) collective-permute-start(bf16[10,2,128,128]{3,2,1,0:T(8,128)(2,1)} %get-tuple-element.90), channel_id=1, source_target_pairs={{0,48},{16,32},{32,80},{48,64},{64,112},{80,96},{96,16},{112,0},{1... | collective-permute-start | bytes 1966088 | tf_op jit(solution)/shard_map/ppermute | solution.py:451
  13.3 37.7 %collective-permute-start.3 = (bf16[10,2,128,128]{3,2,1,0:T(8,128)(2,1)}, bf16[10,2,128,128]{3,2,1,0:T(8,128)(2,1)S(1)}, u32[]{:S(2)}, u32[]{:S(2)}) collective-permute-start(bf16[10,2,128,128]{3,2,1,0:T(8,128)(2,1)} %get-tuple-element.89), channel_id=1, source_target_pairs={{0,112},{16,96},{32,16},{48,0},{64,48},{80,32},{96,80},{112,64},{1... | collective-permute-start | bytes 1966088 | tf_op jit(solution)/shard_map/ppermute | solution.py:451
  16.2 32.2 %all-to-all-start = ((bf16[8,11,16,256]{3,2,1,0:T(8,128)(2,1)}), bf16[8,11,16,256]{3,2,1,0:T(8,128)(2,1)S(1)}, u32[]{:S(2)}, u32[]{:S(2)}) async-start(bf16[8,11,16,256]{3,2,1,0:T(8,128)(2,1)} %pad_maximum_fusion), calls=%async_computation | async-start | bytes 1441792 | tf_op jit(solution)/shard_map/all_to_all | solution.py:481
  48.4 1.7 copy-start.24
  51.8 10.0 %collective-permute-start.4 = (bf16[10,4,2,128,128]{4,3,2,1,0:T(8,128)(2,1)}, bf16[10,4,2,128,128]{4,3,2,1,0:T(8,128)(2,1)S(1)}, u32[]{:S(2)}, u32[]{:S(2)}) collective-permute-start(bf16[10,4,2,128,128]{4,3,2,1,0:T(8,128)(2,1)} %swap.1), channel_id=1, source_target_pairs={{0,16},{16,0},{32,48},{48,32},{64,80},{80,64},{96,112},{112,96},{1... | collective-permute-start | bytes 7864328 | tf_op jit(solution)/shard_map/ppermute | solution.py:451
  53.4 5.5 %copy-start.25 = (bf16[10,2,128,128]{3,2,1,0:T(8,128)(2,1)S(1)}, bf16[10,2,128,128]{3,2,1,0:T(8,128)(2,1)}, u32[]{:S(2)}) copy-start(bf16[10,2,128,128]{3,2,1,0:T(8,128)(2,1)} %get-tuple-element.56) | copy-start | bytes 1966084
  53.4 16.0 %collective-permute-start.11 = (bf16[10,2,128,128]{3,2,1,0:T(8,128)(2,1)}, bf16[10,2,128,128]{3,2,1,0:T(8,128)(2,1)S(1)}, u32[]{:S(2)}, u32[]{:S(2)}) collective-permute-start(bf16[10,2,128,128]{3,2,1,0:T(8,128)(2,1)} %get-tuple-element.62), channel_id=1, source_target_pairs={{0,16},{16,0},{32,48},{48,32},{64,80},{80,64},{96,112},{112,96},{1... | collective-permute-start | bytes 1966088 | tf_op jit(solution)/shard_map/ppermute | solution.py:451
  54.0 22.9 %collective-permute-start.9 = (bf16[10,2,128,128]{3,2,1,0:T(8,128)(2,1)}, bf16[10,2,128,128]{3,2,1,0:T(8,128)(2,1)S(1)}, u32[]{:S(2)}, u32[]{:S(2)}) collective-permute-start(bf16[10,2,128,128]{3,2,1,0:T(8,128)(2,1)} %get-tuple-element.59), channel_id=1, source_target_pairs={{0,80},{16,64},{32,112},{48,96},{64,16},{80,0},{96,48},{112,32},{1... | collective-permute-start | bytes 1966088 | tf_op jit(solution)/shard_map/ppermute | solution.py:451
  54.7 14.7 %copy-start.2 = (bf16[2,5,128,256]{3,2,1,0:T(8,128)(2,1)}, bf16[2,5,128,256]{3,2,1,0:T(8,128)(2,1)S(1)}, u32[]{:S(2)}) copy-start(bf16[2,5,128,256]{3,2,1,0:T(8,128)(2,1)S(1)} %multiply_convert_fusion.own) | copy-start | bytes 1966084
  54.7 27.2 %collective-permute-start.5 = (bf16[2,5,128,256]{3,2,1,0:T(8,128)(2,1)S(1)}, bf16[2,5,128,256]{3,2,1,0:T(8,128)(2,1)S(1)}, u32[]{:S(2)}, u32[]{:S(2)}) collective-permute-start(bf16[2,5,128,256]{3,2,1,0:T(8,128)(2,1)S(1)} %multiply_convert_fusion.own), channel_id=1, source_target_pairs={{1,0},{2,1},{3,2},{4,3},{5,4},{6,5},{7,6},{8,7},{9,8},{10,9},{11,1... | collective-permute-start | bytes 1966088 | tf_op jit(solution)/shard_map/ppermute | solution.py:451
  58.9 28.1 %collective-permute-start.6 = (bf16[10,2,128,128]{3,2,1,0:T(8,128)(2,1)S(1)}, bf16[10,2,128,128]{3,2,1,0:T(8,128)(2,1)S(1)}, u32[]{:S(2)}, u32[]{:S(2)}) collective-permute-start(bf16[10,2,128,128]{3,2,1,0:T(8,128)(2,1)S(1)} %copy-done.25), channel_id=1, source_target_pairs={{0,64},{16,80},{32,96},{48,112},{64,0},{80,16},{96,32},{112,48},{1... | collective-permute-start | bytes 1966088 | tf_op jit(solution)/shard_map/ppermute | solution.py:451
  61.8 2.7 %copy-start = (bf16[10,4,2,128,128]{4,3,2,1,0:T(8,128)(2,1)}, bf16[10,4,2,128,128]{4,3,2,1,0:T(8,128)(2,1)S(1)}, u32[]{:S(2)}) copy-start(bf16[10,4,2,128,128]{4,3,2,1,0:T(8,128)(2,1)S(1)} %collective-permute-done.4.pair) | copy-start | bytes 7864324
  61.8 14.3 %collective-permute-start.8 = (bf16[2,3,128,256]{3,2,1,0:T(8,128)(2,1)S(1)}, bf16[2,3,128,256]{3,2,1,0:T(8,128)(2,1)S(1)}, u32[]{:S(2)}, u32[]{:S(2)}) collective-permute-start(bf16[2,3,128,256]{3,2,1,0:T(8,128)(2,1)S(1)} %slice.14), channel_id=1, source_target_pairs={{2,0},{3,1},{4,2},{5,3},{6,4},{7,5},{8,6},{9,7},{10,8},{11,9},{12,... | collective-permute-start | bytes 1179656 | tf_op jit(solution)/shard_map/ppermute | solution.py:451
  70.2 21.1 %copy-start.3 = (bf16[2,5,128,256]{3,2,1,0:T(8,128)(2,1)S(1)}, bf16[2,5,128,256]{3,2,1,0:T(8,128)(2,1)}, u32[]{:S(2)}) copy-start(bf16[2,5,128,256]{3,2,1,0:T(8,128)(2,1)} %copy-done.2) | copy-start | bytes 1966084
  70.2 57.0 %collective-permute-start.12 = (bf16[20,2,128,128]{3,2,1,0:T(8,128)(2,1)}, bf16[20,2,128,128]{3,2,1,0:T(8,128)(2,1)S(1)}, u32[]{:S(2)}, u32[]{:S(2)}) collective-permute-start(bf16[20,2,128,128]{3,2,1,0:T(8,128)(2,1)} %get-tuple-element.63), channel_id=1, source_target_pairs={{0,64},{16,80},{32,96},{48,112},{64,0},{80,16},{96,32},{112,48},{1... | collective-permute-start | bytes 3932168 | tf_op jit(solution)/shard_map/ppermute | solution.py:451
  77.7 64.5 %collective-permute-start.10 = (bf16[20,2,128,128]{3,2,1,0:T(8,128)(2,1)}, bf16[20,2,128,128]{3,2,1,0:T(8,128)(2,1)}, u32[]{:S(2)}, u32[]{:S(2)}) collective-permute-start(bf16[20,2,128,128]{3,2,1,0:T(8,128)(2,1)} %get-tuple-element.60), channel_id=1, source_target_pairs={{0,96},{16,112},{32,0},{48,16},{64,32},{80,48},{96,64},{112,80},{1... | collective-permute-start | bytes 3932168 | tf_op jit(solution)/shard_map/ppermute | solution.py:451
  87.9 55.2 %collective-permute-start.7 = (bf16[20,2,128,128]{3,2,1,0:T(8,128)(2,1)}, bf16[20,2,128,128]{3,2,1,0:T(8,128)(2,1)}, u32[]{:S(2)}, u32[]{:S(2)}) collective-permute-start(bf16[20,2,128,128]{3,2,1,0:T(8,128)(2,1)} %get-tuple-element.57), channel_id=1, source_target_pairs={{0,32},{16,48},{32,64},{48,80},{64,96},{80,112},{96,0},{112,16},{1... | collective-permute-start | bytes 3932168 | tf_op jit(solution)/shard_map/ppermute | solution.py:451
  89.3 6.1 %copy-start.4 = (bf16[10,2,128,128]{3,2,1,0:T(8,128)(2,1)S(1)}, bf16[10,2,128,128]{3,2,1,0:T(8,128)(2,1)}, u32[]{:S(2)}) copy-start(bf16[10,2,128,128]{3,2,1,0:T(8,128)(2,1)} %get-tuple-element.85.refs_0_) | copy-start | bytes 1966084
  91.3 1.1 copy-start.6
  93.4 2.0 %copy-start.8 = (bf16[10,2,128,128]{3,2,1,0:T(8,128)(2,1)S(1)}, bf16[10,2,128,128]{3,2,1,0:T(8,128)(2,1)}, u32[]{:S(2)}) copy-start(bf16[10,2,128,128]{3,2,1,0:T(8,128)(2,1)} %copy-done.7) | copy-start | bytes 1966084
  93.4 2.0 %copy-start.10 = (bf16[10,2,128,128]{3,2,1,0:T(8,128)(2,1)S(1)}, bf16[10,2,128,128]{3,2,1,0:T(8,128)(2,1)}, u32[]{:S(2)}) copy-start(bf16[10,2,128,128]{3,2,1,0:T(8,128)(2,1)} %copy-done.9) | copy-start | bytes 1966084
  95.4 1.1 copy-start.12
  96.5 1.1 copy-start.14
  97.6 1.1 copy-start.16
  100.9 42.2 %copy-start.1 = (bf16[10,4,2,128,128]{4,3,2,1,0:T(8,128)(2,1)S(1)}, bf16[10,4,2,128,128]{4,3,2,1,0:T(8,128)(2,1)}, u32[]{:S(2)}) copy-start(bf16[10,4,2,128,128]{4,3,2,1,0:T(8,128)(2,1)} %copy-done) | copy-start | bytes 7864324
  100.9 42.2 %copy-start.23 = (s32[2]{0:T(128)S(1)}, s32[2]{0:T(128)}, u32[]{:S(2)}) copy-start(s32[2]{0:T(128)} %pad_add_fusion.place) | copy-start | bytes 28
  109.8 17.5 %collective-permute-start.13 = (bf16[5,128,256]{2,1,0:T(8,128)(2,1)S(1)}, bf16[5,128,256]{2,1,0:T(8,128)(2,1)S(1)}, u32[]{:S(2)}, u32[]{:S(2)}) collective-permute-start(bf16[5,128,256]{2,1,0:T(8,128)(2,1)S(1)} %get-tuple-element.68), channel_id=1, source_target_pairs={{0,1},{1,2},{2,3},{3,4},{4,5},{5,6},{6,7},{7,8},{8,9},{9,10},{10,1... | collective-permute-start | bytes 983048 | tf_op jit(solution)/shard_map/ppermute | solution.py:451
  113.4 13.8 %collective-permute-start.14 = (bf16[3,128,256]{2,1,0:T(8,128)(2,1)S(1)}, bf16[3,128,256]{2,1,0:T(8,128)(2,1)S(1)}, u32[]{:S(2)}, u32[]{:S(2)}) collective-permute-start(bf16[3,128,256]{2,1,0:T(8,128)(2,1)S(1)} %get-tuple-element.69), channel_id=1, source_target_pairs={{0,2},{1,3},{2,4},{3,5},{4,6},{5,7},{6,8},{7,9},{8,10},{9,11},{10,... | collective-permute-start | bytes 589832 | tf_op jit(solution)/shard_map/ppermute | solution.py:451
  149.7 17.9 %collective-permute-start.15 = (bf16[5,128,256]{2,1,0:T(8,128)(2,1)S(1)}, bf16[5,128,256]{2,1,0:T(8,128)(2,1)S(1)}, u32[]{:S(2)}, u32[]{:S(2)}) collective-permute-start(bf16[5,128,256]{2,1,0:T(8,128)(2,1)S(1)} %get-tuple-element.83), channel_id=1, source_target_pairs={{0,1},{1,2},{2,3},{3,4},{4,5},{5,6},{6,7},{7,8},{8,9},{9,10},{10,1... | collective-permute-start | bytes 983048 | tf_op jit(solution)/shard_map/ppermute | solution.py:451
  153.2 14.2 %collective-permute-start.16 = (bf16[3,128,256]{2,1,0:T(8,128)(2,1)S(1)}, bf16[3,128,256]{2,1,0:T(8,128)(2,1)S(1)}, u32[]{:S(2)}, u32[]{:S(2)}) collective-permute-start(bf16[3,128,256]{2,1,0:T(8,128)(2,1)S(1)} %get-tuple-element.84), channel_id=1, source_target_pairs={{0,2},{1,3},{2,4},{3,5},{4,6},{5,7},{6,8},{7,9},{8,10},{9,11},{10,... | collective-permute-start | bytes 589832 | tf_op jit(solution)/shard_map/ppermute | solution.py:451
  (12 other events, 10.7 us)

commit v3 on v2

--- a/solution.py
+++ b/solution.py
@@ -218,7 +218,7 @@
         out_specs=(VMEM, VMEM),
         scratch_shapes=[pltpu.VMEM((count, width, depth), jnp.float32)],
         compiler_params=PARAMS,
-        cost_estimate=cost(4 * count, width, depth),
+        cost_estimate=cost(0, width, depth),
         name="side",
     )(table, held, stack, back)
 
@@ -233,7 +233,7 @@
         out_specs=VMEM,
         scratch_shapes=[pltpu.VMEM((blocks, blocks, double, width), jnp.bfloat16)],
         compiler_params=PARAMS,
-        cost_estimate=cost(20, width, depth),
+        cost_estimate=cost(0, width, depth),
         name="nearby",
     )(table, held, stack, back, close, distant)
 
@@ -466,6 +466,11 @@
     routes = [route_across(*hop) for hop in HOPS]
     obs = observed[0, 0]
 
+    def cut(data, j, k):
+        return lax.dynamic_index_in_dim(data, 8 * j + targets[k], 1, keepdims=False)
+
+    early = [cut(obs, 0, k) for k in range(2)]
+    early, spectra, obs = lax.optimization_barrier((early, spectra, obs))
     meta = jnp.concatenate([tile_count.reshape(1), (tile_list - base).reshape(-1)])
     count = meta.shape[0]
     meta = jnp.pad(meta.astype(jnp.bfloat16).reshape(1, count), ((0, share - 1), (0, depth - count)))
@@ -473,11 +478,6 @@
     load = load.reshape(8, 2 * blocks, share, depth)
     load = jnp.concatenate([load, jnp.broadcast_to(meta, (8, 1) + meta.shape)], axis=1)
 
-    def cut(data, j, k):
-        return lax.dynamic_index_in_dim(data, 8 * j + targets[k], 1, keepdims=False)
-
-    early = [cut(obs, 0, k) for k in range(2)]
-    early, load, obs = lax.optimization_barrier((early, load, obs))
     load = lax.all_to_all(load, "prow", split_axis=0, concat_axis=0, tiled=True)
     parts0 = early + [cut(obs, 0, k) for k in range(2, 4)]
     _, obs = lax.optimization_barrier((parts0[2:], obs))

time: 186 us -> 182 us (0.978)
  waiting for transfers between devices: 63.4 us -> 58.8 us
    all_to_all x1, waiting for transfers between devices: 20.7 us -> 16.2 us  [local(): load = lax.all_to_all(load, 'prow', split_axis=0, concat_axis=0, tiled=True)]
    unnamed x52 -> x56, local copies, waits for them, and re-layouts: 15.1 us -> 15.1 us
  transfers between devices with their start and end apart: 18 -> 18, of which waited for: 9 -> 9; matrix products, arithmetic and copies ran while one was open for 6% -> 8% of each run, Pallas kernels for 12% -> 13%
where the time goes in v3:
time: 182 us; the launch traced here: 181 us
  waiting for transfers between devices  58.8 us (32%)
  starting transfers between devices  41.3 us (23%)
  local copies, waits for them, and re-layouts  32.1 us (18%)
  Pallas kernels  30.2 us (17%)
  blocking collectives  14.7 us (8%)
  other arithmetic  2.33 us (1%)
    ppermute x17, waiting for transfers between devices, send(): return lax.ppermute(values, *route)  42.6 us
    ppermute x17, starting transfers between devices, send(): return lax.ppermute(values, *route)  37.7 us
    all_to_all x1, waiting for transfers between devices, local(): load = lax.all_to_all(load, 'prow', split_axis=0, concat_axis=0, tiled=True)  16.2 us
    unnamed x56, local copies, waits for them, and re-layouts  15.1 us
    all_to_all x1, blocking collectives, local(): grad = lax.all_to_all(grad, 'prow', split_axis=0, concat_axis=0, tiled=True)  14.7 us
    pallas_call x1, Pallas kernels, tile_call(): pl.pallas_call(tile_kernel, out_shape=(jax.ShapeDtypeStruct((blocks, widt...  8.88 us
    squeeze x2, local copies, waits for them, and re-layouts, cut(): return lax.dynamic_index_in_dim(data, 8 * j + targets[k], 1, keepdims=False)  5.08 us
    pallas_call x1, Pallas kernels, pack_call(): pl.pallas_call(functools.partial(pack_kernel, j), out_shape=(out, out, ou...  4.78 us
  transfers between devices with their start and end apart: 18, of which 9 were waited for; matrix products, arithmetic and copies ran while one was open for 8% of the time, Pallas kernels for 13%

profile of v3, /device:TPU:32, one launch (start us, length us, event | category | flops | bytes accessed | tf_op | source)
XLA Modules:
  0.0 180.6 jit_solution(10716213547240437479)
XLA Ops:
  0.0 2.5 %dynamic-slice_bitcast_fusion.6 = (bf16[10,2,128,128]{3,2,1,0:T(8,128)(2,1)}, bf16[10,2,128,128]{3,2,1,0:T(8,128)(2,1)}) fusion(bf16[1,1,10,16,2,128,128]{6,5,4,3,2,1,0:T(8,128)(2,1)} %param.7, s32[]{:T(128)S(6)} %select_n.93, s32[]{:T(128)S(6)} %select_n.91), kind=kLoop, calls=%fused_computation.11 | loop fusion | bytes 2621448 | tf_op jit(solution)/shard_map/jit(dynamic_index_in_dim)/squeeze | solution.py:470
  2.5 1.6 collective-permute-start
  4.1 1.7 collective-permute-start.1
  5.7 2.6 %dynamic-slice_bitcast_fusion.4 = (bf16[10,2,128,128]{3,2,1,0:T(8,128)(2,1)}, bf16[10,2,128,128]{3,2,1,0:T(8,128)(2,1)}) fusion(bf16[10,16,2,128,128]{4,3,2,1,0:T(8,128)(2,1)} %bitcast.51, s32[]{:T(128)S(6)} %select_n.95, s32[]{:T(128)S(6)} %select_n.94), kind=kLoop, calls=%fused_computation.9 | loop fusion | bytes 2621448 | tf_op jit(solution)/shard_map/jit(dynamic_index_in_dim)/squeeze | solution.py:470
  8.3 3.0 %collective-permute-start.3 = (bf16[10,2,128,128]{3,2,1,0:T(8,128)(2,1)}, bf16[10,2,128,128]{3,2,1,0:T(8,128)(2,1)S(1)}, u32[]{:S(2)}, u32[]{:S(2)}) collective-permute-start(bf16[10,2,128,128]{3,2,1,0:T(8,128)(2,1)} %get-tuple-element.89), channel_id=1, source_target_pairs={{0,112},{16,96},{32,16},{48,0},{64,48},{80,32},{96,80},{112,64},{1... | collective-permute-start | bytes 1966088 | tf_op jit(solution)/shard_map/ppermute | solution.py:451
  15.7 3.5 %all-to-all-start = ((bf16[8,11,16,256]{3,2,1,0:T(8,128)(2,1)}), bf16[8,11,16,256]{3,2,1,0:T(8,128)(2,1)S(1)}, u32[]{:S(2)}, u32[]{:S(2)}) async-start(bf16[8,11,16,256]{3,2,1,0:T(8,128)(2,1)} %pad_maximum_fusion), calls=%async_computation | async-start | bytes 1441792 | tf_op jit(solution)/shard_map/all_to_all | solution.py:481
  19.9 3.9 %swap.1 = bf16[10,4,2,128,128]{4,3,2,1,0:T(8,128)(2,1)} custom-call(s32[2]{0:T(128)} %pad_add_fusion.place, bf16[10,2,4,2,2,128,128]{6,5,4,3,2,1,0:T(8,128)(2,1)} %bitcast.52), custom_call_target="tpu_custom_call" | custom-call | tf_op jit(solution)/shard_map/swap/pallas_call | solution.py:289
  23.9 3.3 %dynamic-slice_bitcast_fusion = (bf16[10,2,128,128]{3,2,1,0:T(8,128)(2,1)}, bf16[10,2,128,128]{3,2,1,0:T(8,128)(2,1)}, bf16[10,2,128,128]{3,2,1,0:T(8,128)(2,1)}, bf16[10,2,128,128]{3,2,1,0:T(8,128)(2,1)}) fusion(bf16[10,16,2,128,128]{4,3,2,1,0:T(8,128)(2,1)} %bitcast.53, s32[]{:T(128)S(6)} %select_n.105, s32[]{:T(128)S(6)} %select_n.100, s32[]{:T(128)S(6)} %select_n.99, ...), kind=kLoop, calls=%fused_computation.5 | loop fusion | bytes 5242896 | tf_op jit(solution)/shard_map/jit(dynamic_index_in_dim)/squeeze | solution.py:511
  27.2 16.2 %all-to-all-done = bf16[8,11,16,256]{3,2,1,0:T(8,128)(2,1)S(1)} async-done(((bf16[8,11,16,256]{3,2,1,0:T(8,128)(2,1)}), bf16[8,11,16,256]{3,2,1,0:T(8,128)(2,1)S(1)}, u32[]{:S(2)}, u32[]{:S(2)}) %all-to-all-start) | async-done | bytes 720928 | tf_op jit(solution)/shard_map/all_to_all | solution.py:481
  49.7 4.2 %collective-permute-start.5 = (bf16[2,5,128,256]{3,2,1,0:T(8,128)(2,1)S(1)}, bf16[2,5,128,256]{3,2,1,0:T(8,128)(2,1)S(1)}, u32[]{:S(2)}, u32[]{:S(2)}) collective-permute-start(bf16[2,5,128,256]{3,2,1,0:T(8,128)(2,1)S(1)} %multiply_convert_fusion.own), channel_id=1, source_target_pairs={{1,0},{2,1},{3,2},{4,3},{5,4},{6,5},{7,6},{8,7},{9,8},{10,9},{11,1... | collective-permute-start | bytes 1966088 | tf_op jit(solution)/shard_map/ppermute | solution.py:451
  53.9 2.9 %collective-permute-start.6 = (bf16[10,2,128,128]{3,2,1,0:T(8,128)(2,1)S(1)}, bf16[10,2,128,128]{3,2,1,0:T(8,128)(2,1)S(1)}, u32[]{:S(2)}, u32[]{:S(2)}) collective-permute-start(bf16[10,2,128,128]{3,2,1,0:T(8,128)(2,1)S(1)} %copy-done.25), channel_id=1, source_target_pairs={{0,64},{16,80},{32,96},{48,112},{64,0},{80,16},{96,32},{112,48},{1... | collective-permute-start | bytes 1966088 | tf_op jit(solution)/shard_map/ppermute | solution.py:451
  56.8 2.7 %collective-permute-start.8 = (bf16[2,3,128,256]{3,2,1,0:T(8,128)(2,1)S(1)}, bf16[2,3,128,256]{3,2,1,0:T(8,128)(2,1)S(1)}, u32[]{:S(2)}, u32[]{:S(2)}) collective-permute-start(bf16[2,3,128,256]{3,2,1,0:T(8,128)(2,1)S(1)} %slice.14), channel_id=1, source_target_pairs={{2,0},{3,1},{4,2},{5,3},{6,4},{7,5},{8,6},{9,7},{10,8},{11,9},{12,... | collective-permute-start | bytes 1179656 | tf_op jit(solution)/shard_map/ppermute | solution.py:451
  59.6 4.8 %pack.1 = (bf16[20,2,128,128]{3,2,1,0:T(8,128)(2,1)}, bf16[20,2,128,128]{3,2,1,0:T(8,128)(2,1)}, bf16[20,2,128,128]{3,2,1,0:T(8,128)(2,1)}) custom-call(s32[2]{0:T(128)} %pad_add_fusion.place, bf16[10,2,4,2,2,128,128]{6,5,4,3,2,1,0:T(8,128)(2,1)} %bitcast.54, bf16[10,4,2,128,128]{4,3,2,1,0:T(8,128)(2,1)} %copy-done), custom_call_target="tpu_custom_call" | custom-call | tf_op jit(solution)/shard_map/pack/pallas_call | solution.py:317
  66.0 5.1 %collective-permute-done.8.far = bf16[2,3,128,256]{3,2,1,0:T(8,128)(2,1)S(1)} collective-permute-done((bf16[2,3,128,256]{3,2,1,0:T(8,128)(2,1)S(1)}, bf16[2,3,128,256]{3,2,1,0:T(8,128)(2,1)S(1)}, u32[]{:S(2)}, u32[]{:S(2)}) %collective-permute-start.8) | collective-permute-done | bytes 393248 | tf_op jit(solution)/shard_map/ppermute | solution.py:451
  72.7 1.8 collective-permute-start.10
  74.5 2.4 %collective-permute-done.5.near = bf16[2,5,128,256]{3,2,1,0:T(8,128)(2,1)S(1)} collective-permute-done((bf16[2,5,128,256]{3,2,1,0:T(8,128)(2,1)S(1)}, bf16[2,5,128,256]{3,2,1,0:T(8,128)(2,1)S(1)}, u32[]{:S(2)}, u32[]{:S(2)}) %collective-permute-start.5) | collective-permute-done | bytes 655392 | tf_op jit(solution)/shard_map/ppermute | solution.py:451
  77.8 4.3 %collective-permute-done.6.refs_6_ = bf16[10,2,128,128]{3,2,1,0:T(8,128)(2,1)S(1)} collective-permute-done((bf16[10,2,128,128]{3,2,1,0:T(8,128)(2,1)S(1)}, bf16[10,2,128,128]{3,2,1,0:T(8,128)(2,1)S(1)}, u32[]{:S(2)}, u32[]{:S(2)}) %collective-permute-start.6) | collective-permute-done | bytes 655392 | tf_op jit(solution)/shard_map/ppermute | solution.py:451
  84.3 1.4 copy.18
  88.4 2.0 %setup.1 = (s32[45]{0:T(128)S(1)}, s32[45]{0:T(128)S(1)}, bf16[13,256,256]{2,1,0:T(8,128)(2,1)S(1)}, bf16[13,256,256]{2,1,0:T(8,128)(2,1)S(1)}, bf16[5,256,256]{...) custom-call(s32[8,21]{1,0:T(8,128)S(1)} %gather_fusion, bf16[2,5,128,256]{3,2,1,0:T(8,128)(2,1)S(1)} %copy-done.3, ...), custom_call_target="tpu_custom_call" | custom-call | tf_op jit(solution)/shard_map/setup/pallas_call | solution.py:64
  95.9 8.9 %tiles.1 = (f32[5,128,256]{2,1,0:T(8,128)S(1)}, bf16[5,128,256]{2,1,0:T(8,128)(2,1)S(1)}, bf16[3,128,256]{2,1,0:T(8,128)(2,1)S(1)}) custom-call(s32[45]{0:T(128)S(1)} %get-tuple-element.64.table, bf16[10,2,128,128]{3,2,1,0:T(8,128)(2,1)S(1)} %copy-done.4, bf16[10,2,128,128]{3,2,1,0:T(8,128)(2,1)S(1)} %copy-done.8, bf16[10,2,128,128]{3,2,1,0:T(8,128)(2,1)S(1)} %copy-done.10, ...), custom_call_target="tpu_custom_call" | custom-call | tf_op jit(solution)/shard_map/tiles/pallas_call | solution.py:384
  104.8 3.6 %collective-permute-start.13 = (bf16[5,128,256]{2,1,0:T(8,128)(2,1)S(1)}, bf16[5,128,256]{2,1,0:T(8,128)(2,1)S(1)}, u32[]{:S(2)}, u32[]{:S(2)}) collective-permute-start(bf16[5,128,256]{2,1,0:T(8,128)(2,1)S(1)} %get-tuple-element.68), channel_id=1, source_target_pairs={{0,1},{1,2},{2,3},{3,4},{4,5},{5,6},{6,7},{7,8},{8,9},{9,10},{10,1... | collective-permute-start | bytes 983048 | tf_op jit(solution)/shard_map/ppermute | solution.py:451
  108.4 5.1 %collective-permute-start.14 = (bf16[3,128,256]{2,1,0:T(8,128)(2,1)S(1)}, bf16[3,128,256]{2,1,0:T(8,128)(2,1)S(1)}, u32[]{:S(2)}, u32[]{:S(2)}) collective-permute-start(bf16[3,128,256]{2,1,0:T(8,128)(2,1)S(1)} %get-tuple-element.69), channel_id=1, source_target_pairs={{0,2},{1,3},{2,4},{3,5},{4,6},{5,7},{6,8},{7,9},{8,10},{9,11},{10,... | collective-permute-start | bytes 589832 | tf_op jit(solution)/shard_map/ppermute | solution.py:451
  113.5 8.7 %collective-permute-done.14.far0 = bf16[3,128,256]{2,1,0:T(8,128)(2,1)S(1)} collective-permute-done((bf16[3,128,256]{2,1,0:T(8,128)(2,1)S(1)}, bf16[3,128,256]{2,1,0:T(8,128)(2,1)S(1)}, u32[]{:S(2)}, u32[]{:S(2)}) %collective-permute-start.14) | collective-permute-done | bytes 196640 | tf_op jit(solution)/shard_map/ppermute | solution.py:451
  122.3 15.0 %collective-permute-done.10.second = bf16[20,2,128,128]{3,2,1,0:T(8,128)(2,1)} collective-permute-done((bf16[20,2,128,128]{3,2,1,0:T(8,128)(2,1)}, bf16[20,2,128,128]{3,2,1,0:T(8,128)(2,1)}, u32[]{:S(2)}, u32[]{:S(2)}) %collective-permute-start.10) | collective-permute-done | bytes 1310752 | tf_op jit(solution)/shard_map/ppermute | solution.py:451
  138.1 2.5 %collect.1.held = bf16[80,2,128,128]{3,2,1,0:T(8,128)(2,1)S(1)} custom-call(s32[2]{0:T(128)S(1)} %copy-done.23, bf16[10,2,4,2,2,128,128]{6,5,4,3,2,1,0:T(8,128)(2,1)} %bitcast.55, bf16[10,4,2,128,128]{4,3,2,1,0:T(8,128)(2,1)S(1)} %copy-done.1, bf16[20,2,128,128]{3,2,1,0:T(8,128)(2,1)} %collective-permute-done.7.first, ...), custom_call_target="tpu_custom_call" | custom-call | tf_op jit(solution)/shard_map/collect/pallas_call | solution.py:270
  141.8 2.9 %side.3 = (bf16[5,5,256,128]{3,2,1,0:T(8,128)(2,1)S(1)}, bf16[5,128,256]{2,1,0:T(8,128)(2,1)S(1)}) custom-call(s32[45]{0:T(128)S(1)} %get-tuple-element.73.table, bf16[80,2,128,128]{3,2,1,0:T(8,128)(2,1)S(1)} %collect.1.held, bf16[13,256,256]{2,1,0:T(8,128)(2,1)S(1)} %get-tuple-element.77.stack, bf16[5,256,256]{2,1,0:T(8,128)(2,1)S(1)} %get-tuple-element.78.back), custom_call_target="tpu_custom_call" | custom-call | tf_op jit(solution)/shard_map/side/pallas_call | solution.py:211
  144.8 3.4 %collective-permute-start.15 = (bf16[5,128,256]{2,1,0:T(8,128)(2,1)S(1)}, bf16[5,128,256]{2,1,0:T(8,128)(2,1)S(1)}, u32[]{:S(2)}, u32[]{:S(2)}) collective-permute-start(bf16[5,128,256]{2,1,0:T(8,128)(2,1)S(1)} %get-tuple-element.83), channel_id=1, source_target_pairs={{0,1},{1,2},{2,3},{3,4},{4,5},{5,6},{6,7},{7,8},{8,9},{9,10},{10,1... | collective-permute-start | bytes 983048 | tf_op jit(solution)/shard_map/ppermute | solution.py:451
  148.2 4.8 %collective-permute-start.16 = (bf16[3,128,256]{2,1,0:T(8,128)(2,1)S(1)}, bf16[3,128,256]{2,1,0:T(8,128)(2,1)S(1)}, u32[]{:S(2)}, u32[]{:S(2)}) collective-permute-start(bf16[3,128,256]{2,1,0:T(8,128)(2,1)S(1)} %get-tuple-element.84), channel_id=1, source_target_pairs={{0,2},{1,3},{2,4},{3,5},{4,6},{5,7},{6,8},{7,9},{8,10},{9,11},{10,... | collective-permute-start | bytes 589832 | tf_op jit(solution)/shard_map/ppermute | solution.py:451
  153.0 3.4 %nearby.1.own1 = f32[5,128,256]{2,1,0:T(8,128)S(1)} custom-call(s32[45]{0:T(128)S(1)} %get-tuple-element.73.table, bf16[80,2,128,128]{3,2,1,0:T(8,128)(2,1)S(1)} %collect.1.held, bf16[13,256,256]{2,1,0:T(8,128)(2,1)S(1)} %get-tuple-element.77.stack, bf16[5,256,256]{2,1,0:T(8,128)(2,1)S(1)} %get-tuple-element.78.back, ...), custom_call_target="tpu_custom_call" | custom-call | tf_op jit(solution)/shard_map/nearby/pallas_call | solution.py:229
  156.4 6.0 %collective-permute-done.16.far1 = bf16[3,128,256]{2,1,0:T(8,128)(2,1)S(1)} collective-permute-done((bf16[3,128,256]{2,1,0:T(8,128)(2,1)S(1)}, bf16[3,128,256]{2,1,0:T(8,128)(2,1)S(1)}, u32[]{:S(2)}, u32[]{:S(2)}) %collective-permute-start.16) | collective-permute-done | bytes 196640 | tf_op jit(solution)/shard_map/ppermute | solution.py:451
  163.3 14.7 %all_to_all.10 = bf16[8,2,5,16,256]{4,3,2,1,0:T(8,128)(2,1)S(1)} all-to-all(bf16[8,2,5,16,256]{4,3,2,1,0:T(8,128)(2,1)S(1)} %final.1), channel_id=1, replica_groups=mesh['prow'=8,'pcol'=16] {'prow'}, dimensions={0} | all-to-all | bytes 1310720 | tf_op jit(solution)/shard_map/all_to_all | solution.py:523
  178.9 1.7 reshape.392
  (98 shorter events, 28.9 us)
Async XLA Ops:
  2.5 40.9 %collective-permute-start = (bf16[10,2,128,128]{3,2,1,0:T(8,128)(2,1)}, bf16[10,2,128,128]{3,2,1,0:T(8,128)(2,1)S(1)}, u32[]{:S(2)}, u32[]{:S(2)}) collective-permute-start(bf16[10,2,128,128]{3,2,1,0:T(8,128)(2,1)} %get-tuple-element.46), channel_id=1, source_target_pairs={{0,32},{16,48},{32,64},{48,80},{64,96},{80,112},{96,0},{112,16},{1... | collective-permute-start | bytes 1966088 | tf_op jit(solution)/shard_map/ppermute | solution.py:451
  4.1 40.2 %collective-permute-start.1 = (bf16[10,2,128,128]{3,2,1,0:T(8,128)(2,1)}, bf16[10,2,128,128]{3,2,1,0:T(8,128)(2,1)S(1)}, u32[]{:S(2)}, u32[]{:S(2)}) collective-permute-start(bf16[10,2,128,128]{3,2,1,0:T(8,128)(2,1)} %get-tuple-element.47), channel_id=1, source_target_pairs={{0,96},{16,112},{32,0},{48,16},{64,32},{80,48},{96,64},{112,80},{1... | collective-permute-start | bytes 1966088 | tf_op jit(solution)/shard_map/ppermute | solution.py:451
  5.7 5.5 %copy-start.26 = (bf16[5,16,16,2,128]{4,3,2,1,0:T(2,128)(2,1)S(1)}, bf16[5,16,16,2,128]{4,3,2,1,0:T(2,128)(2,1)}, u32[]{:S(2)}) copy-start(bf16[5,16,16,2,128]{4,3,2,1,0:T(2,128)(2,1)} %param.4) | copy-start | bytes 1966084
  8.3 36.8 %collective-permute-start.2 = (bf16[10,2,128,128]{3,2,1,0:T(8,128)(2,1)}, bf16[10,2,128,128]{3,2,1,0:T(8,128)(2,1)S(1)}, u32[]{:S(2)}, u32[]{:S(2)}) collective-permute-start(bf16[10,2,128,128]{3,2,1,0:T(8,128)(2,1)} %get-tuple-element.90), channel_id=1, source_target_pairs={{0,48},{16,32},{32,80},{48,64},{64,112},{80,96},{96,16},{112,0},{1... | collective-permute-start | bytes 1966088 | tf_op jit(solution)/shard_map/ppermute | solution.py:451
  8.3 5.5 %copy-start.27 = (s32[1,1,10,2]{2,3,1,0:T(2,128)S(1)}, s32[1,1,10,2]{2,3,1,0:T(2,128)}, u32[]{:S(2)}) copy-start(s32[1,1,10,2]{2,3,1,0:T(2,128)} %param.5) | copy-start | bytes 244
  8.3 37.7 %collective-permute-start.3 = (bf16[10,2,128,128]{3,2,1,0:T(8,128)(2,1)}, bf16[10,2,128,128]{3,2,1,0:T(8,128)(2,1)S(1)}, u32[]{:S(2)}, u32[]{:S(2)}) collective-permute-start(bf16[10,2,128,128]{3,2,1,0:T(8,128)(2,1)} %get-tuple-element.89), channel_id=1, source_target_pairs={{0,112},{16,96},{32,16},{48,0},{64,48},{80,32},{96,80},{112,64},{1... | collective-permute-start | bytes 1966088 | tf_op jit(solution)/shard_map/ppermute | solution.py:451
  15.7 27.7 %all-to-all-start = ((bf16[8,11,16,256]{3,2,1,0:T(8,128)(2,1)}), bf16[8,11,16,256]{3,2,1,0:T(8,128)(2,1)S(1)}, u32[]{:S(2)}, u32[]{:S(2)}) async-start(bf16[8,11,16,256]{3,2,1,0:T(8,128)(2,1)} %pad_maximum_fusion), calls=%async_computation | async-start | bytes 1441792 | tf_op jit(solution)/shard_map/all_to_all | solution.py:481
  43.4 1.7 copy-start.24
  46.8 10.0 %collective-permute-start.4 = (bf16[10,4,2,128,128]{4,3,2,1,0:T(8,128)(2,1)}, bf16[10,4,2,128,128]{4,3,2,1,0:T(8,128)(2,1)S(1)}, u32[]{:S(2)}, u32[]{:S(2)}) collective-permute-start(bf16[10,4,2,128,128]{4,3,2,1,0:T(8,128)(2,1)} %swap.1), channel_id=1, source_target_pairs={{0,16},{16,0},{32,48},{48,32},{64,80},{80,64},{96,112},{112,96},{1... | collective-permute-start | bytes 7864328 | tf_op jit(solution)/shard_map/ppermute | solution.py:451
  48.4 5.5 %copy-start.25 = (bf16[10,2,128,128]{3,2,1,0:T(8,128)(2,1)S(1)}, bf16[10,2,128,128]{3,2,1,0:T(8,128)(2,1)}, u32[]{:S(2)}) copy-start(bf16[10,2,128,128]{3,2,1,0:T(8,128)(2,1)} %get-tuple-element.56) | copy-start | bytes 1966084
  48.4 16.0 %collective-permute-start.11 = (bf16[10,2,128,128]{3,2,1,0:T(8,128)(2,1)}, bf16[10,2,128,128]{3,2,1,0:T(8,128)(2,1)S(1)}, u32[]{:S(2)}, u32[]{:S(2)}) collective-permute-start(bf16[10,2,128,128]{3,2,1,0:T(8,128)(2,1)} %get-tuple-element.62), channel_id=1, source_target_pairs={{0,16},{16,0},{32,48},{48,32},{64,80},{80,64},{96,112},{112,96},{1... | collective-permute-start | bytes 1966088 | tf_op jit(solution)/shard_map/ppermute | solution.py:451
  49.0 22.9 %collective-permute-start.9 = (bf16[10,2,128,128]{3,2,1,0:T(8,128)(2,1)}, bf16[10,2,128,128]{3,2,1,0:T(8,128)(2,1)S(1)}, u32[]{:S(2)}, u32[]{:S(2)}) collective-permute-start(bf16[10,2,128,128]{3,2,1,0:T(8,128)(2,1)} %get-tuple-element.59), channel_id=1, source_target_pairs={{0,80},{16,64},{32,112},{48,96},{64,16},{80,0},{96,48},{112,32},{1... | collective-permute-start | bytes 1966088 | tf_op jit(solution)/shard_map/ppermute | solution.py:451
  49.7 14.7 %copy-start.2 = (bf16[2,5,128,256]{3,2,1,0:T(8,128)(2,1)}, bf16[2,5,128,256]{3,2,1,0:T(8,128)(2,1)S(1)}, u32[]{:S(2)}) copy-start(bf16[2,5,128,256]{3,2,1,0:T(8,128)(2,1)S(1)} %multiply_convert_fusion.own) | copy-start | bytes 1966084
  49.7 27.2 %collective-permute-start.5 = (bf16[2,5,128,256]{3,2,1,0:T(8,128)(2,1)S(1)}, bf16[2,5,128,256]{3,2,1,0:T(8,128)(2,1)S(1)}, u32[]{:S(2)}, u32[]{:S(2)}) collective-permute-start(bf16[2,5,128,256]{3,2,1,0:T(8,128)(2,1)S(1)} %multiply_convert_fusion.own), channel_id=1, source_target_pairs={{1,0},{2,1},{3,2},{4,3},{5,4},{6,5},{7,6},{8,7},{9,8},{10,9},{11,1... | collective-permute-start | bytes 1966088 | tf_op jit(solution)/shard_map/ppermute | solution.py:451
  53.9 28.1 %collective-permute-start.6 = (bf16[10,2,128,128]{3,2,1,0:T(8,128)(2,1)S(1)}, bf16[10,2,128,128]{3,2,1,0:T(8,128)(2,1)S(1)}, u32[]{:S(2)}, u32[]{:S(2)}) collective-permute-start(bf16[10,2,128,128]{3,2,1,0:T(8,128)(2,1)S(1)} %copy-done.25), channel_id=1, source_target_pairs={{0,64},{16,80},{32,96},{48,112},{64,0},{80,16},{96,32},{112,48},{1... | collective-permute-start | bytes 1966088 | tf_op jit(solution)/shard_map/ppermute | solution.py:451
  56.8 2.7 %copy-start = (bf16[10,4,2,128,128]{4,3,2,1,0:T(8,128)(2,1)}, bf16[10,4,2,128,128]{4,3,2,1,0:T(8,128)(2,1)S(1)}, u32[]{:S(2)}) copy-start(bf16[10,4,2,128,128]{4,3,2,1,0:T(8,128)(2,1)S(1)} %collective-permute-done.4.pair) | copy-start | bytes 7864324
  56.8 14.3 %collective-permute-start.8 = (bf16[2,3,128,256]{3,2,1,0:T(8,128)(2,1)S(1)}, bf16[2,3,128,256]{3,2,1,0:T(8,128)(2,1)S(1)}, u32[]{:S(2)}, u32[]{:S(2)}) collective-permute-start(bf16[2,3,128,256]{3,2,1,0:T(8,128)(2,1)S(1)} %slice.14), channel_id=1, source_target_pairs={{2,0},{3,1},{4,2},{5,3},{6,4},{7,5},{8,6},{9,7},{10,8},{11,9},{12,... | collective-permute-start | bytes 1179656 | tf_op jit(solution)/shard_map/ppermute | solution.py:451
  65.3 21.0 %copy-start.3 = (bf16[2,5,128,256]{3,2,1,0:T(8,128)(2,1)S(1)}, bf16[2,5,128,256]{3,2,1,0:T(8,128)(2,1)}, u32[]{:S(2)}) copy-start(bf16[2,5,128,256]{3,2,1,0:T(8,128)(2,1)} %copy-done.2) | copy-start | bytes 1966084
  65.3 57.0 %collective-permute-start.12 = (bf16[20,2,128,128]{3,2,1,0:T(8,128)(2,1)}, bf16[20,2,128,128]{3,2,1,0:T(8,128)(2,1)S(1)}, u32[]{:S(2)}, u32[]{:S(2)}) collective-permute-start(bf16[20,2,128,128]{3,2,1,0:T(8,128)(2,1)} %get-tuple-element.63), channel_id=1, source_target_pairs={{0,64},{16,80},{32,96},{48,112},{64,0},{80,16},{96,32},{112,48},{1... | collective-permute-start | bytes 3932168 | tf_op jit(solution)/shard_map/ppermute | solution.py:451
  72.7 64.5 %collective-permute-start.10 = (bf16[20,2,128,128]{3,2,1,0:T(8,128)(2,1)}, bf16[20,2,128,128]{3,2,1,0:T(8,128)(2,1)}, u32[]{:S(2)}, u32[]{:S(2)}) collective-permute-start(bf16[20,2,128,128]{3,2,1,0:T(8,128)(2,1)} %get-tuple-element.60), channel_id=1, source_target_pairs={{0,96},{16,112},{32,0},{48,16},{64,32},{80,48},{96,64},{112,80},{1... | collective-permute-start | bytes 3932168 | tf_op jit(solution)/shard_map/ppermute | solution.py:451
  82.9 55.1 %collective-permute-start.7 = (bf16[20,2,128,128]{3,2,1,0:T(8,128)(2,1)}, bf16[20,2,128,128]{3,2,1,0:T(8,128)(2,1)}, u32[]{:S(2)}, u32[]{:S(2)}) collective-permute-start(bf16[20,2,128,128]{3,2,1,0:T(8,128)(2,1)} %get-tuple-element.57), channel_id=1, source_target_pairs={{0,32},{16,48},{32,64},{48,80},{64,96},{80,112},{96,0},{112,16},{1... | collective-permute-start | bytes 3932168 | tf_op jit(solution)/shard_map/ppermute | solution.py:451
  84.3 6.1 %copy-start.4 = (bf16[10,2,128,128]{3,2,1,0:T(8,128)(2,1)S(1)}, bf16[10,2,128,128]{3,2,1,0:T(8,128)(2,1)}, u32[]{:S(2)}) copy-start(bf16[10,2,128,128]{3,2,1,0:T(8,128)(2,1)} %get-tuple-element.85.refs_0_) | copy-start | bytes 1966084
  86.3 1.1 copy-start.6
  88.4 2.0 %copy-start.8 = (bf16[10,2,128,128]{3,2,1,0:T(8,128)(2,1)S(1)}, bf16[10,2,128,128]{3,2,1,0:T(8,128)(2,1)}, u32[]{:S(2)}) copy-start(bf16[10,2,128,128]{3,2,1,0:T(8,128)(2,1)} %copy-done.7) | copy-start | bytes 1966084
  88.4 2.0 %copy-start.10 = (bf16[10,2,128,128]{3,2,1,0:T(8,128)(2,1)S(1)}, bf16[10,2,128,128]{3,2,1,0:T(8,128)(2,1)}, u32[]{:S(2)}) copy-start(bf16[10,2,128,128]{3,2,1,0:T(8,128)(2,1)} %copy-done.9) | copy-start | bytes 1966084
  90.4 1.1 copy-start.12
  95.9 42.2 %copy-start.1 = (bf16[10,4,2,128,128]{4,3,2,1,0:T(8,128)(2,1)S(1)}, bf16[10,4,2,128,128]{4,3,2,1,0:T(8,128)(2,1)}, u32[]{:S(2)}) copy-start(bf16[10,4,2,128,128]{4,3,2,1,0:T(8,128)(2,1)} %copy-done) | copy-start | bytes 7864324
  95.9 42.2 %copy-start.23 = (s32[2]{0:T(128)S(1)}, s32[2]{0:T(128)}, u32[]{:S(2)}) copy-start(s32[2]{0:T(128)} %pad_add_fusion.place) | copy-start | bytes 28
  104.8 17.5 %collective-permute-start.13 = (bf16[5,128,256]{2,1,0:T(8,128)(2,1)S(1)}, bf16[5,128,256]{2,1,0:T(8,128)(2,1)S(1)}, u32[]{:S(2)}, u32[]{:S(2)}) collective-permute-start(bf16[5,128,256]{2,1,0:T(8,128)(2,1)S(1)} %get-tuple-element.68), channel_id=1, source_target_pairs={{0,1},{1,2},{2,3},{3,4},{4,5},{5,6},{6,7},{7,8},{8,9},{9,10},{10,1... | collective-permute-start | bytes 983048 | tf_op jit(solution)/shard_map/ppermute | solution.py:451
  108.4 13.8 %collective-permute-start.14 = (bf16[3,128,256]{2,1,0:T(8,128)(2,1)S(1)}, bf16[3,128,256]{2,1,0:T(8,128)(2,1)S(1)}, u32[]{:S(2)}, u32[]{:S(2)}) collective-permute-start(bf16[3,128,256]{2,1,0:T(8,128)(2,1)S(1)} %get-tuple-element.69), channel_id=1, source_target_pairs={{0,2},{1,3},{2,4},{3,5},{4,6},{5,7},{6,8},{7,9},{8,10},{9,11},{10,... | collective-permute-start | bytes 589832 | tf_op jit(solution)/shard_map/ppermute | solution.py:451
  144.8 17.9 %collective-permute-start.15 = (bf16[5,128,256]{2,1,0:T(8,128)(2,1)S(1)}, bf16[5,128,256]{2,1,0:T(8,128)(2,1)S(1)}, u32[]{:S(2)}, u32[]{:S(2)}) collective-permute-start(bf16[5,128,256]{2,1,0:T(8,128)(2,1)S(1)} %get-tuple-element.83), channel_id=1, source_target_pairs={{0,1},{1,2},{2,3},{3,4},{4,5},{5,6},{6,7},{7,8},{8,9},{9,10},{10,1... | collective-permute-start | bytes 983048 | tf_op jit(solution)/shard_map/ppermute | solution.py:451
  148.2 14.2 %collective-permute-start.16 = (bf16[3,128,256]{2,1,0:T(8,128)(2,1)S(1)}, bf16[3,128,256]{2,1,0:T(8,128)(2,1)S(1)}, u32[]{:S(2)}, u32[]{:S(2)}) collective-permute-start(bf16[3,128,256]{2,1,0:T(8,128)(2,1)S(1)} %get-tuple-element.84), channel_id=1, source_target_pairs={{0,2},{1,3},{2,4},{3,5},{4,6},{5,7},{6,8},{7,9},{8,10},{9,11},{10,... | collective-permute-start | bytes 589832 | tf_op jit(solution)/shard_map/ppermute | solution.py:451
  (14 other events, 13.0 us)

commit v4 on v3

--- a/solution.py
+++ b/solution.py
@@ -469,8 +469,10 @@
     def cut(data, j, k):
         return lax.dynamic_index_in_dim(data, 8 * j + targets[k], 1, keepdims=False)
 
-    early = [cut(obs, 0, k) for k in range(2)]
-    early, spectra, obs = lax.optimization_barrier((early, spectra, obs))
+    early = [cut(obs, 0, 0)]
+    _, obs = lax.optimization_barrier((early, obs))
+    early.append(cut(obs, 0, 1))
+    _, spectra, obs = lax.optimization_barrier((early, spectra, obs))
     meta = jnp.concatenate([tile_count.reshape(1), (tile_list - base).reshape(-1)])
     count = meta.shape[0]
     meta = jnp.pad(meta.astype(jnp.bfloat16).reshape(1, count), ((0, share - 1), (0, depth - count)))

time: 182 us -> 183 us (level)
  waiting for transfers between devices: 58.8 us -> 52.2 us
  starting transfers between devices: 41.3 us -> 45.9 us
    ppermute x17, starting transfers between devices: 37.7 us -> 42.4 us  [send(): return lax.ppermute(values, *route)]
    ppermute x17, waiting for transfers between devices: 42.6 us -> 38.1 us  [send(): return lax.ppermute(values, *route)]
    all_to_all x1, waiting for transfers between devices: 16.2 us -> 14.1 us  [local(): load = lax.all_to_all(load, 'prow', split_axis=0, concat_axis=0, tiled=True)]
    squeeze x2 -> x3, local copies, waits for them, and re-layouts: 5.08 us -> 6.64 us  [cut(): return lax.dynamic_index_in_dim(data, 8 * j + targets[k], 1, keepdims=False)]
  transfers between devices with their start and end apart: 18 -> 18, of which waited for: 9 -> 8; matrix products, arithmetic and copies ran while one was open for 8% -> 9% of each run, Pallas kernels for 13% -> 13%
where the time goes in v4:
time: 183 us; the launch traced here: 182 us
  waiting for transfers between devices  52.2 us (29%)
  starting transfers between devices  45.9 us (25%)
  local copies, waits for them, and re-layouts  33.6 us (18%)
  Pallas kernels  30.3 us (17%)
  blocking collectives  16.1 us (9%)
  other arithmetic  2.36 us (1%)
    ppermute x17, starting transfers between devices, send(): return lax.ppermute(values, *route)  42.4 us
    ppermute x17, waiting for transfers between devices, send(): return lax.ppermute(values, *route)  38.1 us
    all_to_all x1, blocking collectives, local(): grad = lax.all_to_all(grad, 'prow', split_axis=0, concat_axis=0, tiled=True)  16.1 us
    unnamed x56, local copies, waits for them, and re-layouts  15.1 us
    all_to_all x1, waiting for transfers between devices, local(): load = lax.all_to_all(load, 'prow', split_axis=0, concat_axis=0, tiled=True)  14.1 us
    pallas_call x1, Pallas kernels, tile_call(): pl.pallas_call(tile_kernel, out_shape=(jax.ShapeDtypeStruct((blocks, widt...  8.88 us
    squeeze x3, local copies, waits for them, and re-layouts, cut(): return lax.dynamic_index_in_dim(data, 8 * j + targets[k], 1, keepdims=False)  6.64 us
    pallas_call x1, Pallas kernels, pack_call(): pl.pallas_call(functools.partial(pack_kernel, j), out_shape=(out, out, ou...  4.79 us
  transfers between devices with their start and end apart: 18, of which 8 were waited for; matrix products, arithmetic and copies ran while one was open for 9% of the time, Pallas kernels for 13%

profile of v4, /device:TPU:32, one launch (start us, length us, event | category | flops | bytes accessed | tf_op | source)
XLA Modules:
  0.0 181.5 jit_solution(3690259799236996590)
XLA Ops:
  0.0 2.0 %dynamic-slice_bitcast_fusion.7 = bf16[10,2,128,128]{3,2,1,0:T(8,128)(2,1)} fusion(bf16[1,1,10,16,2,128,128]{6,5,4,3,2,1,0:T(8,128)(2,1)} %param.7, s32[]{:T(128)S(6)} %select_n.91), kind=kLoop, calls=%fused_computation.12 | loop fusion | bytes 1310724 | tf_op jit(solution)/shard_map/jit(dynamic_index_in_dim)/squeeze | solution.py:470
  2.0 1.6 collective-permute-start
  3.6 2.0 %dynamic-slice_bitcast_fusion.6 = bf16[10,2,128,128]{3,2,1,0:T(8,128)(2,1)} fusion(bf16[10,16,2,128,128]{4,3,2,1,0:T(8,128)(2,1)} %bitcast.51, s32[]{:T(128)S(6)} %select_n.93), kind=kLoop, calls=%fused_computation.11 | loop fusion | bytes 1310724 | tf_op jit(solution)/shard_map/jit(dynamic_index_in_dim)/squeeze | solution.py:470
  5.6 1.7 collective-permute-start.1
  7.2 2.7 %dynamic-slice_bitcast_fusion.4 = (bf16[10,2,128,128]{3,2,1,0:T(8,128)(2,1)}, bf16[10,2,128,128]{3,2,1,0:T(8,128)(2,1)}) fusion(bf16[10,16,2,128,128]{4,3,2,1,0:T(8,128)(2,1)} %bitcast.52, s32[]{:T(128)S(6)} %select_n.95, s32[]{:T(128)S(6)} %select_n.94), kind=kLoop, calls=%fused_computation.9 | loop fusion | bytes 2621448 | tf_op jit(solution)/shard_map/jit(dynamic_index_in_dim)/squeeze | solution.py:470
  9.9 3.0 %collective-permute-start.3 = (bf16[10,2,128,128]{3,2,1,0:T(8,128)(2,1)}, bf16[10,2,128,128]{3,2,1,0:T(8,128)(2,1)S(1)}, u32[]{:S(2)}, u32[]{:S(2)}) collective-permute-start(bf16[10,2,128,128]{3,2,1,0:T(8,128)(2,1)} %get-tuple-element.87), channel_id=1, source_target_pairs={{0,112},{16,96},{32,16},{48,0},{64,48},{80,32},{96,80},{112,64},{1... | collective-permute-start | bytes 1966088 | tf_op jit(solution)/shard_map/ppermute | solution.py:451
  17.3 3.5 %all-to-all-start = ((bf16[8,11,16,256]{3,2,1,0:T(8,128)(2,1)}), bf16[8,11,16,256]{3,2,1,0:T(8,128)(2,1)S(1)}, u32[]{:S(2)}, u32[]{:S(2)}) async-start(bf16[8,11,16,256]{3,2,1,0:T(8,128)(2,1)} %pad_maximum_fusion), calls=%async_computation | async-start | bytes 1441792 | tf_op jit(solution)/shard_map/all_to_all | solution.py:483
  21.5 3.9 %swap.1 = bf16[10,4,2,128,128]{4,3,2,1,0:T(8,128)(2,1)} custom-call(s32[2]{0:T(128)} %pad_add_fusion.place, bf16[10,2,4,2,2,128,128]{6,5,4,3,2,1,0:T(8,128)(2,1)} %bitcast.53), custom_call_target="tpu_custom_call" | custom-call | tf_op jit(solution)/shard_map/swap/pallas_call | solution.py:289
  25.5 3.3 %dynamic-slice_bitcast_fusion = (bf16[10,2,128,128]{3,2,1,0:T(8,128)(2,1)}, bf16[10,2,128,128]{3,2,1,0:T(8,128)(2,1)}, bf16[10,2,128,128]{3,2,1,0:T(8,128)(2,1)}, bf16[10,2,128,128]{3,2,1,0:T(8,128)(2,1)}) fusion(bf16[10,16,2,128,128]{4,3,2,1,0:T(8,128)(2,1)} %bitcast.54, s32[]{:T(128)S(6)} %select_n.105, s32[]{:T(128)S(6)} %select_n.100, s32[]{:T(128)S(6)} %select_n.99, ...), kind=kLoop, calls=%fused_computation.5 | loop fusion | bytes 5242896 | tf_op jit(solution)/shard_map/jit(dynamic_index_in_dim)/squeeze | solution.py:513
  28.8 14.1 %all-to-all-done = bf16[8,11,16,256]{3,2,1,0:T(8,128)(2,1)S(1)} async-done(((bf16[8,11,16,256]{3,2,1,0:T(8,128)(2,1)}), bf16[8,11,16,256]{3,2,1,0:T(8,128)(2,1)S(1)}, u32[]{:S(2)}, u32[]{:S(2)}) %all-to-all-start) | async-done | bytes 720928 | tf_op jit(solution)/shard_map/all_to_all | solution.py:483
  49.7 4.2 %collective-permute-start.5 = (bf16[2,5,128,256]{3,2,1,0:T(8,128)(2,1)S(1)}, bf16[2,5,128,256]{3,2,1,0:T(8,128)(2,1)S(1)}, u32[]{:S(2)}, u32[]{:S(2)}) collective-permute-start(bf16[2,5,128,256]{3,2,1,0:T(8,128)(2,1)S(1)} %multiply_convert_fusion.own), channel_id=1, source_target_pairs={{1,0},{2,1},{3,2},{4,3},{5,4},{6,5},{7,6},{8,7},{9,8},{10,9},{11,1... | collective-permute-start | bytes 1966088 | tf_op jit(solution)/shard_map/ppermute | solution.py:451
  53.9 2.3 %collective-permute-start.6 = (bf16[10,2,128,128]{3,2,1,0:T(8,128)(2,1)S(1)}, bf16[10,2,128,128]{3,2,1,0:T(8,128)(2,1)S(1)}, u32[]{:S(2)}, u32[]{:S(2)}) collective-permute-start(bf16[10,2,128,128]{3,2,1,0:T(8,128)(2,1)S(1)} %copy-done.25), channel_id=1, source_target_pairs={{0,64},{16,80},{32,96},{48,112},{64,0},{80,16},{96,32},{112,48},{1... | collective-permute-start | bytes 1966088 | tf_op jit(solution)/shard_map/ppermute | solution.py:451
  56.2 2.7 %collective-permute-start.8 = (bf16[2,3,128,256]{3,2,1,0:T(8,128)(2,1)S(1)}, bf16[2,3,128,256]{3,2,1,0:T(8,128)(2,1)S(1)}, u32[]{:S(2)}, u32[]{:S(2)}) collective-permute-start(bf16[2,3,128,256]{3,2,1,0:T(8,128)(2,1)S(1)} %slice.14), channel_id=1, source_target_pairs={{2,0},{3,1},{4,2},{5,3},{6,4},{7,5},{8,6},{9,7},{10,8},{11,9},{12,... | collective-permute-start | bytes 1179656 | tf_op jit(solution)/shard_map/ppermute | solution.py:451
  59.0 4.8 %pack.1 = (bf16[20,2,128,128]{3,2,1,0:T(8,128)(2,1)}, bf16[20,2,128,128]{3,2,1,0:T(8,128)(2,1)}, bf16[20,2,128,128]{3,2,1,0:T(8,128)(2,1)}) custom-call(s32[2]{0:T(128)} %pad_add_fusion.place, bf16[10,2,4,2,2,128,128]{6,5,4,3,2,1,0:T(8,128)(2,1)} %bitcast.55, bf16[10,4,2,128,128]{4,3,2,1,0:T(8,128)(2,1)} %copy-done), custom_call_target="tpu_custom_call" | custom-call | tf_op jit(solution)/shard_map/pack/pallas_call | solution.py:317
  66.0 4.6 %collective-permute-done.8.far = bf16[2,3,128,256]{3,2,1,0:T(8,128)(2,1)S(1)} collective-permute-done((bf16[2,3,128,256]{3,2,1,0:T(8,128)(2,1)S(1)}, bf16[2,3,128,256]{3,2,1,0:T(8,128)(2,1)S(1)}, u32[]{:S(2)}, u32[]{:S(2)}) %collective-permute-start.8) | collective-permute-done | bytes 393248 | tf_op jit(solution)/shard_map/ppermute | solution.py:451
  72.2 3.8 %collective-permute-start.10 = (bf16[20,2,128,128]{3,2,1,0:T(8,128)(2,1)}, bf16[20,2,128,128]{3,2,1,0:T(8,128)(2,1)}, u32[]{:S(2)}, u32[]{:S(2)}) collective-permute-start(bf16[20,2,128,128]{3,2,1,0:T(8,128)(2,1)} %get-tuple-element.58), channel_id=1, source_target_pairs={{0,96},{16,112},{32,0},{48,16},{64,32},{80,48},{96,64},{112,80},{1... | collective-permute-start | bytes 3932168 | tf_op jit(solution)/shard_map/ppermute | solution.py:451
  77.9 3.5 %collective-permute-done.6.refs_6_ = bf16[10,2,128,128]{3,2,1,0:T(8,128)(2,1)S(1)} collective-permute-done((bf16[10,2,128,128]{3,2,1,0:T(8,128)(2,1)S(1)}, bf16[10,2,128,128]{3,2,1,0:T(8,128)(2,1)S(1)}, u32[]{:S(2)}, u32[]{:S(2)}) %collective-permute-start.6) | collective-permute-done | bytes 655392 | tf_op jit(solution)/shard_map/ppermute | solution.py:451
  82.2 3.2 %collective-permute-start.7 = (bf16[20,2,128,128]{3,2,1,0:T(8,128)(2,1)}, bf16[20,2,128,128]{3,2,1,0:T(8,128)(2,1)}, u32[]{:S(2)}, u32[]{:S(2)}) collective-permute-start(bf16[20,2,128,128]{3,2,1,0:T(8,128)(2,1)} %get-tuple-element.55), channel_id=1, source_target_pairs={{0,32},{16,48},{32,64},{48,80},{64,96},{80,112},{96,0},{112,16},{1... | collective-permute-start | bytes 3932168 | tf_op jit(solution)/shard_map/ppermute | solution.py:451
  89.7 2.0 %setup.1 = (s32[45]{0:T(128)S(1)}, s32[45]{0:T(128)S(1)}, bf16[13,256,256]{2,1,0:T(8,128)(2,1)S(1)}, bf16[13,256,256]{2,1,0:T(8,128)(2,1)S(1)}, bf16[5,256,256]{...) custom-call(s32[8,21]{1,0:T(8,128)S(1)} %gather_fusion, bf16[2,5,128,256]{3,2,1,0:T(8,128)(2,1)S(1)} %copy-done.3, ...), custom_call_target="tpu_custom_call" | custom-call | tf_op jit(solution)/shard_map/setup/pallas_call | solution.py:64
  97.2 8.9 %tiles.1 = (f32[5,128,256]{2,1,0:T(8,128)S(1)}, bf16[5,128,256]{2,1,0:T(8,128)(2,1)S(1)}, bf16[3,128,256]{2,1,0:T(8,128)(2,1)S(1)}) custom-call(s32[45]{0:T(128)S(1)} %get-tuple-element.62.table, bf16[10,2,128,128]{3,2,1,0:T(8,128)(2,1)S(1)} %copy-done.4, bf16[10,2,128,128]{3,2,1,0:T(8,128)(2,1)S(1)} %copy-done.8, bf16[10,2,128,128]{3,2,1,0:T(8,128)(2,1)S(1)} %copy-done.10, ...), custom_call_target="tpu_custom_call" | custom-call | tf_op jit(solution)/shard_map/tiles/pallas_call | solution.py:384
  106.1 3.8 %collective-permute-start.13 = (bf16[5,128,256]{2,1,0:T(8,128)(2,1)S(1)}, bf16[5,128,256]{2,1,0:T(8,128)(2,1)S(1)}, u32[]{:S(2)}, u32[]{:S(2)}) collective-permute-start(bf16[5,128,256]{2,1,0:T(8,128)(2,1)S(1)} %get-tuple-element.66), channel_id=1, source_target_pairs={{0,1},{1,2},{2,3},{3,4},{4,5},{5,6},{6,7},{7,8},{8,9},{9,10},{10,1... | collective-permute-start | bytes 983048 | tf_op jit(solution)/shard_map/ppermute | solution.py:451
  109.9 5.1 %collective-permute-start.14 = (bf16[3,128,256]{2,1,0:T(8,128)(2,1)S(1)}, bf16[3,128,256]{2,1,0:T(8,128)(2,1)S(1)}, u32[]{:S(2)}, u32[]{:S(2)}) collective-permute-start(bf16[3,128,256]{2,1,0:T(8,128)(2,1)S(1)} %get-tuple-element.67), channel_id=1, source_target_pairs={{0,2},{1,3},{2,4},{3,5},{4,6},{5,7},{6,8},{7,9},{8,10},{9,11},{10,... | collective-permute-start | bytes 589832 | tf_op jit(solution)/shard_map/ppermute | solution.py:451
  115.0 8.8 %collective-permute-done.14.far0 = bf16[3,128,256]{2,1,0:T(8,128)(2,1)S(1)} collective-permute-done((bf16[3,128,256]{2,1,0:T(8,128)(2,1)S(1)}, bf16[3,128,256]{2,1,0:T(8,128)(2,1)S(1)}, u32[]{:S(2)}, u32[]{:S(2)}) %collective-permute-start.14) | collective-permute-done | bytes 196640 | tf_op jit(solution)/shard_map/ppermute | solution.py:451
  123.8 14.4 %collective-permute-done.10.second = bf16[20,2,128,128]{3,2,1,0:T(8,128)(2,1)} collective-permute-done((bf16[20,2,128,128]{3,2,1,0:T(8,128)(2,1)}, bf16[20,2,128,128]{3,2,1,0:T(8,128)(2,1)}, u32[]{:S(2)}, u32[]{:S(2)}) %collective-permute-start.10) | collective-permute-done | bytes 1310752 | tf_op jit(solution)/shard_map/ppermute | solution.py:451
  138.2 2.5 %collect.1.held = bf16[80,2,128,128]{3,2,1,0:T(8,128)(2,1)S(1)} custom-call(s32[2]{0:T(128)S(1)} %copy-done.23, bf16[10,2,4,2,2,128,128]{6,5,4,3,2,1,0:T(8,128)(2,1)} %bitcast.56, bf16[10,4,2,128,128]{4,3,2,1,0:T(8,128)(2,1)S(1)} %copy-done.1, bf16[20,2,128,128]{3,2,1,0:T(8,128)(2,1)} %collective-permute-done.7.first, ...), custom_call_target="tpu_custom_call" | custom-call | tf_op jit(solution)/shard_map/collect/pallas_call | solution.py:270
  142.0 2.9 %side.3 = (bf16[5,5,256,128]{3,2,1,0:T(8,128)(2,1)S(1)}, bf16[5,128,256]{2,1,0:T(8,128)(2,1)S(1)}) custom-call(s32[45]{0:T(128)S(1)} %get-tuple-element.71.table, bf16[80,2,128,128]{3,2,1,0:T(8,128)(2,1)S(1)} %collect.1.held, bf16[13,256,256]{2,1,0:T(8,128)(2,1)S(1)} %get-tuple-element.75.stack, bf16[5,256,256]{2,1,0:T(8,128)(2,1)S(1)} %get-tuple-element.76.back), custom_call_target="tpu_custom_call" | custom-call | tf_op jit(solution)/shard_map/side/pallas_call | solution.py:211
  144.9 3.4 %collective-permute-start.15 = (bf16[5,128,256]{2,1,0:T(8,128)(2,1)S(1)}, bf16[5,128,256]{2,1,0:T(8,128)(2,1)S(1)}, u32[]{:S(2)}, u32[]{:S(2)}) collective-permute-start(bf16[5,128,256]{2,1,0:T(8,128)(2,1)S(1)} %get-tuple-element.81), channel_id=1, source_target_pairs={{0,1},{1,2},{2,3},{3,4},{4,5},{5,6},{6,7},{7,8},{8,9},{9,10},{10,1... | collective-permute-start | bytes 983048 | tf_op jit(solution)/shard_map/ppermute | solution.py:451
  148.3 4.8 %collective-permute-start.16 = (bf16[3,128,256]{2,1,0:T(8,128)(2,1)S(1)}, bf16[3,128,256]{2,1,0:T(8,128)(2,1)S(1)}, u32[]{:S(2)}, u32[]{:S(2)}) collective-permute-start(bf16[3,128,256]{2,1,0:T(8,128)(2,1)S(1)} %get-tuple-element.82), channel_id=1, source_target_pairs={{0,2},{1,3},{2,4},{3,5},{4,6},{5,7},{6,8},{7,9},{8,10},{9,11},{10,... | collective-permute-start | bytes 589832 | tf_op jit(solution)/shard_map/ppermute | solution.py:451
  153.1 3.4 %nearby.1.own1 = f32[5,128,256]{2,1,0:T(8,128)S(1)} custom-call(s32[45]{0:T(128)S(1)} %get-tuple-element.71.table, bf16[80,2,128,128]{3,2,1,0:T(8,128)(2,1)S(1)} %collect.1.held, bf16[13,256,256]{2,1,0:T(8,128)(2,1)S(1)} %get-tuple-element.75.stack, bf16[5,256,256]{2,1,0:T(8,128)(2,1)S(1)} %get-tuple-element.76.back, ...), custom_call_target="tpu_custom_call" | custom-call | tf_op jit(solution)/shard_map/nearby/pallas_call | solution.py:229
  156.5 5.4 %collective-permute-done.16.far1 = bf16[3,128,256]{2,1,0:T(8,128)(2,1)S(1)} collective-permute-done((bf16[3,128,256]{2,1,0:T(8,128)(2,1)S(1)}, bf16[3,128,256]{2,1,0:T(8,128)(2,1)S(1)}, u32[]{:S(2)}, u32[]{:S(2)}) %collective-permute-start.16) | collective-permute-done | bytes 196640 | tf_op jit(solution)/shard_map/ppermute | solution.py:451
  162.8 16.1 %all_to_all.10 = bf16[8,2,5,16,256]{4,3,2,1,0:T(8,128)(2,1)S(1)} all-to-all(bf16[8,2,5,16,256]{4,3,2,1,0:T(8,128)(2,1)S(1)} %final.1), channel_id=1, replica_groups=mesh['prow'=8,'pcol'=16] {'prow'}, dimensions={0} | all-to-all | bytes 1310720 | tf_op jit(solution)/shard_map/all_to_all | solution.py:525
  179.8 1.7 reshape.390
  (99 shorter events, 30.4 us)
Async XLA Ops:
  2.0 41.8 %collective-permute-start = (bf16[10,2,128,128]{3,2,1,0:T(8,128)(2,1)}, bf16[10,2,128,128]{3,2,1,0:T(8,128)(2,1)S(1)}, u32[]{:S(2)}, u32[]{:S(2)}) collective-permute-start(bf16[10,2,128,128]{3,2,1,0:T(8,128)(2,1)} %dynamic-slice_bitcast_fusion.7), channel_id=1, source_target_pairs={{0,32},{16,48},{32,64},{48,80},{64,96},{80,112},{96,0},{112,16},{1... | collective-permute-start | bytes 1966088 | tf_op jit(solution)/shard_map/ppermute | solution.py:451
  5.6 37.3 %collective-permute-start.1 = (bf16[10,2,128,128]{3,2,1,0:T(8,128)(2,1)}, bf16[10,2,128,128]{3,2,1,0:T(8,128)(2,1)S(1)}, u32[]{:S(2)}, u32[]{:S(2)}) collective-permute-start(bf16[10,2,128,128]{3,2,1,0:T(8,128)(2,1)} %dynamic-slice_bitcast_fusion.6), channel_id=1, source_target_pairs={{0,96},{16,112},{32,0},{48,16},{64,32},{80,48},{96,64},{112,80},{1... | collective-permute-start | bytes 1966088 | tf_op jit(solution)/shard_map/ppermute | solution.py:451
  7.2 5.6 %copy-start.26 = (bf16[5,16,16,2,128]{4,3,2,1,0:T(2,128)(2,1)S(1)}, bf16[5,16,16,2,128]{4,3,2,1,0:T(2,128)(2,1)}, u32[]{:S(2)}) copy-start(bf16[5,16,16,2,128]{4,3,2,1,0:T(2,128)(2,1)} %param.4) | copy-start | bytes 1966084
  9.9 34.7 %collective-permute-start.2 = (bf16[10,2,128,128]{3,2,1,0:T(8,128)(2,1)}, bf16[10,2,128,128]{3,2,1,0:T(8,128)(2,1)S(1)}, u32[]{:S(2)}, u32[]{:S(2)}) collective-permute-start(bf16[10,2,128,128]{3,2,1,0:T(8,128)(2,1)} %get-tuple-element.88), channel_id=1, source_target_pairs={{0,48},{16,32},{32,80},{48,64},{64,112},{80,96},{96,16},{112,0},{1... | collective-permute-start | bytes 1966088 | tf_op jit(solution)/shard_map/ppermute | solution.py:451
  9.9 5.5 %copy-start.27 = (s32[1,1,10,2]{2,3,1,0:T(2,128)S(1)}, s32[1,1,10,2]{2,3,1,0:T(2,128)}, u32[]{:S(2)}) copy-start(s32[1,1,10,2]{2,3,1,0:T(2,128)} %param.5) | copy-start | bytes 244
  9.9 35.6 %collective-permute-start.3 = (bf16[10,2,128,128]{3,2,1,0:T(8,128)(2,1)}, bf16[10,2,128,128]{3,2,1,0:T(8,128)(2,1)S(1)}, u32[]{:S(2)}, u32[]{:S(2)}) collective-permute-start(bf16[10,2,128,128]{3,2,1,0:T(8,128)(2,1)} %get-tuple-element.87), channel_id=1, source_target_pairs={{0,112},{16,96},{32,16},{48,0},{64,48},{80,32},{96,80},{112,64},{1... | collective-permute-start | bytes 1966088 | tf_op jit(solution)/shard_map/ppermute | solution.py:451
  17.3 25.6 %all-to-all-start = ((bf16[8,11,16,256]{3,2,1,0:T(8,128)(2,1)}), bf16[8,11,16,256]{3,2,1,0:T(8,128)(2,1)S(1)}, u32[]{:S(2)}, u32[]{:S(2)}) async-start(bf16[8,11,16,256]{3,2,1,0:T(8,128)(2,1)} %pad_maximum_fusion), calls=%async_computation | async-start | bytes 1441792 | tf_op jit(solution)/shard_map/all_to_all | solution.py:483
  42.9 1.7 copy-start.24
  46.3 9.9 %collective-permute-start.4 = (bf16[10,4,2,128,128]{4,3,2,1,0:T(8,128)(2,1)}, bf16[10,4,2,128,128]{4,3,2,1,0:T(8,128)(2,1)S(1)}, u32[]{:S(2)}, u32[]{:S(2)}) collective-permute-start(bf16[10,4,2,128,128]{4,3,2,1,0:T(8,128)(2,1)} %swap.1), channel_id=1, source_target_pairs={{0,16},{16,0},{32,48},{48,32},{64,80},{80,64},{96,112},{112,96},{1... | collective-permute-start | bytes 7864328 | tf_op jit(solution)/shard_map/ppermute | solution.py:451
  47.9 6.0 %copy-start.25 = (bf16[10,2,128,128]{3,2,1,0:T(8,128)(2,1)S(1)}, bf16[10,2,128,128]{3,2,1,0:T(8,128)(2,1)}, u32[]{:S(2)}) copy-start(bf16[10,2,128,128]{3,2,1,0:T(8,128)(2,1)} %get-tuple-element.54) | copy-start | bytes 1966084
  47.9 23.5 %collective-permute-start.9 = (bf16[10,2,128,128]{3,2,1,0:T(8,128)(2,1)}, bf16[10,2,128,128]{3,2,1,0:T(8,128)(2,1)S(1)}, u32[]{:S(2)}, u32[]{:S(2)}) collective-permute-start(bf16[10,2,128,128]{3,2,1,0:T(8,128)(2,1)} %get-tuple-element.57), channel_id=1, source_target_pairs={{0,80},{16,64},{32,112},{48,96},{64,16},{80,0},{96,48},{112,32},{1... | collective-permute-start | bytes 1966088 | tf_op jit(solution)/shard_map/ppermute | solution.py:451
  49.4 14.3 %collective-permute-start.11 = (bf16[10,2,128,128]{3,2,1,0:T(8,128)(2,1)}, bf16[10,2,128,128]{3,2,1,0:T(8,128)(2,1)S(1)}, u32[]{:S(2)}, u32[]{:S(2)}) collective-permute-start(bf16[10,2,128,128]{3,2,1,0:T(8,128)(2,1)} %get-tuple-element.60), channel_id=1, source_target_pairs={{0,16},{16,0},{32,48},{48,32},{64,80},{80,64},{96,112},{112,96},{1... | collective-permute-start | bytes 1966088 | tf_op jit(solution)/shard_map/ppermute | solution.py:451
  49.7 14.1 %copy-start.2 = (bf16[2,5,128,256]{3,2,1,0:T(8,128)(2,1)}, bf16[2,5,128,256]{3,2,1,0:T(8,128)(2,1)S(1)}, u32[]{:S(2)}) copy-start(bf16[2,5,128,256]{3,2,1,0:T(8,128)(2,1)S(1)} %multiply_convert_fusion.own) | copy-start | bytes 1966084
  49.7 27.3 %collective-permute-start.5 = (bf16[2,5,128,256]{3,2,1,0:T(8,128)(2,1)S(1)}, bf16[2,5,128,256]{3,2,1,0:T(8,128)(2,1)S(1)}, u32[]{:S(2)}, u32[]{:S(2)}) collective-permute-start(bf16[2,5,128,256]{3,2,1,0:T(8,128)(2,1)S(1)} %multiply_convert_fusion.own), channel_id=1, source_target_pairs={{1,0},{2,1},{3,2},{4,3},{5,4},{6,5},{7,6},{8,7},{9,8},{10,9},{11,1... | collective-permute-start | bytes 1966088 | tf_op jit(solution)/shard_map/ppermute | solution.py:451
  53.9 27.5 %collective-permute-start.6 = (bf16[10,2,128,128]{3,2,1,0:T(8,128)(2,1)S(1)}, bf16[10,2,128,128]{3,2,1,0:T(8,128)(2,1)S(1)}, u32[]{:S(2)}, u32[]{:S(2)}) collective-permute-start(bf16[10,2,128,128]{3,2,1,0:T(8,128)(2,1)S(1)} %copy-done.25), channel_id=1, source_target_pairs={{0,64},{16,80},{32,96},{48,112},{64,0},{80,16},{96,32},{112,48},{1... | collective-permute-start | bytes 1966088 | tf_op jit(solution)/shard_map/ppermute | solution.py:451
  56.2 2.7 %copy-start = (bf16[10,4,2,128,128]{4,3,2,1,0:T(8,128)(2,1)}, bf16[10,4,2,128,128]{4,3,2,1,0:T(8,128)(2,1)S(1)}, u32[]{:S(2)}) copy-start(bf16[10,4,2,128,128]{4,3,2,1,0:T(8,128)(2,1)S(1)} %collective-permute-done.4.pair) | copy-start | bytes 7864324
  56.2 14.4 %collective-permute-start.8 = (bf16[2,3,128,256]{3,2,1,0:T(8,128)(2,1)S(1)}, bf16[2,3,128,256]{3,2,1,0:T(8,128)(2,1)S(1)}, u32[]{:S(2)}, u32[]{:S(2)}) collective-permute-start(bf16[2,3,128,256]{3,2,1,0:T(8,128)(2,1)S(1)} %slice.14), channel_id=1, source_target_pairs={{2,0},{3,1},{4,2},{5,3},{6,4},{7,5},{8,6},{9,7},{10,8},{11,9},{12,... | collective-permute-start | bytes 1179656 | tf_op jit(solution)/shard_map/ppermute | solution.py:451
  64.6 23.0 %copy-start.3 = (bf16[2,5,128,256]{3,2,1,0:T(8,128)(2,1)S(1)}, bf16[2,5,128,256]{3,2,1,0:T(8,128)(2,1)}, u32[]{:S(2)}) copy-start(bf16[2,5,128,256]{3,2,1,0:T(8,128)(2,1)} %copy-done.2) | copy-start | bytes 1966084
  64.6 59.1 %collective-permute-start.12 = (bf16[20,2,128,128]{3,2,1,0:T(8,128)(2,1)}, bf16[20,2,128,128]{3,2,1,0:T(8,128)(2,1)S(1)}, u32[]{:S(2)}, u32[]{:S(2)}) collective-permute-start(bf16[20,2,128,128]{3,2,1,0:T(8,128)(2,1)} %get-tuple-element.61), channel_id=1, source_target_pairs={{0,64},{16,80},{32,96},{48,112},{64,0},{80,16},{96,32},{112,48},{1... | collective-permute-start | bytes 3932168 | tf_op jit(solution)/shard_map/ppermute | solution.py:451
  72.2 66.0 %collective-permute-start.10 = (bf16[20,2,128,128]{3,2,1,0:T(8,128)(2,1)}, bf16[20,2,128,128]{3,2,1,0:T(8,128)(2,1)}, u32[]{:S(2)}, u32[]{:S(2)}) collective-permute-start(bf16[20,2,128,128]{3,2,1,0:T(8,128)(2,1)} %get-tuple-element.58), channel_id=1, source_target_pairs={{0,96},{16,112},{32,0},{48,16},{64,32},{80,48},{96,64},{112,80},{1... | collective-permute-start | bytes 3932168 | tf_op jit(solution)/shard_map/ppermute | solution.py:451
  82.2 55.9 %collective-permute-start.7 = (bf16[20,2,128,128]{3,2,1,0:T(8,128)(2,1)}, bf16[20,2,128,128]{3,2,1,0:T(8,128)(2,1)}, u32[]{:S(2)}, u32[]{:S(2)}) collective-permute-start(bf16[20,2,128,128]{3,2,1,0:T(8,128)(2,1)} %get-tuple-element.55), channel_id=1, source_target_pairs={{0,32},{16,48},{32,64},{48,80},{64,96},{80,112},{96,0},{112,16},{1... | collective-permute-start | bytes 3932168 | tf_op jit(solution)/shard_map/ppermute | solution.py:451
  85.6 6.1 %copy-start.4 = (bf16[10,2,128,128]{3,2,1,0:T(8,128)(2,1)S(1)}, bf16[10,2,128,128]{3,2,1,0:T(8,128)(2,1)}, u32[]{:S(2)}) copy-start(bf16[10,2,128,128]{3,2,1,0:T(8,128)(2,1)} %get-tuple-element.83.refs_0_) | copy-start | bytes 1966084
  87.6 1.1 copy-start.6
  89.7 2.0 %copy-start.8 = (bf16[10,2,128,128]{3,2,1,0:T(8,128)(2,1)S(1)}, bf16[10,2,128,128]{3,2,1,0:T(8,128)(2,1)}, u32[]{:S(2)}) copy-start(bf16[10,2,128,128]{3,2,1,0:T(8,128)(2,1)} %copy-done.7) | copy-start | bytes 1966084
  89.7 2.0 %copy-start.10 = (bf16[10,2,128,128]{3,2,1,0:T(8,128)(2,1)S(1)}, bf16[10,2,128,128]{3,2,1,0:T(8,128)(2,1)}, u32[]{:S(2)}) copy-start(bf16[10,2,128,128]{3,2,1,0:T(8,128)(2,1)} %copy-done.9) | copy-start | bytes 1966084
  91.8 1.1 copy-start.12
  97.2 41.0 %copy-start.1 = (bf16[10,4,2,128,128]{4,3,2,1,0:T(8,128)(2,1)S(1)}, bf16[10,4,2,128,128]{4,3,2,1,0:T(8,128)(2,1)}, u32[]{:S(2)}) copy-start(bf16[10,4,2,128,128]{4,3,2,1,0:T(8,128)(2,1)} %copy-done) | copy-start | bytes 7864324
  97.2 41.0 %copy-start.23 = (s32[2]{0:T(128)S(1)}, s32[2]{0:T(128)}, u32[]{:S(2)}) copy-start(s32[2]{0:T(128)} %pad_add_fusion.place) | copy-start | bytes 28
  106.1 17.7 %collective-permute-start.13 = (bf16[5,128,256]{2,1,0:T(8,128)(2,1)S(1)}, bf16[5,128,256]{2,1,0:T(8,128)(2,1)S(1)}, u32[]{:S(2)}, u32[]{:S(2)}) collective-permute-start(bf16[5,128,256]{2,1,0:T(8,128)(2,1)S(1)} %get-tuple-element.66), channel_id=1, source_target_pairs={{0,1},{1,2},{2,3},{3,4},{4,5},{5,6},{6,7},{7,8},{8,9},{9,10},{10,1... | collective-permute-start | bytes 983048 | tf_op jit(solution)/shard_map/ppermute | solution.py:451
  109.9 13.9 %collective-permute-start.14 = (bf16[3,128,256]{2,1,0:T(8,128)(2,1)S(1)}, bf16[3,128,256]{2,1,0:T(8,128)(2,1)S(1)}, u32[]{:S(2)}, u32[]{:S(2)}) collective-permute-start(bf16[3,128,256]{2,1,0:T(8,128)(2,1)S(1)} %get-tuple-element.67), channel_id=1, source_target_pairs={{0,2},{1,3},{2,4},{3,5},{4,6},{5,7},{6,8},{7,9},{8,10},{9,11},{10,... | collective-permute-start | bytes 589832 | tf_op jit(solution)/shard_map/ppermute | solution.py:451
  144.9 17.3 %collective-permute-start.15 = (bf16[5,128,256]{2,1,0:T(8,128)(2,1)S(1)}, bf16[5,128,256]{2,1,0:T(8,128)(2,1)S(1)}, u32[]{:S(2)}, u32[]{:S(2)}) collective-permute-start(bf16[5,128,256]{2,1,0:T(8,128)(2,1)S(1)} %get-tuple-element.81), channel_id=1, source_target_pairs={{0,1},{1,2},{2,3},{3,4},{4,5},{5,6},{6,7},{7,8},{8,9},{9,10},{10,1... | collective-permute-start | bytes 983048 | tf_op jit(solution)/shard_map/ppermute | solution.py:451
  148.3 13.6 %collective-permute-start.16 = (bf16[3,128,256]{2,1,0:T(8,128)(2,1)S(1)}, bf16[3,128,256]{2,1,0:T(8,128)(2,1)S(1)}, u32[]{:S(2)}, u32[]{:S(2)}) collective-permute-start(bf16[3,128,256]{2,1,0:T(8,128)(2,1)S(1)} %get-tuple-element.82), channel_id=1, source_target_pairs={{0,2},{1,3},{2,4},{3,5},{4,6},{5,7},{6,8},{7,9},{8,10},{9,11},{10,... | collective-permute-start | bytes 589832 | tf_op jit(solution)/shard_map/ppermute | solution.py:451
  (14 other events, 12.9 us)

commit v5 on v3

--- a/solution.py
+++ b/solution.py
@@ -17,7 +17,7 @@
 SMEM = pl.BlockSpec(memory_space=pltpu.SMEM)
 ANY = pl.BlockSpec(memory_space=pl.ANY)
 HBM = pl.BlockSpec(memory_space=pltpu.HBM)
-COPY_PARAMS = pltpu.CompilerParams(vmem_limit_bytes=55 * 1024 * 1024)
+COPY_PARAMS = pltpu.CompilerParams(vmem_limit_bytes=46 * 1024 * 1024)
 PARAMS = pltpu.CompilerParams(vmem_limit_bytes=40 * 1024 * 1024)
 
 

time: 182 us -> 181 us (level)
  local copies, waits for them, and re-layouts: 32.1 us -> 34.9 us
  Pallas kernels: 30.2 us -> 28.3 us
    unnamed x56 -> x52, local copies, waits for them, and re-layouts: 15.1 us -> 18 us
  transfers between devices with their start and end apart: 18 -> 18, of which waited for: 9 -> 9; matrix products, arithmetic and copies ran while one was open for 8% -> 7% of each run, Pallas kernels for 13% -> 11%
where the time goes in v5:
time: 181 us; the launch traced here: 180 us
  waiting for transfers between devices  58.3 us (32%)
  starting transfers between devices  41.3 us (23%)
  local copies, waits for them, and re-layouts  34.9 us (19%)
  Pallas kernels  28.3 us (16%)
  blocking collectives  14.7 us (8%)
    ppermute x17, waiting for transfers between devices, send(): return lax.ppermute(values, *route)  41.3 us
    ppermute x17, starting transfers between devices, send(): return lax.ppermute(values, *route)  37.7 us
    unnamed x52, local copies, waits for them, and re-layouts  18 us
    all_to_all x1, waiting for transfers between devices, local(): load = lax.all_to_all(load, 'prow', split_axis=0, concat_axis=0, tiled=True)  17 us
    all_to_all x1, blocking collectives, local(): grad = lax.all_to_all(grad, 'prow', split_axis=0, concat_axis=0, tiled=True)  14.7 us
    pallas_call x1, Pallas kernels, tile_call(): pl.pallas_call(tile_kernel, out_shape=(jax.ShapeDtypeStruct((blocks, widt...  8.88 us
    squeeze x2, local copies, waits for them, and re-layouts, cut(): return lax.dynamic_index_in_dim(data, 8 * j + targets[k], 1, keepdims=False)  5.13 us
    pallas_call x2, Pallas kernels, side_call(): pl.pallas_call(functools.partial(side_kernel, start), out_shape=(jax.Shap...  4.15 us
  transfers between devices with their start and end apart: 18, of which 9 were waited for; matrix products, arithmetic and copies ran while one was open for 7% of the time, Pallas kernels for 11%

profile of v5, /device:TPU:32, one launch (start us, length us, event | category | flops | bytes accessed | tf_op | source)
XLA Modules:
  0.0 180.3 jit_solution(14778634498660976564)
XLA Ops:
  0.0 2.6 %dynamic-slice_bitcast_fusion.6 = (bf16[10,2,128,128]{3,2,1,0:T(8,128)(2,1)}, bf16[10,2,128,128]{3,2,1,0:T(8,128)(2,1)}) fusion(bf16[1,1,10,16,2,128,128]{6,5,4,3,2,1,0:T(8,128)(2,1)} %param.7, s32[]{:T(128)S(6)} %select_n.93, s32[]{:T(128)S(6)} %select_n.91), kind=kLoop, calls=%fused_computation.11 | loop fusion | bytes 2621448 | tf_op jit(solution)/shard_map/jit(dynamic_index_in_dim)/squeeze | solution.py:470
  2.6 1.6 collective-permute-start
  4.2 1.7 collective-permute-start.1
  5.8 2.5 %dynamic-slice_bitcast_fusion.4 = (bf16[10,2,128,128]{3,2,1,0:T(8,128)(2,1)}, bf16[10,2,128,128]{3,2,1,0:T(8,128)(2,1)}) fusion(bf16[10,16,2,128,128]{4,3,2,1,0:T(8,128)(2,1)} %bitcast.51, s32[]{:T(128)S(6)} %select_n.95, s32[]{:T(128)S(6)} %select_n.94), kind=kLoop, calls=%fused_computation.9 | loop fusion | bytes 2621448 | tf_op jit(solution)/shard_map/jit(dynamic_index_in_dim)/squeeze | solution.py:470
  8.4 3.0 %collective-permute-start.3 = (bf16[10,2,128,128]{3,2,1,0:T(8,128)(2,1)}, bf16[10,2,128,128]{3,2,1,0:T(8,128)(2,1)S(1)}, u32[]{:S(2)}, u32[]{:S(2)}) collective-permute-start(bf16[10,2,128,128]{3,2,1,0:T(8,128)(2,1)} %get-tuple-element.89), channel_id=1, source_target_pairs={{0,112},{16,96},{32,16},{48,0},{64,48},{80,32},{96,80},{112,64},{1... | collective-permute-start | bytes 1966088 | tf_op jit(solution)/shard_map/ppermute | solution.py:451
  15.8 3.5 %all-to-all-start = ((bf16[8,11,16,256]{3,2,1,0:T(8,128)(2,1)}), bf16[8,11,16,256]{3,2,1,0:T(8,128)(2,1)S(1)}, u32[]{:S(2)}, u32[]{:S(2)}) async-start(bf16[8,11,16,256]{3,2,1,0:T(8,128)(2,1)} %pad_maximum_fusion), calls=%async_computation | async-start | bytes 1441792 | tf_op jit(solution)/shard_map/all_to_all | solution.py:481
  19.4 2.3 %swap.1 = bf16[10,4,2,128,128]{4,3,2,1,0:T(8,128)(2,1)S(1)} custom-call(s32[2]{0:T(128)S(1)} %pad_add_fusion.place, bf16[10,2,4,2,2,128,128]{6,5,4,3,2,1,0:T(8,128)(2,1)} %bitcast.52), custom_call_target="tpu_custom_call" | custom-call | tf_op jit(solution)/shard_map/swap/pallas_call | solution.py:289
  21.8 1.5 copy-done.2
  23.2 3.3 %dynamic-slice_bitcast_fusion = (bf16[10,2,128,128]{3,2,1,0:T(8,128)(2,1)}, bf16[10,2,128,128]{3,2,1,0:T(8,128)(2,1)}, bf16[10,2,128,128]{3,2,1,0:T(8,128)(2,1)}, bf16[10,2,128,128]{3,2,1,0:T(8,128)(2,1)}) fusion(bf16[10,16,2,128,128]{4,3,2,1,0:T(8,128)(2,1)} %bitcast.53, s32[]{:T(128)S(6)} %select_n.105, s32[]{:T(128)S(6)} %select_n.100, s32[]{:T(128)S(6)} %select_n.99, ...), kind=kLoop, calls=%fused_computation.5 | loop fusion | bytes 5242896 | tf_op jit(solution)/shard_map/jit(dynamic_index_in_dim)/squeeze | solution.py:511
  26.5 17.0 %all-to-all-done = bf16[8,11,16,256]{3,2,1,0:T(8,128)(2,1)S(1)} async-done(((bf16[8,11,16,256]{3,2,1,0:T(8,128)(2,1)}), bf16[8,11,16,256]{3,2,1,0:T(8,128)(2,1)S(1)}, u32[]{:S(2)}, u32[]{:S(2)}) %all-to-all-start) | async-done | bytes 720928 | tf_op jit(solution)/shard_map/all_to_all | solution.py:481
  49.1 4.2 %collective-permute-start.5 = (bf16[2,5,128,256]{3,2,1,0:T(8,128)(2,1)S(1)}, bf16[2,5,128,256]{3,2,1,0:T(8,128)(2,1)S(1)}, u32[]{:S(2)}, u32[]{:S(2)}) collective-permute-start(bf16[2,5,128,256]{3,2,1,0:T(8,128)(2,1)S(1)} %multiply_convert_fusion.own), channel_id=1, source_target_pairs={{1,0},{2,1},{3,2},{4,3},{5,4},{6,5},{7,6},{8,7},{9,8},{10,9},{11,1... | collective-permute-start | bytes 1966088 | tf_op jit(solution)/shard_map/ppermute | solution.py:451
  53.3 2.9 %collective-permute-start.6 = (bf16[10,2,128,128]{3,2,1,0:T(8,128)(2,1)S(1)}, bf16[10,2,128,128]{3,2,1,0:T(8,128)(2,1)S(1)}, u32[]{:S(2)}, u32[]{:S(2)}) collective-permute-start(bf16[10,2,128,128]{3,2,1,0:T(8,128)(2,1)S(1)} %copy-done.23), channel_id=1, source_target_pairs={{0,64},{16,80},{32,96},{48,112},{64,0},{80,16},{96,32},{112,48},{1... | collective-permute-start | bytes 1966088 | tf_op jit(solution)/shard_map/ppermute | solution.py:451
  56.2 2.7 %collective-permute-start.8 = (bf16[2,3,128,256]{3,2,1,0:T(8,128)(2,1)S(1)}, bf16[2,3,128,256]{3,2,1,0:T(8,128)(2,1)S(1)}, u32[]{:S(2)}, u32[]{:S(2)}) collective-permute-start(bf16[2,3,128,256]{3,2,1,0:T(8,128)(2,1)S(1)} %slice.14), channel_id=1, source_target_pairs={{2,0},{3,1},{4,2},{5,3},{6,4},{7,5},{8,6},{9,7},{10,8},{11,9},{12,... | collective-permute-start | bytes 1179656 | tf_op jit(solution)/shard_map/ppermute | solution.py:451
  59.0 4.0 %pack.1 = (bf16[20,2,128,128]{3,2,1,0:T(8,128)(2,1)}, bf16[20,2,128,128]{3,2,1,0:T(8,128)(2,1)}, bf16[20,2,128,128]{3,2,1,0:T(8,128)(2,1)}) custom-call(s32[2]{0:T(128)S(1)} %pad_add_fusion.place, bf16[10,2,4,2,2,128,128]{6,5,4,3,2,1,0:T(8,128)(2,1)} %bitcast.54, bf16[10,4,2,128,128]{4,3,2,1,0:T(8,128)(2,1)S(1)} %collective-permute-done.4.pair), custom_call_target="tpu_custom_call" | custom-call | tf_op jit(solution)/shard_map/pack/pallas_call | solution.py:317
  64.6 5.9 %collective-permute-done.8.far = bf16[2,3,128,256]{3,2,1,0:T(8,128)(2,1)S(1)} collective-permute-done((bf16[2,3,128,256]{3,2,1,0:T(8,128)(2,1)S(1)}, bf16[2,3,128,256]{3,2,1,0:T(8,128)(2,1)S(1)}, u32[]{:S(2)}, u32[]{:S(2)}) %collective-permute-start.8) | collective-permute-done | bytes 393248 | tf_op jit(solution)/shard_map/ppermute | solution.py:451
  72.2 1.8 collective-permute-start.10
  73.9 2.4 %collective-permute-done.5.near = bf16[2,5,128,256]{3,2,1,0:T(8,128)(2,1)S(1)} collective-permute-done((bf16[2,5,128,256]{3,2,1,0:T(8,128)(2,1)S(1)}, bf16[2,5,128,256]{3,2,1,0:T(8,128)(2,1)S(1)}, u32[]{:S(2)}, u32[]{:S(2)}) %collective-permute-start.5) | collective-permute-done | bytes 655392 | tf_op jit(solution)/shard_map/ppermute | solution.py:451
  77.2 4.3 %collective-permute-done.6.refs_6_ = bf16[10,2,128,128]{3,2,1,0:T(8,128)(2,1)S(1)} collective-permute-done((bf16[10,2,128,128]{3,2,1,0:T(8,128)(2,1)S(1)}, bf16[10,2,128,128]{3,2,1,0:T(8,128)(2,1)S(1)}, u32[]{:S(2)}, u32[]{:S(2)}) %collective-permute-start.6) | collective-permute-done | bytes 655392 | tf_op jit(solution)/shard_map/ppermute | solution.py:451
  88.8 2.0 %setup.1 = (s32[45]{0:T(128)S(1)}, s32[45]{0:T(128)S(1)}, bf16[13,256,256]{2,1,0:T(8,128)(2,1)S(1)}, bf16[13,256,256]{2,1,0:T(8,128)(2,1)S(1)}, bf16[5,256,256]{...) custom-call(s32[8,21]{1,0:T(8,128)S(1)} %gather_fusion, bf16[2,5,128,256]{3,2,1,0:T(8,128)(2,1)S(1)} %copy-done.1, ...), custom_call_target="tpu_custom_call" | custom-call | tf_op jit(solution)/shard_map/setup/pallas_call | solution.py:64
  97.4 8.9 %tiles.1 = (f32[5,128,256]{2,1,0:T(8,128)S(1)}, bf16[5,128,256]{2,1,0:T(8,128)(2,1)S(1)}, bf16[3,128,256]{2,1,0:T(8,128)(2,1)S(1)}) custom-call(s32[45]{0:T(128)S(1)} %get-tuple-element.64.table, bf16[10,2,128,128]{3,2,1,0:T(8,128)(2,1)S(1)} %copy-done.3, bf16[10,2,128,128]{3,2,1,0:T(8,128)(2,1)S(1)} %copy-done.7, bf16[10,2,128,128]{3,2,1,0:T(8,128)(2,1)S(1)} %copy-done.9, ...), custom_call_target="tpu_custom_call" | custom-call | tf_op jit(solution)/shard_map/tiles/pallas_call | solution.py:384
  106.2 3.7 %collective-permute-start.13 = (bf16[5,128,256]{2,1,0:T(8,128)(2,1)S(1)}, bf16[5,128,256]{2,1,0:T(8,128)(2,1)S(1)}, u32[]{:S(2)}, u32[]{:S(2)}) collective-permute-start(bf16[5,128,256]{2,1,0:T(8,128)(2,1)S(1)} %get-tuple-element.68), channel_id=1, source_target_pairs={{0,1},{1,2},{2,3},{3,4},{4,5},{5,6},{6,7},{7,8},{8,9},{9,10},{10,1... | collective-permute-start | bytes 983048 | tf_op jit(solution)/shard_map/ppermute | solution.py:451
  109.9 5.1 %collective-permute-start.14 = (bf16[3,128,256]{2,1,0:T(8,128)(2,1)S(1)}, bf16[3,128,256]{2,1,0:T(8,128)(2,1)S(1)}, u32[]{:S(2)}, u32[]{:S(2)}) collective-permute-start(bf16[3,128,256]{2,1,0:T(8,128)(2,1)S(1)} %get-tuple-element.69), channel_id=1, source_target_pairs={{0,2},{1,3},{2,4},{3,5},{4,6},{5,7},{6,8},{7,9},{8,10},{9,11},{10,... | collective-permute-start | bytes 589832 | tf_op jit(solution)/shard_map/ppermute | solution.py:451
  115.0 8.7 %collective-permute-done.14.far0 = bf16[3,128,256]{2,1,0:T(8,128)(2,1)S(1)} collective-permute-done((bf16[3,128,256]{2,1,0:T(8,128)(2,1)S(1)}, bf16[3,128,256]{2,1,0:T(8,128)(2,1)S(1)}, u32[]{:S(2)}, u32[]{:S(2)}) %collective-permute-start.14) | collective-permute-done | bytes 196640 | tf_op jit(solution)/shard_map/ppermute | solution.py:451
  123.7 12.9 %collective-permute-done.10.second = bf16[20,2,128,128]{3,2,1,0:T(8,128)(2,1)} collective-permute-done((bf16[20,2,128,128]{3,2,1,0:T(8,128)(2,1)}, bf16[20,2,128,128]{3,2,1,0:T(8,128)(2,1)}, u32[]{:S(2)}, u32[]{:S(2)}) %collective-permute-start.10) | collective-permute-done | bytes 1310752 | tf_op jit(solution)/shard_map/ppermute | solution.py:451
  137.5 2.9 %collect.1.held = bf16[80,2,128,128]{3,2,1,0:T(8,128)(2,1)S(1)} custom-call(s32[2]{0:T(128)S(1)} %pad_add_fusion.place, bf16[10,2,4,2,2,128,128]{6,5,4,3,2,1,0:T(8,128)(2,1)} %bitcast.55, bf16[10,4,2,128,128]{4,3,2,1,0:T(8,128)(2,1)S(1)} %collective-permute-done.4.pair, bf16[20,2,128,128]{3,2,1,0:T(8,128)(2,1)} %collective-permute-done.7.first, ...), custom_call_target="tpu_custom_call" | custom-call | tf_op jit(solution)/shard_map/collect/pallas_call | solution.py:270
  141.6 2.9 %side.3 = (bf16[5,5,256,128]{3,2,1,0:T(8,128)(2,1)S(1)}, bf16[5,128,256]{2,1,0:T(8,128)(2,1)S(1)}) custom-call(s32[45]{0:T(128)S(1)} %get-tuple-element.73.table, bf16[80,2,128,128]{3,2,1,0:T(8,128)(2,1)S(1)} %collect.1.held, bf16[13,256,256]{2,1,0:T(8,128)(2,1)S(1)} %get-tuple-element.77.stack, bf16[5,256,256]{2,1,0:T(8,128)(2,1)S(1)} %get-tuple-element.78.back), custom_call_target="tpu_custom_call" | custom-call | tf_op jit(solution)/shard_map/side/pallas_call | solution.py:211
  144.5 3.6 %collective-permute-start.15 = (bf16[5,128,256]{2,1,0:T(8,128)(2,1)S(1)}, bf16[5,128,256]{2,1,0:T(8,128)(2,1)S(1)}, u32[]{:S(2)}, u32[]{:S(2)}) collective-permute-start(bf16[5,128,256]{2,1,0:T(8,128)(2,1)S(1)} %get-tuple-element.83), channel_id=1, source_target_pairs={{0,1},{1,2},{2,3},{3,4},{4,5},{5,6},{6,7},{7,8},{8,9},{9,10},{10,1... | collective-permute-start | bytes 983048 | tf_op jit(solution)/shard_map/ppermute | solution.py:451
  148.1 4.7 %collective-permute-start.16 = (bf16[3,128,256]{2,1,0:T(8,128)(2,1)S(1)}, bf16[3,128,256]{2,1,0:T(8,128)(2,1)S(1)}, u32[]{:S(2)}, u32[]{:S(2)}) collective-permute-start(bf16[3,128,256]{2,1,0:T(8,128)(2,1)S(1)} %get-tuple-element.84), channel_id=1, source_target_pairs={{0,2},{1,3},{2,4},{3,5},{4,6},{5,7},{6,8},{7,9},{8,10},{9,11},{10,... | collective-permute-start | bytes 589832 | tf_op jit(solution)/shard_map/ppermute | solution.py:451
  152.8 3.4 %nearby.1.own1 = f32[5,128,256]{2,1,0:T(8,128)S(1)} custom-call(s32[45]{0:T(128)S(1)} %get-tuple-element.73.table, bf16[80,2,128,128]{3,2,1,0:T(8,128)(2,1)S(1)} %collect.1.held, bf16[13,256,256]{2,1,0:T(8,128)(2,1)S(1)} %get-tuple-element.77.stack, bf16[5,256,256]{2,1,0:T(8,128)(2,1)S(1)} %get-tuple-element.78.back, ...), custom_call_target="tpu_custom_call" | custom-call | tf_op jit(solution)/shard_map/nearby/pallas_call | solution.py:229
  156.2 6.0 %collective-permute-done.16.far1 = bf16[3,128,256]{2,1,0:T(8,128)(2,1)S(1)} collective-permute-done((bf16[3,128,256]{2,1,0:T(8,128)(2,1)S(1)}, bf16[3,128,256]{2,1,0:T(8,128)(2,1)S(1)}, u32[]{:S(2)}, u32[]{:S(2)}) %collective-permute-start.16) | collective-permute-done | bytes 196640 | tf_op jit(solution)/shard_map/ppermute | solution.py:451
  163.0 14.7 %all_to_all.10 = bf16[8,2,5,16,256]{4,3,2,1,0:T(8,128)(2,1)S(1)} all-to-all(bf16[8,2,5,16,256]{4,3,2,1,0:T(8,128)(2,1)S(1)} %final.1), channel_id=1, replica_groups=mesh['prow'=8,'pcol'=16] {'prow'}, dimensions={0} | all-to-all | bytes 1310720 | tf_op jit(solution)/shard_map/all_to_all | solution.py:523
  178.6 1.7 reshape.392
  (94 shorter events, 31.2 us)
Async XLA Ops:
  2.6 40.9 %collective-permute-start = (bf16[10,2,128,128]{3,2,1,0:T(8,128)(2,1)}, bf16[10,2,128,128]{3,2,1,0:T(8,128)(2,1)S(1)}, u32[]{:S(2)}, u32[]{:S(2)}) collective-permute-start(bf16[10,2,128,128]{3,2,1,0:T(8,128)(2,1)} %get-tuple-element.46), channel_id=1, source_target_pairs={{0,32},{16,48},{32,64},{48,80},{64,96},{80,112},{96,0},{112,16},{1... | collective-permute-start | bytes 1966088 | tf_op jit(solution)/shard_map/ppermute | solution.py:451
  4.2 39.3 %collective-permute-start.1 = (bf16[10,2,128,128]{3,2,1,0:T(8,128)(2,1)}, bf16[10,2,128,128]{3,2,1,0:T(8,128)(2,1)S(1)}, u32[]{:S(2)}, u32[]{:S(2)}) collective-permute-start(bf16[10,2,128,128]{3,2,1,0:T(8,128)(2,1)} %get-tuple-element.47), channel_id=1, source_target_pairs={{0,96},{16,112},{32,0},{48,16},{64,32},{80,48},{96,64},{112,80},{1... | collective-permute-start | bytes 1966088 | tf_op jit(solution)/shard_map/ppermute | solution.py:451
  5.8 5.5 %copy-start.24 = (bf16[5,16,16,2,128]{4,3,2,1,0:T(2,128)(2,1)S(1)}, bf16[5,16,16,2,128]{4,3,2,1,0:T(2,128)(2,1)}, u32[]{:S(2)}) copy-start(bf16[5,16,16,2,128]{4,3,2,1,0:T(2,128)(2,1)} %param.4) | copy-start | bytes 1966084
  8.4 36.0 %collective-permute-start.2 = (bf16[10,2,128,128]{3,2,1,0:T(8,128)(2,1)}, bf16[10,2,128,128]{3,2,1,0:T(8,128)(2,1)S(1)}, u32[]{:S(2)}, u32[]{:S(2)}) collective-permute-start(bf16[10,2,128,128]{3,2,1,0:T(8,128)(2,1)} %get-tuple-element.90), channel_id=1, source_target_pairs={{0,48},{16,32},{32,80},{48,64},{64,112},{80,96},{96,16},{112,0},{1... | collective-permute-start | bytes 1966088 | tf_op jit(solution)/shard_map/ppermute | solution.py:451
  8.4 5.5 %copy-start.25 = (s32[1,1,10,2]{2,3,1,0:T(2,128)S(1)}, s32[1,1,10,2]{2,3,1,0:T(2,128)}, u32[]{:S(2)}) copy-start(s32[1,1,10,2]{2,3,1,0:T(2,128)} %param.5) | copy-start | bytes 244
  8.4 37.0 %collective-permute-start.3 = (bf16[10,2,128,128]{3,2,1,0:T(8,128)(2,1)}, bf16[10,2,128,128]{3,2,1,0:T(8,128)(2,1)S(1)}, u32[]{:S(2)}, u32[]{:S(2)}) collective-permute-start(bf16[10,2,128,128]{3,2,1,0:T(8,128)(2,1)} %get-tuple-element.89), channel_id=1, source_target_pairs={{0,112},{16,96},{32,16},{48,0},{64,48},{80,32},{96,80},{112,64},{1... | collective-permute-start | bytes 1966088 | tf_op jit(solution)/shard_map/ppermute | solution.py:451
  15.8 27.7 %all-to-all-start = ((bf16[8,11,16,256]{3,2,1,0:T(8,128)(2,1)}), bf16[8,11,16,256]{3,2,1,0:T(8,128)(2,1)S(1)}, u32[]{:S(2)}, u32[]{:S(2)}) async-start(bf16[8,11,16,256]{3,2,1,0:T(8,128)(2,1)} %pad_maximum_fusion), calls=%async_computation | async-start | bytes 1441792 | tf_op jit(solution)/shard_map/all_to_all | solution.py:481
  21.8 1.5 copy-start.2
  43.5 3.9 %copy-start.6 = (bf16[10,2,128,128]{3,2,1,0:T(8,128)(2,1)}, bf16[10,2,128,128]{3,2,1,0:T(8,128)(2,1)S(1)}, u32[]{:S(2)}) copy-start(bf16[10,2,128,128]{3,2,1,0:T(8,128)(2,1)S(1)} %collective-permute-done.refs_1_) | copy-start | bytes 1966084
  46.2 10.0 %collective-permute-start.4 = (bf16[10,4,2,128,128]{4,3,2,1,0:T(8,128)(2,1)}, bf16[10,4,2,128,128]{4,3,2,1,0:T(8,128)(2,1)S(1)}, u32[]{:S(2)}, u32[]{:S(2)}) collective-permute-start(bf16[10,4,2,128,128]{4,3,2,1,0:T(8,128)(2,1)} %copy-done.2), channel_id=1, source_target_pairs={{0,16},{16,0},{32,48},{48,32},{64,80},{80,64},{96,112},{112,96},{1... | collective-permute-start | bytes 7864328 | tf_op jit(solution)/shard_map/ppermute | solution.py:451
  47.8 5.5 %copy-start.23 = (bf16[10,2,128,128]{3,2,1,0:T(8,128)(2,1)S(1)}, bf16[10,2,128,128]{3,2,1,0:T(8,128)(2,1)}, u32[]{:S(2)}) copy-start(bf16[10,2,128,128]{3,2,1,0:T(8,128)(2,1)} %get-tuple-element.56) | copy-start | bytes 1966084
  47.8 15.2 %collective-permute-start.11 = (bf16[10,2,128,128]{3,2,1,0:T(8,128)(2,1)}, bf16[10,2,128,128]{3,2,1,0:T(8,128)(2,1)S(1)}, u32[]{:S(2)}, u32[]{:S(2)}) collective-permute-start(bf16[10,2,128,128]{3,2,1,0:T(8,128)(2,1)} %get-tuple-element.62), channel_id=1, source_target_pairs={{0,16},{16,0},{32,48},{48,32},{64,80},{80,64},{96,112},{112,96},{1... | collective-permute-start | bytes 1966088 | tf_op jit(solution)/shard_map/ppermute | solution.py:451
  48.4 22.9 %collective-permute-start.9 = (bf16[10,2,128,128]{3,2,1,0:T(8,128)(2,1)}, bf16[10,2,128,128]{3,2,1,0:T(8,128)(2,1)S(1)}, u32[]{:S(2)}, u32[]{:S(2)}) collective-permute-start(bf16[10,2,128,128]{3,2,1,0:T(8,128)(2,1)} %get-tuple-element.59), channel_id=1, source_target_pairs={{0,80},{16,64},{32,112},{48,96},{64,16},{80,0},{96,48},{112,32},{1... | collective-permute-start | bytes 1966088 | tf_op jit(solution)/shard_map/ppermute | solution.py:451
  49.1 13.9 %copy-start = (bf16[2,5,128,256]{3,2,1,0:T(8,128)(2,1)}, bf16[2,5,128,256]{3,2,1,0:T(8,128)(2,1)S(1)}, u32[]{:S(2)}) copy-start(bf16[2,5,128,256]{3,2,1,0:T(8,128)(2,1)S(1)} %multiply_convert_fusion.own) | copy-start | bytes 1966084
  49.1 27.2 %collective-permute-start.5 = (bf16[2,5,128,256]{3,2,1,0:T(8,128)(2,1)S(1)}, bf16[2,5,128,256]{3,2,1,0:T(8,128)(2,1)S(1)}, u32[]{:S(2)}, u32[]{:S(2)}) collective-permute-start(bf16[2,5,128,256]{3,2,1,0:T(8,128)(2,1)S(1)} %multiply_convert_fusion.own), channel_id=1, source_target_pairs={{1,0},{2,1},{3,2},{4,3},{5,4},{6,5},{7,6},{8,7},{9,8},{10,9},{11,1... | collective-permute-start | bytes 1966088 | tf_op jit(solution)/shard_map/ppermute | solution.py:451
  53.3 28.1 %collective-permute-start.6 = (bf16[10,2,128,128]{3,2,1,0:T(8,128)(2,1)S(1)}, bf16[10,2,128,128]{3,2,1,0:T(8,128)(2,1)S(1)}, u32[]{:S(2)}, u32[]{:S(2)}) collective-permute-start(bf16[10,2,128,128]{3,2,1,0:T(8,128)(2,1)S(1)} %copy-done.23), channel_id=1, source_target_pairs={{0,64},{16,80},{32,96},{48,112},{64,0},{80,16},{96,32},{112,48},{1... | collective-permute-start | bytes 1966088 | tf_op jit(solution)/shard_map/ppermute | solution.py:451
  56.2 14.3 %collective-permute-start.8 = (bf16[2,3,128,256]{3,2,1,0:T(8,128)(2,1)S(1)}, bf16[2,3,128,256]{3,2,1,0:T(8,128)(2,1)S(1)}, u32[]{:S(2)}, u32[]{:S(2)}) collective-permute-start(bf16[2,3,128,256]{3,2,1,0:T(8,128)(2,1)S(1)} %slice.14), channel_id=1, source_target_pairs={{2,0},{3,1},{4,2},{5,3},{6,4},{7,5},{8,6},{9,7},{10,8},{11,9},{12,... | collective-permute-start | bytes 1179656 | tf_op jit(solution)/shard_map/ppermute | solution.py:451
  63.9 59.9 %collective-permute-start.12 = (bf16[20,2,128,128]{3,2,1,0:T(8,128)(2,1)}, bf16[20,2,128,128]{3,2,1,0:T(8,128)(2,1)}, u32[]{:S(2)}, u32[]{:S(2)}) collective-permute-start(bf16[20,2,128,128]{3,2,1,0:T(8,128)(2,1)} %get-tuple-element.63), channel_id=1, source_target_pairs={{0,64},{16,80},{32,96},{48,112},{64,0},{80,16},{96,32},{112,48},{1... | collective-permute-start | bytes 3932168 | tf_op jit(solution)/shard_map/ppermute | solution.py:451
  72.2 64.5 %collective-permute-start.10 = (bf16[20,2,128,128]{3,2,1,0:T(8,128)(2,1)}, bf16[20,2,128,128]{3,2,1,0:T(8,128)(2,1)}, u32[]{:S(2)}, u32[]{:S(2)}) collective-permute-start(bf16[20,2,128,128]{3,2,1,0:T(8,128)(2,1)} %get-tuple-element.60), channel_id=1, source_target_pairs={{0,96},{16,112},{32,0},{48,16},{64,32},{80,48},{96,64},{112,80},{1... | collective-permute-start | bytes 3932168 | tf_op jit(solution)/shard_map/ppermute | solution.py:451
  82.3 55.2 %collective-permute-start.7 = (bf16[20,2,128,128]{3,2,1,0:T(8,128)(2,1)}, bf16[20,2,128,128]{3,2,1,0:T(8,128)(2,1)}, u32[]{:S(2)}, u32[]{:S(2)}) collective-permute-start(bf16[20,2,128,128]{3,2,1,0:T(8,128)(2,1)} %get-tuple-element.57), channel_id=1, source_target_pairs={{0,32},{16,48},{32,64},{48,80},{64,96},{80,112},{96,0},{112,16},{1... | collective-permute-start | bytes 3932168 | tf_op jit(solution)/shard_map/ppermute | solution.py:451
  85.6 1.1 copy-start.1
  86.7 1.1 copy-start.5
  88.8 2.0 %copy-start.3 = (bf16[10,2,128,128]{3,2,1,0:T(8,128)(2,1)S(1)}, bf16[10,2,128,128]{3,2,1,0:T(8,128)(2,1)}, u32[]{:S(2)}) copy-start(bf16[10,2,128,128]{3,2,1,0:T(8,128)(2,1)} %get-tuple-element.85.refs_0_) | copy-start | bytes 1966084
  88.8 2.0 %copy-start.7 = (bf16[10,2,128,128]{3,2,1,0:T(8,128)(2,1)S(1)}, bf16[10,2,128,128]{3,2,1,0:T(8,128)(2,1)}, u32[]{:S(2)}) copy-start(bf16[10,2,128,128]{3,2,1,0:T(8,128)(2,1)} %copy-done.6) | copy-start | bytes 1966084
  90.8 1.1 copy-start.9
  91.9 1.1 copy-start.11
  93.0 1.1 copy-start.13
  94.1 1.1 copy-start.15
  106.2 17.5 %collective-permute-start.13 = (bf16[5,128,256]{2,1,0:T(8,128)(2,1)S(1)}, bf16[5,128,256]{2,1,0:T(8,128)(2,1)S(1)}, u32[]{:S(2)}, u32[]{:S(2)}) collective-permute-start(bf16[5,128,256]{2,1,0:T(8,128)(2,1)S(1)} %get-tuple-element.68), channel_id=1, source_target_pairs={{0,1},{1,2},{2,3},{3,4},{4,5},{5,6},{6,7},{7,8},{8,9},{9,10},{10,1... | collective-permute-start | bytes 983048 | tf_op jit(solution)/shard_map/ppermute | solution.py:451
  109.9 13.8 %collective-permute-start.14 = (bf16[3,128,256]{2,1,0:T(8,128)(2,1)S(1)}, bf16[3,128,256]{2,1,0:T(8,128)(2,1)S(1)}, u32[]{:S(2)}, u32[]{:S(2)}) collective-permute-start(bf16[3,128,256]{2,1,0:T(8,128)(2,1)S(1)} %get-tuple-element.69), channel_id=1, source_target_pairs={{0,2},{1,3},{2,4},{3,5},{4,6},{5,7},{6,8},{7,9},{8,10},{9,11},{10,... | collective-permute-start | bytes 589832 | tf_op jit(solution)/shard_map/ppermute | solution.py:451
  144.5 17.8 %collective-permute-start.15 = (bf16[5,128,256]{2,1,0:T(8,128)(2,1)S(1)}, bf16[5,128,256]{2,1,0:T(8,128)(2,1)S(1)}, u32[]{:S(2)}, u32[]{:S(2)}) collective-permute-start(bf16[5,128,256]{2,1,0:T(8,128)(2,1)S(1)} %get-tuple-element.83), channel_id=1, source_target_pairs={{0,1},{1,2},{2,3},{3,4},{4,5},{5,6},{6,7},{7,8},{8,9},{9,10},{10,1... | collective-permute-start | bytes 983048 | tf_op jit(solution)/shard_map/ppermute | solution.py:451
  148.1 14.0 %collective-permute-start.16 = (bf16[3,128,256]{2,1,0:T(8,128)(2,1)S(1)}, bf16[3,128,256]{2,1,0:T(8,128)(2,1)S(1)}, u32[]{:S(2)}, u32[]{:S(2)}) collective-permute-start(bf16[3,128,256]{2,1,0:T(8,128)(2,1)S(1)} %get-tuple-element.84), channel_id=1, source_target_pairs={{0,2},{1,3},{2,4},{3,5},{4,6},{5,7},{6,8},{7,9},{8,10},{9,11},{10,... | collective-permute-start | bytes 589832 | tf_op jit(solution)/shard_map/ppermute | solution.py:451
  (12 other events, 10.9 us)
